TPU v7x, 512 devices: a whole 4x4x16 slice. The times are simulated.
512 devices in a mesh: row: 16 (over z_lo, core), col: 16 (over x, y), dim: 2 (over z_hi).
Axes of the slice: x: 4, y: 4, z: 16 (z_hi: 2, z_lo: 8; z = z_hi * 8 + z_lo), core: 2. Of those that a mesh axis runs over, the one named last changes fastest.
Arguments:
- row_emb: bfloat16 [16, 1024, 256], P('row', None, 'dim'), may hold values from -2 to 2
- col_emb: bfloat16 [16, 1024, 256], P('col', None, 'dim'), may hold values from -2 to 2
- row_acc: float32 [16, 1024], P('row'), may hold values from 0.01 to 1
- col_acc: float32 [16, 1024], P('col'), may hold values from 0.01 to 1
- counts: int32 [16, 16, 1024, 1024], P('row', 'col', 'dim'), may hold values from 0 to 4000, as said below
- live_rows: int32 [16, 16], P('row', 'col'), may hold values from 128 to 1024, as said below
- row_marg: int32 [16, 1024], replicated, may hold values from 1000 to 99999
- col_marg: int32 [16, 1024], replicated, may hold values from 1000 to 99999
Outputs:
- row_new: bfloat16 [16, 1024, 256], P('row', None, 'dim')
- row_acc_new: float32 [16, 1024], P('row')
- col_new: bfloat16 [16, 1024, 256], P('col', None, 'dim')
- col_acc_new: float32 [16, 1024], P('col')
Inputs may be any that keep to these rules, and one draw needn't show every extreme that they name: `live_rows`: a multiple of 128; some tile uses all 1024 rows in every draw. About half of the counts are zero.
All inputs are finite; a program needn't handle non-finite values.
Results may differ from a plain program's by a relative error of at most 0.012.
Values may be sent and summed in bfloat16 or wider, within the bound.
No kernel may reach another device: no remote copies, remote signals or barrier semaphores. Data moves between devices by JAX's collectives and lax.ppermute only.
A program may use at most 64 MiB of HBM per device.

v0:
```python
import jax
import jax.numpy as jnp
from jax import lax
from jax.sharding import PartitionSpec as P

STEPS = 2


learn_rate = 0.1


def swapped(block, axis, stride):
    count = lax.axis_size(axis)
    route = []
    for low in range(count):
        high = low | 1 << stride
        if high != low and high < count:
            route += [(low, high), (high, low)]
    return lax.ppermute(block, axis, route)


def cell_grad(scores, tile_counts, shift_log):
    count_f = tile_counts.astype(jnp.float32)
    target = jnp.log(jnp.maximum(count_f, 1.0)) + shift_log
    confidence = 0.1 + 0.25 * jnp.sqrt(count_f)
    return jnp.where(
        tile_counts > 0, confidence * (scores - target), jax.nn.sigmoid(scores - shift_log)
    )


def shards(row_emb, col_emb, row_acc, col_acc, counts, live_rows, row_marg, col_marg):
    tile_side = row_emb.shape[1]
    half_d = row_emb.shape[2]
    full_width = half_d * lax.axis_size("dim")
    half_rows = tile_side // lax.axis_size("dim")
    dim_side = lax.axis_index("dim")
    contract_last = (((1,), (1,)), ((), ()))
    contract_first = (((0,), (0,)), ((), ()))
    tile_counts = counts[0, 0]
    live_here = live_rows[0, 0]
    log_total = jnp.log(jnp.sum(row_marg).astype(jnp.float32))
    own_marg = lax.dynamic_index_in_dim(row_marg, lax.axis_index("row"), 0, False)
    row_logs = lax.dynamic_slice_in_dim(
        jnp.log(own_marg.astype(jnp.float32)), dim_side * half_rows, half_rows, 0
    )
    col_logs = jnp.log(
        lax.dynamic_index_in_dim(col_marg, lax.axis_index("col"), 0, False).astype(jnp.float32)
    )
    shift_log = log_total - row_logs[:, None] - col_logs[None, :]
    row_live = dim_side * half_rows + jnp.arange(half_rows, dtype=jnp.int32) < live_here
    for step in range(STEPS):
        full_rows, full_cols = (
            lax.all_gather(row_emb, "dim", axis=2, tiled=True),
            lax.all_gather(col_emb, "dim", axis=2, tiled=True),
        )
        w_block = lax.dynamic_slice_in_dim(full_rows[0], dim_side * half_rows, half_rows, 0)
        c_block = full_cols[0]
        lower_half = lax.dot_general(
            w_block[:, :half_d],
            c_block[:, :half_d],
            contract_last,
            preferred_element_type=jnp.float32,
        ).astype(jnp.bfloat16)
        upper_half = lax.dot_general(
            w_block[:, half_d:],
            c_block[:, half_d:],
            contract_last,
            preferred_element_type=jnp.float32,
        ).astype(jnp.bfloat16)
        scores = lower_half.astype(jnp.float32) + upper_half.astype(jnp.float32)
        grad_tile = cell_grad(scores, tile_counts, shift_log) / tile_side
        grad_tile = jnp.where(row_live[:, None], grad_tile, 0.0).astype(jnp.bfloat16)
        row_term = jnp.dot(grad_tile, c_block, preferred_element_type=jnp.float32)
        col_term = lax.dot_general(
            grad_tile, w_block, contract_first, preferred_element_type=jnp.float32
        )
        own_part = lax.dynamic_slice_in_dim(row_term, dim_side * half_d, half_d, 1)
        other_part = lax.dynamic_slice_in_dim(row_term, (1 - dim_side) * half_d, half_d, 1)
        received = swapped(other_part.astype(jnp.bfloat16), "dim", 0).astype(other_part.dtype)
        leading = jnp.where(dim_side == 0, own_part, received)
        trailing = jnp.where(dim_side == 0, received, own_part)
        row_grad = jnp.concatenate([leading, trailing], axis=0)[None]
        col_grad = lax.psum_scatter(
            col_term[None].astype(jnp.bfloat16), "dim", scatter_dimension=2, tiled=True
        )
        row_total = lax.psum(row_grad.astype(jnp.bfloat16), "col").astype(jnp.float32)
        col_total = lax.psum(col_grad, "row").astype(jnp.float32)
        row_square, col_square = lax.psum(
            (jnp.sum(row_total * row_total, axis=2), jnp.sum(col_total * col_total, axis=2)), "dim"
        )
        row_acc = row_acc + row_square / full_width
        col_acc = col_acc + col_square / full_width
        row_emb = (
            row_emb.astype(jnp.float32) - learn_rate * row_total / jnp.sqrt(row_acc)[:, :, None]
        ).astype(jnp.bfloat16)
        col_emb = (
            col_emb.astype(jnp.float32) - learn_rate * col_total / jnp.sqrt(col_acc)[:, :, None]
        ).astype(jnp.bfloat16)
    return (row_emb, row_acc, col_emb, col_acc)


def solution(mesh):
    return jax.shard_map(
        shards,
        mesh=mesh,
        in_specs=(
            P("row", None, "dim"),
            P("col", None, "dim"),
            P("row", None),
            P("col", None),
            P("row", "col", "dim", None),
            P("row", "col"),
            P(),
            P(),
        ),
        out_specs=(P("row", None, "dim"), P("row", None), P("col", None, "dim"), P("col", None)),
        check_vma=False,
    )
```

profile of v0, /device:TPU:8, one launch (start us, length us, event | category | flops | bytes accessed | tf_op | source)
XLA Modules:
  0.0 846.1 jit_solution(13488465103290317736)
XLA Ops:
  8.7 1.5 reduce_sum.53
  10.9 21.3 %all_gather.13 = bf16[1,1024,256]{2,1,0:T(8,128)(2,1)S(1)} all-gather(bf16[1,1024,128]{2,1,0:T(8,128)(2,1)} %param.9), channel_id=1, replica_groups=mesh['row'=16,'col'=16,'dim'=2] {'dim'}, dimensions={2}, use_global_device_ids=true | all-gather | bytes 786432 | tf_op jit(solution)/shard_map/all_gather | solution.py:54
  32.2 28.5 %all_gather.12 = bf16[1,1024,256]{2,1,0:T(8,128)(2,1)S(1)} all-gather(bf16[1,1024,128]{2,1,0:T(8,128)(2,1)} %param.8), channel_id=1, replica_groups=mesh['row'=16,'col'=16,'dim'=2] {'dim'}, dimensions={2}, use_global_device_ids=true | all-gather | bytes 786432 | tf_op jit(solution)/shard_map/all_gather | solution.py:53
  62.8 4.6 select_convert_fusion.1
  70.4 4.7 collective-permute-start
  75.1 11.3 %collective-permute-done = bf16[512,128]{1,0:T(8,128)(2,1)S(1)} collective-permute-done((bf16[512,128]{1,0:T(8,128)(2,1)S(1)}, bf16[512,128]{1,0:T(8,128)(2,1)S(1)}, u32[]{:S(2)}, u32[]{:S(2)}) %collective-permute-start) | collective-permute-done | bytes 131104 | tf_op jit(solution)/shard_map/ppermute | solution.py:19
  87.3 44.5 %reduce-scatter.7.cloned.1.call-done = bf16[128,1024]{1,0:T(8,128)(2,1)} async-done(((bf16[256,1024]{1,0:T(8,128)(2,1)}), bf16[128,1024]{1,0:T(8,128)(2,1)}) %reduce-scatter.7.cloned.1.call-update) | async-done | bytes 262160
  131.7 1.2 reshape_bitcast_fusion.1
  133.0 1.1 copy.13
  134.1 82.8 %all-reduce.7.cloned.1.call-done = bf16[1,1024,128]{2,1,0:T(8,128)(2,1)} async-done(((bf16[1,1024,128]{2,1,0:T(8,128)(2,1)}), bf16[1,1024,128]{2,1,0:T(8,128)(2,1)}) %all-reduce.7.cloned.1.call-update) | async-done | bytes 262160 | tf_op jit(solution)/shard_map/psum | solution.py:86
  216.9 1.2 fusion.17
  218.2 197.1 %all-reduce.9.cloned.1.call-done = bf16[1,1024,128]{2,1,0:T(8,128)(2,1)} async-done(((bf16[1,1024,128]{2,1,0:T(8,128)(2,1)}), bf16[1,1024,128]{2,1,0:T(8,128)(2,1)}) %all-reduce.9.cloned.1.call-update) | async-done | bytes 262160 | tf_op jit(solution)/shard_map/psum | solution.py:87
  415.2 1.2 fusion.21
  416.4 17.1 %all-reduce.1 = (f32[1,1024]{1,0:T(1,128)S(1)}, f32[1,1024]{1,0:T(1,128)S(1)}) all-reduce(f32[1,1024]{1,0:T(1,128)S(1)} %bitcast.84, f32[1,1024]{1,0:T(1,128)S(1)} %bitcast.82), channel_id=1, replica_groups=mesh['row'=16,'col'=16,'dim'=2] {'dim'}, use_global_device_ids=true, to_apply=%region_7.8 | all-reduce | flops 2048 | bytes 16384 | tf_op jit(solution)/shard_map/psum | solution.py:88
  433.6 1.2 fusion.20
  434.8 25.6 %all_gather.15 = bf16[1,1024,256]{2,1,0:T(8,128)(2,1)S(1)} all-gather(bf16[1,1024,128]{2,1,0:T(8,128)(2,1)S(1)} %fusion.20), channel_id=1, replica_groups=mesh['row'=16,'col'=16,'dim'=2] {'dim'}, dimensions={2}, use_global_device_ids=true | all-gather | bytes 786432 | tf_op jit(solution)/shard_map/all_gather | solution.py:54
  460.6 21.9 %all_gather.14 = bf16[1,1024,256]{2,1,0:T(8,128)(2,1)S(1)} all-gather(bf16[1,1024,128]{2,1,0:T(8,128)(2,1)S(1)} %fusion.16), channel_id=1, replica_groups=mesh['row'=16,'col'=16,'dim'=2] {'dim'}, dimensions={2}, use_global_device_ids=true | all-gather | bytes 786432 | tf_op jit(solution)/shard_map/all_gather | solution.py:53
  482.9 2.4 select_convert_fusion
  486.8 1.0 copy.14
  488.9 1.7 fusion.48
  490.6 9.6 %collective-permute-start.1 = (bf16[512,128]{1,0:T(8,128)(2,1)S(1)}, bf16[512,128]{1,0:T(8,128)(2,1)S(1)}, u32[]{:S(2)}, u32[]{:S(2)}) collective-permute-start(bf16[512,128]{1,0:T(8,128)(2,1)S(1)} %dynamic-slice_convert_fusion), channel_id=1, source_target_pairs={{0,1},{1,0},{2,3},{3,2},{4,5},{5,4},{6,7},{7,6},{8,9},{9,8},{10,11... | collective-permute-start | bytes 393224 | tf_op jit(solution)/shard_map/ppermute | solution.py:19
  500.2 6.5 collective-permute-done.1
  507.6 30.5 %reduce-scatter.9.cloned.1.call-done = bf16[128,1024]{1,0:T(8,128)(2,1)} async-done(((bf16[256,1024]{1,0:T(8,128)(2,1)}), bf16[128,1024]{1,0:T(8,128)(2,1)}) %reduce-scatter.9.cloned.1.call-update) | async-done | bytes 262160
  538.1 1.2 reshape_bitcast_fusion
  539.3 1.1 copy.15
  540.4 79.5 %all-reduce.11.cloned.1.call-done = bf16[1,1024,128]{2,1,0:T(8,128)(2,1)} async-done(((bf16[1,1024,128]{2,1,0:T(8,128)(2,1)}), bf16[1,1024,128]{2,1,0:T(8,128)(2,1)}) %all-reduce.11.cloned.1.call-update) | async-done | bytes 262160 | tf_op jit(solution)/shard_map/psum | solution.py:86
  619.9 1.2 fusion.25
  621.1 197.6 %all-reduce.13.cloned.1.call-done = bf16[1,1024,128]{2,1,0:T(8,128)(2,1)} async-done(((bf16[1,1024,128]{2,1,0:T(8,128)(2,1)}), bf16[1,1024,128]{2,1,0:T(8,128)(2,1)}) %all-reduce.13.cloned.1.call-update) | async-done | bytes 262160 | tf_op jit(solution)/shard_map/psum | solution.py:87
  818.7 1.2 fusion.29
  819.8 13.7 %all-reduce = (f32[1,1024]{1,0:T(1,128)S(1)}, f32[1,1024]{1,0:T(1,128)S(1)}) all-reduce(f32[1,1024]{1,0:T(1,128)S(1)} %bitcast.83, f32[1,1024]{1,0:T(1,128)S(1)} %bitcast.85), channel_id=1, replica_groups=mesh['row'=16,'col'=16,'dim'=2] {'dim'}, use_global_device_ids=true, to_apply=%region_10.11 | all-reduce | flops 2048 | bytes 16384 | tf_op jit(solution)/shard_map/psum | solution.py:88
  834.7 1.9 fusion.24
  836.6 1.9 fusion.28
  (49 shorter events, 11.3 us)
Async XLA Ops:
  8.0 123.7 %reduce-scatter.7.cloned.1.call-start = ((), (), s32[]{:S(2)}) async-start(), calls=%async_computation.6 | async-start | bytes 786432
  69.9 147.0 %all-reduce.7.cloned.1.call-start = ((), (), s32[]{:S(2)}) async-start(), calls=%async_computation.2 | async-start | bytes 524288 | tf_op jit(solution)/shard_map/psum | solution.py:86
  70.4 363.1 %copy-start.3 = (f32[1,1024]{1,0:T(1,128)S(1)}, f32[1,1024]{1,0:T(1,128)}, u32[]{:S(2)}) copy-start(f32[1,1024]{1,0:T(1,128)} %param.10) | copy-start | bytes 12292
  70.4 363.1 %copy-start.4 = (f32[1,1024]{1,0:T(1,128)S(1)}, f32[1,1024]{1,0:T(1,128)}, u32[]{:S(2)}) copy-start(f32[1,1024]{1,0:T(1,128)} %param.11) | copy-start | bytes 12292
  70.4 363.2 %copy-start = (bf16[1,1024,128]{2,1,0:T(8,128)(2,1)S(1)}, bf16[1,1024,128]{2,1,0:T(8,128)(2,1)}, u32[]{:S(2)}) copy-start(bf16[1,1024,128]{2,1,0:T(8,128)(2,1)} %param.9) | copy-start | bytes 786436
  70.4 16.0 %collective-permute-start = (bf16[512,128]{1,0:T(8,128)(2,1)S(1)}, bf16[512,128]{1,0:T(8,128)(2,1)S(1)}, u32[]{:S(2)}, u32[]{:S(2)}) collective-permute-start(bf16[512,128]{1,0:T(8,128)(2,1)S(1)} %dynamic-slice_convert_fusion.1), channel_id=1, source_target_pairs={{0,1},{1,0},{2,3},{3,2},{4,5},{5,4},{6,7},{7,6},{8,9},{9,8},{10,11... | collective-permute-start | bytes 393224 | tf_op jit(solution)/shard_map/ppermute | solution.py:19
  87.2 373.1 %copy-start.1 = (bf16[1,1024,128]{2,1,0:T(8,128)(2,1)S(1)}, bf16[1,1024,128]{2,1,0:T(8,128)(2,1)}, u32[]{:S(2)}) copy-start(bf16[1,1024,128]{2,1,0:T(8,128)(2,1)} %param.8) | copy-start | bytes 786436
  87.2 328.0 %all-reduce.9.cloned.1.call-start = ((), (), s32[]{:S(2)}) async-start(), calls=%async_computation.3 | async-start | bytes 524288 | tf_op jit(solution)/shard_map/psum | solution.py:87
  134.0 404.0 %reduce-scatter.9.cloned.1.call-start = ((), (), s32[]{:S(2)}) async-start(), calls=%async_computation.7 | async-start | bytes 786432
  216.9 243.4 %copy-start.2 = (bf16[1,1024,128]{2,1,0:T(8,128)(2,1)S(1)}, bf16[1,1024,128]{2,1,0:T(8,128)(2,1)}, u32[]{:S(2)}) copy-start(bf16[1,1024,128]{2,1,0:T(8,128)(2,1)} %all-reduce.7.cloned.1.call-done) | copy-start | bytes 786436
  434.7 48.1 %copy-start.5 = (s32[1,1,512,1024]{3,2,1,0:T(8,128)S(1)}, s32[1,1,512,1024]{3,2,1,0:T(8,128)}, u32[]{:S(2)}) copy-start(s32[1,1,512,1024]{3,2,1,0:T(8,128)} %param.12) | copy-start | bytes 6291460
  485.3 1.0 copy-start.6
  488.8 131.1 %all-reduce.11.cloned.1.call-start = ((), (), s32[]{:S(2)}) async-start(), calls=%async_computation.4 | async-start | bytes 524288 | tf_op jit(solution)/shard_map/psum | solution.py:86
  490.6 16.1 %collective-permute-start.1 = (bf16[512,128]{1,0:T(8,128)(2,1)S(1)}, bf16[512,128]{1,0:T(8,128)(2,1)S(1)}, u32[]{:S(2)}, u32[]{:S(2)}) collective-permute-start(bf16[512,128]{1,0:T(8,128)(2,1)S(1)} %dynamic-slice_convert_fusion), channel_id=1, source_target_pairs={{0,1},{1,0},{2,3},{3,2},{4,5},{5,4},{6,7},{7,6},{8,9},{9,8},{10,11... | collective-permute-start | bytes 393224 | tf_op jit(solution)/shard_map/ppermute | solution.py:19
  507.5 311.1 %all-reduce.13.cloned.1.call-start = ((), (), s32[]{:S(2)}) async-start(), calls=%async_computation.5 | async-start | bytes 524288 | tf_op jit(solution)/shard_map/psum | solution.py:87
Sparse Core Ops, SparseCore 0:
  70.0 61.6 reduce-scatter.6
  489.0 49.0 reduce-scatter.8
Sparse Core Ops, SparseCore 1:
  87.3 129.5 all-reduce.6
  220.3 194.9 all-reduce.8
  507.6 112.3 all-reduce.10
  623.7 194.9 all-reduce.12
where the time goes:
time: 847 us; the launch traced here: 846 us
  waiting for transfers between devices  650 us (77%)
  blocking collectives  128 us (15%)
  between operations  17.3 us (2%)
  other arithmetic  15.7 us (2%)
  starting transfers between devices  14.5 us (2%)
  matrix products  11 us (1%)
  local copies, waits for them, and re-layouts  9.59 us (1%)
    psum x2, waiting for transfers between devices, shards(): col_total = lax.psum(col_grad, 'row').astype(jnp.float32)  395 us
    psum x2, waiting for transfers between devices, shards(): lax.psum(row_grad.astype(jnp.bfloat16), 'col').astype(jnp.float32)  162 us
    unnamed x8, waiting for transfers between devices  75.1 us
    all_gather x2, blocking collectives, shards(): lax.all_gather(row_emb, 'dim', axis=2, tiled=True)  50.3 us
    all_gather x2, blocking collectives, shards(): lax.all_gather(col_emb, 'dim', axis=2, tiled=True)  46.9 us
    psum x2, blocking collectives, shards(): lax.psum((jnp.sum(row_total * row_total, axis=2), jnp.sum(col_total * col...  30.8 us
    ppermute x2, waiting for transfers between devices, swapped(): return lax.ppermute(block, axis, route)  17.8 us
  transfers between devices with their start and end apart: 8, of which 8 were waited for; matrix products, arithmetic and copies ran while one was open for 1% of the time, Pallas kernels for 0%

commit v1 on v0

v1 whole, which is shorter than its diff:
```python
import jax
import jax.numpy as jnp
from jax import lax
from jax.sharding import PartitionSpec as P

STEPS = 2
LEARN_RATE = 0.1
SIDE = 1024
HALF_ROWS = 512
WIDTH = 256
HALF_D = 128
N_COL = 16
ROW_PART = HALF_ROWS // N_COL
COL_PART = 128

CORE_PAIRS = [[2 * z, 2 * z + 1] for z in range(8)]
Z_QUADS = [[2 * (4 * h + k) + core for k in range(4)] for h in range(2) for core in range(2)]
FAR_Z = [(i, i ^ 8) for i in range(16)]
DIM_SWAP = [(0, 1), (1, 0)]


def swap_halves(block):
    return jnp.concatenate([block[:, HALF_D:], block[:, :HALF_D]], axis=1)


def adagrad(total, acc, emb):
    squares = total * total
    square = jnp.sum(squares[:, :HALF_D] + squares[:, HALF_D:], axis=1, keepdims=True)
    acc = acc + square / WIDTH
    emb = emb.astype(jnp.float32) - LEARN_RATE * total / jnp.sqrt(acc)
    return emb.astype(jnp.bfloat16), acc


def spread(block, count):
    return jnp.broadcast_to(block[None], (count,) + block.shape)


def split(values):
    high = lax.reduce_precision(values, 8, 7)
    return high.astype(jnp.bfloat16), (values - high).astype(jnp.bfloat16)


def joined(parts):
    high, low = parts
    return high.astype(jnp.float32) + low.astype(jnp.float32)


def with_acc(emb, acc):
    flat = jnp.concatenate(split(acc[:, 0]))
    width = emb.shape[1]
    flat = jnp.pad(flat, (0, 8 * width - flat.shape[0])).reshape(8, width)
    return jnp.concatenate([emb, flat])


def without_acc(blocks, count):
    k, _, width = blocks.shape
    flat = blocks[:, count:].reshape(k, 8 * width)
    parts = flat[:, :count].reshape(-1), flat[:, count : 2 * count].reshape(-1)
    return blocks[:, :count].reshape(k * count, width), parts


def shards(row_emb, col_emb, row_acc, col_acc, counts, live_rows, row_marg, col_marg):
    d, r, c = (lax.axis_index(a) for a in ("dim", "row", "col"))
    core, quad = r % 2, (r // 2) % 4
    row_emb, col_emb = row_emb[0], col_emb[0]

    def rows_at(block, start, size):
        return lax.dynamic_slice_in_dim(block, start, size, 0)

    col_at = core * HALF_ROWS + quad * COL_PART
    row_at = d * HALF_ROWS + c * ROW_PART

    sent = jnp.concatenate(
        [rows_at(row_emb, (1 - d) * HALF_ROWS, HALF_ROWS), rows_at(col_emb, core * HALF_ROWS, HALF_ROWS)]
    )
    got = lax.ppermute(sent, "dim", DIM_SWAP)
    col_other = lax.all_gather(got[HALF_ROWS:], "row", tiled=True, axis_index_groups=CORE_PAIRS)
    rows = jnp.concatenate([rows_at(row_emb, d * HALF_ROWS, HALF_ROWS), got[:HALF_ROWS]], axis=1)
    cols = jnp.concatenate([col_emb, col_other], axis=1)

    log_total = jnp.log(jnp.sum(row_marg).astype(jnp.float32))
    own_marg = lax.dynamic_index_in_dim(row_marg, r, 0, False)
    row_logs = jnp.log(rows_at(own_marg, d * HALF_ROWS, HALF_ROWS).astype(jnp.float32))
    col_logs = jnp.log(lax.dynamic_index_in_dim(col_marg, c, 0, False).astype(jnp.float32))
    shift_log = log_total - row_logs[:, None] - col_logs[None, :]
    tile = counts[0, 0]
    count_f = tile.astype(jnp.float32)
    present = tile > 0
    live = d * HALF_ROWS + jnp.arange(HALF_ROWS, dtype=jnp.int32) < live_rows[0, 0]
    weight = jnp.where(present, (0.1 + 0.25 * jnp.sqrt(count_f)) / SIDE, 0.0)
    target = jnp.log(jnp.maximum(count_f, 1.0)) + shift_log
    weight, target = lax.optimization_barrier((weight, target))

    row_acc = rows_at(row_acc[0], row_at, ROW_PART)[:, None]
    col_acc = rows_at(col_acc[0], col_at, COL_PART)[:, None]

    for step in range(STEPS):
        last = step == STEPS - 1
        scores = lax.dot_general(
            rows, cols, (((1,), (1,)), ((), ())), preferred_element_type=jnp.float32
        )
        gap = scores - target
        cell = jnp.where(weight > 0, weight * gap, jax.nn.sigmoid(gap) / SIDE)
        grad = jnp.where(live[:, None], cell, 0.0).astype(jnp.bfloat16)
        row_term = jnp.dot(grad, cols, preferred_element_type=jnp.float32).astype(jnp.bfloat16)
        col_term = lax.dot_general(
            grad, rows, (((0,), (0,)), ((), ())), preferred_element_type=jnp.float32
        ).astype(jnp.bfloat16)

        kept = rows_at(col_term, core * HALF_ROWS, HALF_ROWS)
        given = rows_at(col_term, (1 - core) * HALF_ROWS, HALF_ROWS)
        pair = lax.all_gather(given, "row", axis_index_groups=CORE_PAIRS)
        taken = lax.dynamic_index_in_dim(pair, 1 - core, 0, False)
        half = (kept.astype(jnp.float32) + taken.astype(jnp.float32)).astype(jnp.bfloat16)
        parts = lax.all_to_all(
            half.reshape(4, COL_PART, WIDTH), "row", 0, 0, axis_index_groups=Z_QUADS
        )
        near = jnp.sum(parts.astype(jnp.float32), axis=0).astype(jnp.bfloat16)
        far = lax.ppermute(near, "row", FAR_Z)

        row_parts = lax.all_to_all(row_term.reshape(N_COL, ROW_PART, WIDTH), "col", 0, 0)
        row_parts, far = lax.optimization_barrier((row_parts, far))

        near = (near.astype(jnp.float32) + far.astype(jnp.float32)).astype(jnp.bfloat16)
        far = lax.ppermute(near, "dim", DIM_SWAP)
        row_total = jnp.sum(row_parts.astype(jnp.float32), axis=0)
        row_new, row_acc = adagrad(row_total, row_acc, rows_at(rows, c * ROW_PART, ROW_PART))
        if last:
            row_new = with_acc(row_new, row_acc)
        rows = lax.all_to_all(spread(row_new, N_COL), "col", 0, 0)
        if last:
            rows, acc_rows = without_acc(rows, ROW_PART)
            rows_far = jnp.concatenate([rows[:, HALF_D:], jnp.concatenate(acc_rows).reshape(8, HALF_D)])
            rows_far = lax.ppermute(rows_far, "dim", DIM_SWAP)
            flat = rows_far[HALF_ROWS:].reshape(-1)
            rows_far, acc_rows_far = rows_far[:HALF_ROWS], (flat[:HALF_ROWS], flat[HALF_ROWS:])
        else:
            rows = rows.reshape(HALF_ROWS, WIDTH)
        col_total = near.astype(jnp.float32) + swap_halves(far).astype(jnp.float32)
        col_new, col_acc = adagrad(col_total, col_acc, rows_at(cols, col_at, COL_PART))
        if last:
            col_new = with_acc(col_new[:, :HALF_D], col_acc)
        quarter = lax.all_to_all(spread(col_new, 4), "row", 0, 0, axis_index_groups=Z_QUADS)
        cols = lax.all_gather(quarter, "row", tiled=True, axis_index_groups=CORE_PAIRS)
        if last:
            cols, acc_cols = without_acc(cols, COL_PART)
        else:
            cols = cols.reshape(SIDE, WIDTH)

    own = rows[:, :HALF_D]
    row_out = jnp.where(
        d == 0, jnp.concatenate([own, rows_far]), jnp.concatenate([rows_far, own])
    )
    acc_own, acc_far = joined(acc_rows), joined(acc_rows_far)
    row_acc_out = jnp.where(
        d == 0, jnp.concatenate([acc_own, acc_far]), jnp.concatenate([acc_far, acc_own])
    )
    return row_out[None], row_acc_out[None], cols[None], joined(acc_cols)[None]


def solution(mesh):
    return jax.shard_map(
        shards,
        mesh=mesh,
        in_specs=(
            P("row", None, "dim"),
            P("col", None, "dim"),
            P("row", None),
            P("col", None),
            P("row", "col", "dim", None),
            P("row", "col"),
            P(),
            P(),
        ),
        out_specs=(P("row", None, "dim"), P("row", None), P("col", None, "dim"), P("col", None)),
        check_vma=False,
    )
```

time: 847 us -> 218 us (0.26)
  the two profiles are of different devices: /device:TPU:8 before, /device:TPU:33 now
where the time goes in v1:
time: 218 us; the launch traced here: 217 us
  starting transfers between devices  95 us (44%)
  waiting for transfers between devices  54.2 us (25%)
  blocking collectives  33.8 us (16%)
  other arithmetic  15.1 us (7%)
  matrix products  10.8 us (5%)
  local copies, waits for them, and re-layouts  5.22 us (2%)
  between operations  2.44 us (1%)
    ppermute x2, starting transfers between devices, shards(): far = lax.ppermute(near, 'dim', DIM_SWAP)  23.8 us
    all_gather x2, blocking collectives, shards(): lax.all_gather(quarter, 'row', tiled=True, axis_index_groups=CORE_PAIRS)  20.1 us
    ppermute x1, starting transfers between devices, shards(): got = lax.ppermute(sent, 'dim', DIM_SWAP)  14.5 us
    ppermute x1, waiting for transfers between devices, shards(): got = lax.ppermute(sent, 'dim', DIM_SWAP)  14 us
    ppermute x2, starting transfers between devices, shards(): far = lax.ppermute(near, 'row', FAR_Z)  12.8 us
    ppermute x1, waiting for transfers between devices, shards(): rows_far = lax.ppermute(rows_far, 'dim', DIM_SWAP)  12.5 us
    all_to_all x2, starting transfers between devices, shards(): lax.all_to_all(spread(col_new, 4), 'row', 0, 0, axis_index_groups=Z_QUADS)  12.3 us
    all_to_all x2, starting transfers between devices, shards(): rows = lax.all_to_all(spread(row_new, N_COL), 'col', 0, 0)  12.2 us
  transfers between devices with their start and end apart: 14, of which 11 were waited for; matrix products, arithmetic and copies ran while one was open for 8% of the time, Pallas kernels for 0%

profile of v1, /device:TPU:33, one launch (start us, length us, event | category | flops | bytes accessed | tf_op | source)
XLA Modules:
  0.0 216.5 jit_solution(2197052222685660711)
XLA Ops:
  1.8 14.5 %collective-permute-start = (bf16[1024,128]{1,0:T(8,128)(2,1)S(1)}, bf16[1024,128]{1,0:T(8,128)(2,1)S(1)}, u32[]{:S(2)}, u32[]{:S(2)}) collective-permute-start(bf16[1024,128]{1,0:T(8,128)(2,1)S(1)} %pad_maximum_fusion.4), channel_id=1, source_target_pairs={{0,1},{1,0},{2,3},{3,2},{4,5},{5,4},{6,7},{7,6},{8,9},{9,8},{10,11... | collective-permute-start | bytes 786440 | tf_op jit(solution)/shard_map/ppermute | solution.py:76
  22.3 2.2 %select_bitcast_fusion = f32[512,1024]{1,0:T(8,128)} fusion(s32[1,1,512,1024]{3,2,1,0:T(8,128)S(1)} %copy-done), kind=kLoop, calls=%fused_computation.1 | loop fusion | flops 3145728 | bytes 4194304 | tf_op jit(solution)/shard_map/jit(_where)/select_n | solution.py:90
  25.2 14.0 %collective-permute-done = bf16[1024,128]{1,0:T(8,128)(2,1)S(1)} collective-permute-done((bf16[1024,128]{1,0:T(8,128)(2,1)S(1)}, bf16[1024,128]{1,0:T(8,128)(2,1)S(1)}, u32[]{:S(2)}, u32[]{:S(2)}) %collective-permute-start) | collective-permute-done | bytes 262176 | tf_op jit(solution)/shard_map/ppermute | solution.py:76
  39.2 3.1 %all_gather.21 = bf16[1024,128]{1,0:T(8,128)(2,1)S(1)} all-gather(bf16[512,128]{1,0:T(8,128)(2,1)S(1)} %get-tuple-element.25), channel_id=1, replica_groups={{0,32},{64,96},{128,160},{192,224},{256,288},{320,352},{384,416},{448,4..., dimensions={0}, use_global_device_ids=true | all-gather | bytes 393216 | tf_op jit(solution)/shard_map/all_gather | solution.py:77
  42.3 2.5 %select_convert_fusion.1 = bf16[512,1024]{1,0:T(8,128)(2,1)S(1)} fusion(f32[512,1024]{1,0:T(8,128)} %select_bitcast_fusion, f32[512,1024]{1,0:T(8,128)S(1)} %bitcast_add_fusion, pred[512]{0:T(512)(128)(4,1)S(1)} %add_compare_fusion, bf16[1024,128]{1,0:T(8,128)(2,1)S(1)} %all_gather.21, bf16[1024,128]{1,0:T(8,128)(2,1)S(1)} %bitcast.78, ...), kind=kOutput, calls=%fused_computation.3 | convolution fusion | flops 275251200 | bytes 6029824 | tf_op jit(solution)/shard_map/dot_general | solution.py:99
  45.4 2.2 %all-gather = bf16[1024,256]{1,0:T(8,128)(2,1)S(1)} all-gather(bf16[512,256]{1,0:T(8,128)(2,1)S(1)} %constant_dynamic-slice_fusion.3), channel_id=2, replica_groups={{0,32},{64,96},{128,160},{192,224},{256,288},{320,352},{384,416},{448,4..., dimensions={0}, use_global_device_ids=true | all-gather | bytes 786432 | tf_op jit(solution)/shard_map/all_gather | solution.py:112
  48.3 3.4 %all-to-all-start.1 = ((bf16[4,128,256]{2,1,0:T(8,128)(2,1)}), bf16[4,128,256]{2,1,0:T(8,128)(2,1)S(1)}, u32[]{:S(2)}, u32[]{:S(2)}) async-start(bf16[4,128,256]{2,1,0:T(8,128)(2,1)} %bitcast.12), calls=%async_computation.1 | async-start | bytes 524288 | tf_op jit(solution)/shard_map/all_to_all | solution.py:115
  51.7 2.4 %convolution_convert_fusion.3 = bf16[512,256]{1,0:T(8,128)(2,1)} fusion(bf16[512,1024]{1,0:T(8,128)(2,1)} %copy-done.3, bf16[1024,128]{1,0:T(8,128)(2,1)S(1)} %all_gather.21, bf16[1024,128]{1,0:T(8,128)(2,1)S(1)} %bitcast.79), kind=kOutput, calls=%fused_computation.7 | convolution fusion | flops 269615104 | bytes 1835008 | tf_op jit(solution)/shard_map/dot_general | solution.py:105
  54.1 3.6 %all-to-all-done.1 = bf16[4,128,256]{2,1,0:T(8,128)(2,1)S(1)} async-done(((bf16[4,128,256]{2,1,0:T(8,128)(2,1)}), bf16[4,128,256]{2,1,0:T(8,128)(2,1)S(1)}, u32[]{:S(2)}, u32[]{:S(2)}) %all-to-all-start.1) | async-done | bytes 262176 | tf_op jit(solution)/shard_map/all_to_all | solution.py:115
  57.7 6.8 %all-to-all-start = ((bf16[16,32,256]{2,1,0:T(8,128)(2,1)}), bf16[16,32,256]{2,1,0:T(8,128)(2,1)S(1)}, u32[]{:S(2)}, u32[]{:S(2)}) async-start(bf16[16,32,256]{2,1,0:T(8,128)(2,1)} %bitcast.84), calls=%async_computation | async-start | bytes 524288 | tf_op jit(solution)/shard_map/all_to_all | solution.py:121
  64.5 6.5 %collective-permute-start.1 = (bf16[128,256]{1,0:T(8,128)(2,1)S(1)}, bf16[128,256]{1,0:T(8,128)(2,1)S(1)}, u32[]{:S(2)}, u32[]{:S(2)}) collective-permute-start(bf16[128,256]{1,0:T(8,128)(2,1)S(1)} %reduce_sum.88), channel_id=1, source_target_pairs={{0,256},{32,288},{64,320},{96,352},{128,384},{160,416},{192,448},{... | collective-permute-start | bytes 196616 | tf_op jit(solution)/shard_map/ppermute | solution.py:119
  71.8 2.4 %collective-permute-done.1 = bf16[128,256]{1,0:T(8,128)(2,1)S(1)} collective-permute-done((bf16[128,256]{1,0:T(8,128)(2,1)S(1)}, bf16[128,256]{1,0:T(8,128)(2,1)S(1)}, u32[]{:S(2)}, u32[]{:S(2)}) %collective-permute-start.1) | collective-permute-done | bytes 65568 | tf_op jit(solution)/shard_map/ppermute | solution.py:119
  74.3 11.9 %collective-permute-start.2 = (bf16[128,256]{1,0:T(8,128)(2,1)S(1)}, bf16[128,256]{1,0:T(8,128)(2,1)S(1)}, u32[]{:S(2)}, u32[]{:S(2)}) collective-permute-start(bf16[128,256]{1,0:T(8,128)(2,1)S(1)} %add_convert_fusion.1), channel_id=1, source_target_pairs={{0,1},{1,0},{2,3},{3,2},{4,5},{5,4},{6,7},{7,6},{8,9},{9,8},{10,11... | collective-permute-start | bytes 196616 | tf_op jit(solution)/shard_map/ppermute | solution.py:125
  86.2 2.5 %collective-permute-done.2 = bf16[128,256]{1,0:T(8,128)(2,1)S(1)} collective-permute-done((bf16[128,256]{1,0:T(8,128)(2,1)S(1)}, bf16[128,256]{1,0:T(8,128)(2,1)S(1)}, u32[]{:S(2)}, u32[]{:S(2)}) %collective-permute-start.2) | collective-permute-done | bytes 65568 | tf_op jit(solution)/shard_map/ppermute | solution.py:125
  90.4 5.0 %all-to-all-start.3 = ((bf16[4,128,256]{2,1,0:T(8,128)(2,1)}), bf16[4,128,256]{2,1,0:T(8,128)(2,1)S(1)}, u32[]{:S(2)}, u32[]{:S(2)}) async-start(bf16[4,128,256]{2,1,0:T(8,128)(2,1)} %broadcast_in_dim.35), calls=%async_computation.3 | async-start | bytes 524288 | tf_op jit(solution)/shard_map/all_to_all | solution.py:143
  96.3 4.4 %all-to-all-done.3 = bf16[4,128,256]{2,1,0:T(8,128)(2,1)S(1)} async-done(((bf16[4,128,256]{2,1,0:T(8,128)(2,1)}), bf16[4,128,256]{2,1,0:T(8,128)(2,1)S(1)}, u32[]{:S(2)}, u32[]{:S(2)}) %all-to-all-start.3) | async-done | bytes 262176 | tf_op jit(solution)/shard_map/all_to_all | solution.py:143
  101.4 5.8 %all-to-all-start.2 = ((bf16[16,32,256]{2,1,0:T(8,128)(2,1)}), bf16[16,32,256]{2,1,0:T(8,128)(2,1)S(1)}, u32[]{:S(2)}, u32[]{:S(2)}) async-start(bf16[16,32,256]{2,1,0:T(8,128)(2,1)} %broadcast_in_dim.33), calls=%async_computation.2 | async-start | bytes 524288 | tf_op jit(solution)/shard_map/all_to_all | solution.py:130
  107.2 9.2 %all_gather.24 = bf16[8,128,256]{2,1,0:T(8,128)(2,1)S(1)} all-gather(bf16[4,128,256]{2,1,0:T(8,128)(2,1)S(1)} %all-to-all-done.3), channel_id=1, replica_groups={{0,32},{64,96},{128,160},{192,224},{256,288},{320,352},{384,416},{448,4..., dimensions={0}, use_global_device_ids=true | all-gather | bytes 786432 | tf_op jit(solution)/shard_map/all_gather | solution.py:144
  116.4 2.5 %select_convert_fusion = bf16[512,1024]{1,0:T(8,128)(2,1)S(1)} fusion(f32[512,1024]{1,0:T(8,128)} %select_bitcast_fusion, f32[512,1024]{1,0:T(8,128)S(1)} %bitcast_add_fusion, bf16[512,256]{1,0:T(8,128)(2,1)S(1)} %bitcast.81, bf16[1024,256]{1,0:T(8,128)(2,1)S(1)} %bitcast.75, pred[512]{0:T(512)(128)(4,1)S(1)} %add_compare_fusion), kind=kOutput, calls=%fused_computation.2 | convolution fusion | flops 273678336 | bytes 6029824 | tf_op jit(solution)/shard_map/dot_general | solution.py:99
  119.5 8.5 %all-gather.1 = bf16[1024,256]{1,0:T(8,128)(2,1)S(1)} all-gather(bf16[512,256]{1,0:T(8,128)(2,1)S(1)} %constant_dynamic-slice_fusion), channel_id=3, replica_groups={{0,32},{64,96},{128,160},{192,224},{256,288},{320,352},{384,416},{448,4..., dimensions={0}, use_global_device_ids=true | all-gather | bytes 786432 | tf_op jit(solution)/shard_map/all_gather | solution.py:112
  128.7 3.7 %all-to-all-start.5 = ((bf16[4,128,256]{2,1,0:T(8,128)(2,1)}), bf16[4,128,256]{2,1,0:T(8,128)(2,1)S(1)}, u32[]{:S(2)}, u32[]{:S(2)}) async-start(bf16[4,128,256]{2,1,0:T(8,128)(2,1)} %bitcast.20), calls=%async_computation.5 | async-start | bytes 524288 | tf_op jit(solution)/shard_map/all_to_all | solution.py:115
  132.4 2.4 %convolution_convert_fusion.2 = bf16[512,256]{1,0:T(8,128)(2,1)} fusion(bf16[512,1024]{1,0:T(8,128)(2,1)} %copy-done.2, bf16[1024,256]{1,0:T(8,128)(2,1)S(1)} %bitcast.76), kind=kOutput, calls=%fused_computation.6 | convolution fusion | flops 268566528 | bytes 1835008 | tf_op jit(solution)/shard_map/dot_general | solution.py:105
  134.8 4.2 %all-to-all-done.5 = bf16[4,128,256]{2,1,0:T(8,128)(2,1)S(1)} async-done(((bf16[4,128,256]{2,1,0:T(8,128)(2,1)}), bf16[4,128,256]{2,1,0:T(8,128)(2,1)S(1)}, u32[]{:S(2)}, u32[]{:S(2)}) %all-to-all-start.5) | async-done | bytes 262176 | tf_op jit(solution)/shard_map/all_to_all | solution.py:115
  139.0 3.5 %all-to-all-start.4 = ((bf16[16,32,256]{2,1,0:T(8,128)(2,1)}), bf16[16,32,256]{2,1,0:T(8,128)(2,1)S(1)}, u32[]{:S(2)}, u32[]{:S(2)}) async-start(bf16[16,32,256]{2,1,0:T(8,128)(2,1)} %bitcast.17), calls=%async_computation.4 | async-start | bytes 524288 | tf_op jit(solution)/shard_map/all_to_all | solution.py:121
  142.6 6.3 %collective-permute-start.3 = (bf16[128,256]{1,0:T(8,128)(2,1)S(1)}, bf16[128,256]{1,0:T(8,128)(2,1)S(1)}, u32[]{:S(2)}, u32[]{:S(2)}) collective-permute-start(bf16[128,256]{1,0:T(8,128)(2,1)S(1)} %reduce_sum.92), channel_id=1, source_target_pairs={{0,256},{32,288},{64,320},{96,352},{128,384},{160,416},{192,448},{... | collective-permute-start | bytes 196616 | tf_op jit(solution)/shard_map/ppermute | solution.py:119
  149.8 2.2 %collective-permute-done.3 = bf16[128,256]{1,0:T(8,128)(2,1)S(1)} collective-permute-done((bf16[128,256]{1,0:T(8,128)(2,1)S(1)}, bf16[128,256]{1,0:T(8,128)(2,1)S(1)}, u32[]{:S(2)}, u32[]{:S(2)}) %collective-permute-start.3) | collective-permute-done | bytes 65568 | tf_op jit(solution)/shard_map/ppermute | solution.py:119
  153.1 11.9 %collective-permute-start.5 = (bf16[128,256]{1,0:T(8,128)(2,1)S(1)}, bf16[128,256]{1,0:T(8,128)(2,1)S(1)}, u32[]{:S(2)}, u32[]{:S(2)}) collective-permute-start(bf16[128,256]{1,0:T(8,128)(2,1)S(1)} %add_convert_fusion), channel_id=1, source_target_pairs={{0,1},{1,0},{2,3},{3,2},{4,5},{5,4},{6,7},{7,6},{8,9},{9,8},{10,11... | collective-permute-start | bytes 196616 | tf_op jit(solution)/shard_map/ppermute | solution.py:125
  165.8 6.4 %all-to-all-start.6 = ((bf16[16,40,256]{2,1,0:T(8,128)(2,1)}), bf16[16,40,256]{2,1,0:T(8,128)(2,1)S(1)}, u32[]{:S(2)}, u32[]{:S(2)}) async-start(bf16[16,40,256]{2,1,0:T(8,128)(2,1)} %broadcast_in_dim.36), calls=%async_computation.6 | async-start | bytes 655360 | tf_op jit(solution)/shard_map/all_to_all | solution.py:130
  173.2 6.7 %all-to-all-done.6 = bf16[16,40,256]{2,1,0:T(8,128)(2,1)S(1)} async-done(((bf16[16,40,256]{2,1,0:T(8,128)(2,1)}), bf16[16,40,256]{2,1,0:T(8,128)(2,1)S(1)}, u32[]{:S(2)}, u32[]{:S(2)}) %all-to-all-start.6) | async-done | bytes 327712 | tf_op jit(solution)/shard_map/all_to_all | solution.py:130
  180.6 7.3 %all-to-all-start.7 = ((bf16[4,136,128]{2,1,0:T(8,128)(2,1)}), bf16[4,136,128]{2,1,0:T(8,128)(2,1)S(1)}, u32[]{:S(2)}, u32[]{:S(2)}) async-start(bf16[4,136,128]{2,1,0:T(8,128)(2,1)} %broadcast_in_dim.37), calls=%async_computation.7 | async-start | bytes 278528 | tf_op jit(solution)/shard_map/all_to_all | solution.py:143
  190.5 12.5 %collective-permute-done.4 = bf16[520,128]{1,0:T(8,128)(2,1)S(1)} collective-permute-done((bf16[520,128]{1,0:T(8,128)(2,1)S(1)}, bf16[520,128]{1,0:T(8,128)(2,1)S(1)}, u32[]{:S(2)}, u32[]{:S(2)}) %collective-permute-start.4) | collective-permute-done | bytes 133152 | tf_op jit(solution)/shard_map/ppermute | solution.py:134
  204.3 10.9 %all_gather.27 = bf16[8,136,128]{2,1,0:T(8,128)(2,1)S(1)} all-gather(bf16[4,136,128]{2,1,0:T(8,128)(2,1)S(1)} %all-to-all-done.7), channel_id=1, replica_groups={{0,32},{64,96},{128,160},{192,224},{256,288},{320,352},{384,416},{448,4..., dimensions={0}, use_global_device_ids=true | all-gather | bytes 417792 | tf_op jit(solution)/shard_map/all_gather | solution.py:144
  (81 shorter events, 22.9 us)
Async XLA Ops:
  1.8 37.5 %collective-permute-start = (bf16[1024,128]{1,0:T(8,128)(2,1)S(1)}, bf16[1024,128]{1,0:T(8,128)(2,1)S(1)}, u32[]{:S(2)}, u32[]{:S(2)}) collective-permute-start(bf16[1024,128]{1,0:T(8,128)(2,1)S(1)} %pad_maximum_fusion.4), channel_id=1, source_target_pairs={{0,1},{1,0},{2,3},{3,2},{4,5},{5,4},{6,7},{7,6},{8,9},{9,8},{10,11... | collective-permute-start | bytes 786440 | tf_op jit(solution)/shard_map/ppermute | solution.py:76
  20.1 2.2 %copy-start = (s32[1,1,512,1024]{3,2,1,0:T(8,128)S(1)}, s32[1,1,512,1024]{3,2,1,0:T(8,128)}, u32[]{:S(2)}) copy-start(s32[1,1,512,1024]{3,2,1,0:T(8,128)} %param.12) | copy-start | bytes 6291460
  22.3 20.0 %copy-start.1 = (bf16[1,1024,128]{2,1,0:T(8,128)(2,1)S(1)}, bf16[1,1024,128]{2,1,0:T(8,128)(2,1)}, u32[]{:S(2)}) copy-start(bf16[1,1024,128]{2,1,0:T(8,128)(2,1)} %param.9) | copy-start | bytes 786436
  44.8 3.5 %copy-start.3 = (bf16[512,1024]{1,0:T(8,128)(2,1)}, bf16[512,1024]{1,0:T(8,128)(2,1)S(1)}, u32[]{:S(2)}) copy-start(bf16[512,1024]{1,0:T(8,128)(2,1)S(1)} %select_convert_fusion.1) | copy-start | bytes 3145732
  48.3 9.4 %all-to-all-start.1 = ((bf16[4,128,256]{2,1,0:T(8,128)(2,1)}), bf16[4,128,256]{2,1,0:T(8,128)(2,1)S(1)}, u32[]{:S(2)}, u32[]{:S(2)}) async-start(bf16[4,128,256]{2,1,0:T(8,128)(2,1)} %bitcast.12), calls=%async_computation.1 | async-start | bytes 524288 | tf_op jit(solution)/shard_map/all_to_all | solution.py:115
  57.7 14.1 %all-to-all-start = ((bf16[16,32,256]{2,1,0:T(8,128)(2,1)}), bf16[16,32,256]{2,1,0:T(8,128)(2,1)S(1)}, u32[]{:S(2)}, u32[]{:S(2)}) async-start(bf16[16,32,256]{2,1,0:T(8,128)(2,1)} %bitcast.84), calls=%async_computation | async-start | bytes 524288 | tf_op jit(solution)/shard_map/all_to_all | solution.py:121
  64.5 9.7 %collective-permute-start.1 = (bf16[128,256]{1,0:T(8,128)(2,1)S(1)}, bf16[128,256]{1,0:T(8,128)(2,1)S(1)}, u32[]{:S(2)}, u32[]{:S(2)}) collective-permute-start(bf16[128,256]{1,0:T(8,128)(2,1)S(1)} %reduce_sum.88), channel_id=1, source_target_pairs={{0,256},{32,288},{64,320},{96,352},{128,384},{160,416},{192,448},{... | collective-permute-start | bytes 196616 | tf_op jit(solution)/shard_map/ppermute | solution.py:119
  74.3 14.4 %collective-permute-start.2 = (bf16[128,256]{1,0:T(8,128)(2,1)S(1)}, bf16[128,256]{1,0:T(8,128)(2,1)S(1)}, u32[]{:S(2)}, u32[]{:S(2)}) collective-permute-start(bf16[128,256]{1,0:T(8,128)(2,1)S(1)} %add_convert_fusion.1), channel_id=1, source_target_pairs={{0,1},{1,0},{2,3},{3,2},{4,5},{5,4},{6,7},{7,6},{8,9},{9,8},{10,11... | collective-permute-start | bytes 196616 | tf_op jit(solution)/shard_map/ppermute | solution.py:125
  90.4 10.3 %all-to-all-start.3 = ((bf16[4,128,256]{2,1,0:T(8,128)(2,1)}), bf16[4,128,256]{2,1,0:T(8,128)(2,1)S(1)}, u32[]{:S(2)}, u32[]{:S(2)}) async-start(bf16[4,128,256]{2,1,0:T(8,128)(2,1)} %broadcast_in_dim.35), calls=%async_computation.3 | async-start | bytes 524288 | tf_op jit(solution)/shard_map/all_to_all | solution.py:143
  101.4 15.0 %all-to-all-start.2 = ((bf16[16,32,256]{2,1,0:T(8,128)(2,1)}), bf16[16,32,256]{2,1,0:T(8,128)(2,1)S(1)}, u32[]{:S(2)}, u32[]{:S(2)}) async-start(bf16[16,32,256]{2,1,0:T(8,128)(2,1)} %broadcast_in_dim.33), calls=%async_computation.2 | async-start | bytes 524288 | tf_op jit(solution)/shard_map/all_to_all | solution.py:130
  119.0 9.8 %copy-start.2 = (bf16[512,1024]{1,0:T(8,128)(2,1)}, bf16[512,1024]{1,0:T(8,128)(2,1)S(1)}, u32[]{:S(2)}) copy-start(bf16[512,1024]{1,0:T(8,128)(2,1)S(1)} %select_convert_fusion) | copy-start | bytes 3145732
  128.7 10.2 %all-to-all-start.5 = ((bf16[4,128,256]{2,1,0:T(8,128)(2,1)}), bf16[4,128,256]{2,1,0:T(8,128)(2,1)S(1)}, u32[]{:S(2)}, u32[]{:S(2)}) async-start(bf16[4,128,256]{2,1,0:T(8,128)(2,1)} %bitcast.20), calls=%async_computation.5 | async-start | bytes 524288 | tf_op jit(solution)/shard_map/all_to_all | solution.py:115
  139.0 10.8 %all-to-all-start.4 = ((bf16[16,32,256]{2,1,0:T(8,128)(2,1)}), bf16[16,32,256]{2,1,0:T(8,128)(2,1)S(1)}, u32[]{:S(2)}, u32[]{:S(2)}) async-start(bf16[16,32,256]{2,1,0:T(8,128)(2,1)} %bitcast.17), calls=%async_computation.4 | async-start | bytes 524288 | tf_op jit(solution)/shard_map/all_to_all | solution.py:121
  142.6 9.4 %collective-permute-start.3 = (bf16[128,256]{1,0:T(8,128)(2,1)S(1)}, bf16[128,256]{1,0:T(8,128)(2,1)S(1)}, u32[]{:S(2)}, u32[]{:S(2)}) collective-permute-start(bf16[128,256]{1,0:T(8,128)(2,1)S(1)} %reduce_sum.92), channel_id=1, source_target_pairs={{0,256},{32,288},{64,320},{96,352},{128,384},{160,416},{192,448},{... | collective-permute-start | bytes 196616 | tf_op jit(solution)/shard_map/ppermute | solution.py:119
  153.1 19.1 %collective-permute-start.5 = (bf16[128,256]{1,0:T(8,128)(2,1)S(1)}, bf16[128,256]{1,0:T(8,128)(2,1)S(1)}, u32[]{:S(2)}, u32[]{:S(2)}) collective-permute-start(bf16[128,256]{1,0:T(8,128)(2,1)S(1)} %add_convert_fusion), channel_id=1, source_target_pairs={{0,1},{1,0},{2,3},{3,2},{4,5},{5,4},{6,7},{7,6},{8,9},{9,8},{10,11... | collective-permute-start | bytes 196616 | tf_op jit(solution)/shard_map/ppermute | solution.py:125
  165.8 14.1 %all-to-all-start.6 = ((bf16[16,40,256]{2,1,0:T(8,128)(2,1)}), bf16[16,40,256]{2,1,0:T(8,128)(2,1)S(1)}, u32[]{:S(2)}, u32[]{:S(2)}) async-start(bf16[16,40,256]{2,1,0:T(8,128)(2,1)} %broadcast_in_dim.36), calls=%async_computation.6 | async-start | bytes 655360 | tf_op jit(solution)/shard_map/all_to_all | solution.py:130
  180.6 23.8 %all-to-all-start.7 = ((bf16[4,136,128]{2,1,0:T(8,128)(2,1)}), bf16[4,136,128]{2,1,0:T(8,128)(2,1)S(1)}, u32[]{:S(2)}, u32[]{:S(2)}) async-start(bf16[4,136,128]{2,1,0:T(8,128)(2,1)} %broadcast_in_dim.37), calls=%async_computation.7 | async-start | bytes 278528 | tf_op jit(solution)/shard_map/all_to_all | solution.py:143
  188.2 14.7 %collective-permute-start.4 = (bf16[520,128]{1,0:T(8,128)(2,1)S(1)}, bf16[520,128]{1,0:T(8,128)(2,1)S(1)}, u32[]{:S(2)}, u32[]{:S(2)}) collective-permute-start(bf16[520,128]{1,0:T(8,128)(2,1)S(1)} %pad_maximum_fusion.7), channel_id=1, source_target_pairs={{0,1},{1,0},{2,3},{3,2},{4,5},{5,4},{6,7},{7,6},{8,9},{9,8},{10,11... | collective-permute-start | bytes 399368 | tf_op jit(solution)/shard_map/ppermute | solution.py:134

commit v2 on v1

v2 whole, which is shorter than its diff:
```python
import jax
import jax.numpy as jnp
from jax import lax
from jax.experimental import pallas as pl
from jax.experimental.pallas import tpu as pltpu
from jax.sharding import PartitionSpec as P

STEPS = 2
LEARN_RATE = 0.1
SIDE = 1024
HALF_ROWS = 512
WIDTH = 256
HALF_D = 128
N_COL = 16
ROW_PART = HALF_ROWS // N_COL
COL_PART = 128
FAR_ROWS = COL_PART + ROW_PART

C_PAIR, C_ROW, C_COL = 20, 1, 20

CORE_PAIRS = [[2 * z, 2 * z + 1] for z in range(8)]
Z_QUADS = [[2 * (4 * h + k) + core for k in range(4)] for h in range(2) for core in range(2)]
FAR_Z = [(i, i ^ 8) for i in range(16)]
DIM_SWAP = [(0, 1), (1, 0)]


def swap_halves(block):
    return jnp.concatenate([block[:, HALF_D:], block[:, :HALF_D]], axis=1)


def adagrad(total, acc, emb):
    squares = total * total
    square = jnp.sum(squares[:, :HALF_D] + squares[:, HALF_D:], axis=1, keepdims=True)
    acc = acc + square / WIDTH
    emb = emb.astype(jnp.float32) - LEARN_RATE * total / jnp.sqrt(acc)
    return emb.astype(jnp.bfloat16), acc


def acc_lanes(acc, start, width):
    high = acc.astype(jnp.bfloat16).astype(jnp.float32)
    lane = lax.broadcasted_iota(jnp.int32, (acc.shape[0], HALF_D), 1) - start
    part = jnp.where(lane < width, high, acc - high)
    return jnp.where((lane >= 0) & (lane < 2 * width), part, 0.0).astype(jnp.bfloat16)


def pair_kernel(part, mine, theirs, both):
    both[...] = (mine[...].astype(jnp.float32) + theirs[...].astype(jnp.float32)).astype(jnp.bfloat16)


def row_kernel(part, parts, acc, emb, emb_out, acc_out):
    total = jnp.sum(parts[...].astype(jnp.float32), axis=0)
    emb_new, acc_out[...] = adagrad(total, acc[...], emb[0])
    emb_out[...] = jnp.broadcast_to(emb_new[None], emb_out.shape)


def row_last_kernel(part, parts, acc, emb, near, kept, sent):
    total = jnp.sum(parts[...].astype(jnp.float32), axis=0)
    emb_new, acc_new = adagrad(total, acc[...], emb[0])
    kept[:, :HALF_D] = emb_new[:, :HALF_D]
    kept[:, HALF_D:] = acc_lanes(acc_new, 0, 32)
    sent[:COL_PART, :] = near[...]
    sent[COL_PART:, :HALF_D] = emb_new[:, HALF_D:]
    sent[COL_PART:, HALF_D:] = acc_lanes(acc_new, 64, 32)


def col_kernel(part, mine, theirs, acc, emb, emb_out, acc_out):
    total = mine[...].astype(jnp.float32) + swap_halves(theirs[...].astype(jnp.float32))
    emb_new, acc_out[...] = adagrad(total, acc[...], emb[0])
    emb_out[...] = jnp.broadcast_to(emb_new[None], emb_out.shape)


def col_last_kernel(part, mine, theirs, acc, emb, kept, col_out, row_out):
    total = mine[...].astype(jnp.float32) + swap_halves(theirs[:COL_PART, :].astype(jnp.float32))
    emb_new, acc_new = adagrad(total, acc[...], emb[0])
    col_new = jnp.concatenate([emb_new[:, :HALF_D], acc_lanes(acc_new, 0, 64)], axis=1)
    col_out[...] = jnp.broadcast_to(col_new[None], col_out.shape)
    there = theirs[COL_PART:, :]
    here = kept[...]
    both = (here[:, HALF_D:].astype(jnp.float32) + there[:, HALF_D:].astype(jnp.float32)).astype(jnp.bfloat16)
    row_new = jnp.concatenate([here[:, :HALF_D], there[:, :HALF_D], both], axis=1)
    row_out[...] = jnp.broadcast_to(row_new[None], row_out.shape)


def on_device(kernel, part, operands, shapes, micros, chunk=None):
    def whole(shape):
        zeros = (0,) * len(shape)
        return pl.BlockSpec(shape, lambda i, s: zeros)

    def one(shape):
        rest = (0,) * (len(shape) - 1)
        return pl.BlockSpec((1,) + shape[1:], lambda i, s: (s[0],) + rest)

    return pl.pallas_call(
        kernel,
        grid_spec=pltpu.PrefetchScalarGridSpec(
            num_scalar_prefetch=1,
            grid=(1,),
            in_specs=[one(o.shape) if k == chunk else whole(o.shape) for k, o in enumerate(operands)],
            out_specs=[whole(o.shape) for o in shapes],
        ),
        out_shape=shapes,
        cost_estimate=pl.CostEstimate(flops=micros * 10**9, bytes_accessed=1 << 20, transcendentals=0),
    )(part, *operands)


def bf16(*shape):
    return jax.ShapeDtypeStruct(shape, jnp.bfloat16)


def f32(*shape):
    return jax.ShapeDtypeStruct(shape, jnp.float32)


def spread(block, count):
    return jnp.broadcast_to(block[None], (count,) + block.shape)


def joined(block, high, low):
    return (block[:, :, high].astype(jnp.float32) + block[:, :, low].astype(jnp.float32)).reshape(-1)


def shards(row_emb, col_emb, row_acc, col_acc, counts, live_rows, row_marg, col_marg):
    d, r, c = (lax.axis_index(a) for a in ("dim", "row", "col"))
    core, quad = r % 2, (r // 2) % 4
    row_emb, col_emb = row_emb[0], col_emb[0]
    col_part = core * 4 + quad

    def rows_at(block, start, size):
        return lax.dynamic_slice_in_dim(block, start, size, 0)

    col_got = lax.ppermute(rows_at(col_emb, col_part * COL_PART, COL_PART), "dim", DIM_SWAP)
    row_got = lax.ppermute(rows_at(row_emb, (1 - d) * HALF_ROWS, HALF_ROWS), "dim", DIM_SWAP)
    col_other = lax.all_to_all(spread(col_got, 4), "row", 0, 0, axis_index_groups=Z_QUADS)
    col_other = lax.all_gather(col_other, "row", tiled=True, axis_index_groups=CORE_PAIRS)
    rows = jnp.concatenate([rows_at(row_emb, d * HALF_ROWS, HALF_ROWS), row_got], axis=1)
    cols = jnp.concatenate([col_emb, col_other.reshape(SIDE, HALF_D)], axis=1)

    log_total = jnp.log(jnp.sum(row_marg).astype(jnp.float32))
    own_marg = lax.dynamic_index_in_dim(row_marg, r, 0, False)
    row_logs = jnp.log(rows_at(own_marg, d * HALF_ROWS, HALF_ROWS).astype(jnp.float32))
    col_logs = jnp.log(lax.dynamic_index_in_dim(col_marg, c, 0, False).astype(jnp.float32))
    shift_log = log_total - row_logs[:, None] - col_logs[None, :]
    tile = counts[0, 0]
    count_f = tile.astype(jnp.float32)
    present = tile > 0
    live = d * HALF_ROWS + jnp.arange(HALF_ROWS, dtype=jnp.int32) < live_rows[0, 0]
    weight = jnp.where(present, (0.1 + 0.25 * jnp.sqrt(count_f)) / SIDE, 0.0)
    target = jnp.log(jnp.maximum(count_f, 1.0)) + shift_log
    row_acc = rows_at(row_acc[0], d * HALF_ROWS + c * ROW_PART, ROW_PART)[:, None]
    col_acc = rows_at(col_acc[0], col_part * COL_PART, COL_PART)[:, None]
    row_at, col_at = c.reshape(1).astype(jnp.int32), col_part.reshape(1).astype(jnp.int32)
    weight, target, row_acc, col_acc, row_at, col_at = lax.optimization_barrier(
        (weight, target, row_acc, col_acc, row_at, col_at)
    )

    for step in range(STEPS):
        last = step == STEPS - 1
        scores = lax.dot_general(
            rows, cols, (((1,), (1,)), ((), ())), preferred_element_type=jnp.float32
        )
        gap = scores - target
        cell = jnp.where(weight > 0, weight * gap, jax.nn.sigmoid(gap) / SIDE)
        grad = jnp.where(live[:, None], cell, 0.0).astype(jnp.bfloat16)
        col_term = lax.dot_general(
            grad, rows, (((0,), (0,)), ((), ())), preferred_element_type=jnp.float32
        ).astype(jnp.bfloat16)

        kept = rows_at(col_term, core * HALF_ROWS, HALF_ROWS)
        given = rows_at(col_term, (1 - core) * HALF_ROWS, HALF_ROWS)
        pair = lax.all_gather(given, "row", axis_index_groups=CORE_PAIRS)
        taken = lax.dynamic_index_in_dim(pair, 1 - core, 0, False)
        half = (kept.astype(jnp.float32) + taken.astype(jnp.float32)).astype(jnp.bfloat16)
        parts = lax.all_to_all(
            half.reshape(4, COL_PART, WIDTH), "row", 0, 0, axis_index_groups=Z_QUADS
        )
        near = jnp.sum(parts.astype(jnp.float32), axis=0).astype(jnp.bfloat16)
        grad, near = lax.optimization_barrier((grad, near))
        far = lax.ppermute(near, "row", FAR_Z)

        row_term = jnp.dot(grad, cols, preferred_element_type=jnp.float32).astype(jnp.bfloat16)
        row_parts = lax.all_to_all(row_term.reshape(N_COL, ROW_PART, WIDTH), "col", 0, 0)
        (near,) = on_device(pair_kernel, row_at, (near, far), (bf16(COL_PART, WIDTH),), C_PAIR)
        rows = rows.reshape(N_COL, ROW_PART, WIDTH)
        cols = cols.reshape(8, COL_PART, WIDTH)
        if not last:
            far = lax.ppermute(near, "dim", DIM_SWAP)
            rows, row_acc = on_device(
                row_kernel,
                row_at,
                (row_parts, row_acc, rows),
                (bf16(N_COL, ROW_PART, WIDTH), f32(ROW_PART, 1)),
                C_ROW,
                2,
            )
            rows = lax.all_to_all(rows, "col", 0, 0).reshape(HALF_ROWS, WIDTH)
            cols, col_acc = on_device(
                col_kernel,
                col_at,
                (near, far, col_acc, cols),
                (bf16(4, COL_PART, WIDTH), f32(COL_PART, 1)),
                C_COL,
                3,
            )
            rows, cols = lax.optimization_barrier((rows, cols))
            cols = lax.all_to_all(cols, "row", 0, 0, axis_index_groups=Z_QUADS)
            cols = lax.all_gather(cols, "row", tiled=True, axis_index_groups=CORE_PAIRS)
            cols = cols.reshape(SIDE, WIDTH)
            continue

        kept, sent = on_device(
            row_last_kernel,
            row_at,
            (row_parts, row_acc, rows, near),
            (bf16(ROW_PART, WIDTH), bf16(FAR_ROWS, WIDTH)),
            1,
            2,
        )
        far = lax.ppermute(sent, "dim", DIM_SWAP)
        cols, rows = on_device(
            col_last_kernel,
            col_at,
            (near, far, col_acc, cols, kept),
            (bf16(4, COL_PART, WIDTH), bf16(N_COL, ROW_PART, WIDTH + HALF_D)),
            1,
            3,
        )
        cols = lax.all_to_all(cols, "row", 0, 0, axis_index_groups=Z_QUADS)
        rows, cols = lax.optimization_barrier((rows, cols))
        rows = lax.all_to_all(rows, "col", 0, 0)
        cols = lax.all_gather(cols, "row", tiled=True, axis_index_groups=CORE_PAIRS)
        rows, cols = lax.optimization_barrier((rows, cols))
    here = rows[:, :, :HALF_D].reshape(HALF_ROWS, HALF_D)
    there = rows[:, :, HALF_D:WIDTH].reshape(HALF_ROWS, HALF_D)
    row_out = jnp.where(d == 0, jnp.concatenate([here, there]), jnp.concatenate([there, here]))
    here = joined(rows, WIDTH, WIDTH + 32)
    there = joined(rows, WIDTH + 64, WIDTH + 96)
    row_acc_out = jnp.where(d == 0, jnp.concatenate([here, there]), jnp.concatenate([there, here]))
    col_out = cols[:, :, :HALF_D].reshape(SIDE, HALF_D)
    col_acc_out = joined(cols, HALF_D, HALF_D + 64)
    return row_out[None], row_acc_out[None], col_out[None], col_acc_out[None]


def solution(mesh):
    return jax.shard_map(
        shards,
        mesh=mesh,
        in_specs=(
            P("row", None, "dim"),
            P("col", None, "dim"),
            P("row", None),
            P("col", None),
            P("row", "col", "dim", None),
            P("row", "col"),
            P(),
            P(),
        ),
        out_specs=(P("row", None, "dim"), P("row", None), P("col", None, "dim"), P("col", None)),
        check_vma=False,
    )
```

time: 218 us -> 207 us (0.950)
  the two profiles are of different devices: /device:TPU:33 before, /device:TPU:32 now
where the time goes in v2:
time: 207 us; the launch traced here: 205 us
  starting transfers between devices  75.5 us (36%)
  blocking collectives  43.6 us (21%)
  waiting for transfers between devices  38.8 us (19%)
  other arithmetic  13.6 us (7%)
  Pallas kernels  10.6 us (5%)
  matrix products  10.4 us (5%)
  local copies, waits for them, and re-layouts  9.83 us (5%)
  between operations  2.41 us (1%)
    all_to_all x2, blocking collectives, shards(): cols = lax.all_to_all(cols, 'row', 0, 0, axis_index_groups=Z_QUADS)  22 us
    ppermute x1, starting transfers between devices, shards(): lax.ppermute(rows_at(col_emb, col_part * COL_PART, COL_PART), 'dim', DIM_...  14.8 us
    ppermute x1, waiting for transfers between devices, shards(): far = lax.ppermute(sent, 'dim', DIM_SWAP)  13.1 us
    ppermute x2, starting transfers between devices, shards(): far = lax.ppermute(near, 'row', FAR_Z)  12.8 us
    all_to_all x1, blocking collectives, shards(): lax.all_to_all(half.reshape(4, COL_PART, WIDTH), 'row', 0, 0, axis_index_...  11 us
    all_to_all x2, starting transfers between devices, shards(): lax.all_to_all(row_term.reshape(N_COL, ROW_PART, WIDTH), 'col', 0, 0)  10.7 us
    pallas_call x6, Pallas kernels, on_device(): pl.pallas_call(kernel, grid_spec=pltpu.PrefetchScalarGridSpec(num_scalar_...  10.6 us
    all_to_all x1, starting transfers between devices, shards(): rows = lax.all_to_all(rows, 'col', 0, 0).reshape(HALF_ROWS, WIDTH)  7.21 us
  transfers between devices with their start and end apart: 12, of which 7 were waited for; matrix products, arithmetic and copies ran while one was open for 9% of the time, Pallas kernels for 3%

profile of v2, /device:TPU:32, one launch (start us, length us, event | category | flops | bytes accessed | tf_op | source)
XLA Modules:
  0.0 204.9 jit_solution(10128897785015671468)
XLA Ops:
  1.5 14.8 %collective-permute-start.1 = (bf16[128,128]{1,0:T(8,128)(2,1)S(1)}, bf16[128,128]{1,0:T(8,128)(2,1)S(1)}, u32[]{:S(2)}, u32[]{:S(2)}) collective-permute-start(bf16[128,128]{1,0:T(8,128)(2,1)S(1)} %dynamic-slice_bitcast_fusion.1), channel_id=1, source_target_pairs={{0,1},{1,0},{2,3},{3,2},{4,5},{5,4},{6,7},{7,6},{8,9},{9,8},{10,11... | collective-permute-start | bytes 98312 | tf_op jit(solution)/shard_map/ppermute | solution.py:131
  17.3 1.9 collective-permute-start
  23.1 3.5 %bitcast_add_fusion = f32[512,1024]{1,0:T(8,128)} fusion(s32[1,1,512,1024]{3,2,1,0:T(8,128)} %param.12, f32[1024]{0:T(1024)S(1)} %bitcast.70, f32[512]{0:T(512)S(1)} %bitcast.71), kind=kLoop, calls=%fused_computation | loop fusion | flops 2097152 | bytes 4200448 | tf_op jit(solution)/shard_map/add | solution.py:148
  27.9 6.6 %all-to-all-start = ((bf16[4,128,128]{2,1,0:T(8,128)(2,1)}), bf16[4,128,128]{2,1,0:T(8,128)(2,1)S(1)}, u32[]{:S(2)}, u32[]{:S(2)}) async-start(bf16[4,128,128]{2,1,0:T(8,128)(2,1)} %broadcast_in_dim.40), calls=%async_computation | async-start | bytes 262144 | tf_op jit(solution)/shard_map/all_to_all | solution.py:133
  34.5 2.2 %select_bitcast_fusion = f32[512,1024]{1,0:T(8,128)} fusion(s32[1,1,512,1024]{3,2,1,0:T(8,128)S(1)} %copy-done.1), kind=kLoop, calls=%fused_computation.1 | loop fusion | flops 3145728 | bytes 4194304 | tf_op jit(solution)/shard_map/jit(_where)/select_n | solution.py:147
  37.4 2.3 %all-to-all-done = bf16[4,128,128]{2,1,0:T(8,128)(2,1)S(1)} async-done(((bf16[4,128,128]{2,1,0:T(8,128)(2,1)}), bf16[4,128,128]{2,1,0:T(8,128)(2,1)S(1)}, u32[]{:S(2)}, u32[]{:S(2)}) %all-to-all-start) | async-done | bytes 131104 | tf_op jit(solution)/shard_map/all_to_all | solution.py:133
  39.7 2.0 all_gather.21
  41.7 3.2 %select_convert_fusion.1 = bf16[512,1024]{1,0:T(8,128)(2,1)S(1)} fusion(f32[512,1024]{1,0:T(8,128)} %select_bitcast_fusion, f32[512,1024]{1,0:T(8,128)} %bitcast_add_fusion, pred[512]{0:T(512)(128)(4,1)S(1)} %add_compare_fusion, bf16[1024,128]{1,0:T(8,128)(2,1)S(1)} %bitcast.54, bf16[1024,128]{1,0:T(8,128)(2,1)S(1)} %bitcast.63, ...), kind=kOutput, calls=%fused_computation.3 | convolution fusion | flops 275251200 | bytes 6029824 | tf_op jit(solution)/shard_map/dot_general | solution.py:158
  45.4 2.2 %all-gather = bf16[1024,256]{1,0:T(8,128)(2,1)S(1)} all-gather(bf16[512,256]{1,0:T(8,128)(2,1)S(1)} %constant_dynamic-slice_fusion), channel_id=2, replica_groups={{0,32},{64,96},{128,160},{192,224},{256,288},{320,352},{384,416},{448,4..., dimensions={0}, use_global_device_ids=true | all-gather | bytes 786432 | tf_op jit(solution)/shard_map/all_gather | solution.py:170
  48.3 4.6 %all-to-all-start.1 = ((bf16[4,128,256]{2,1,0:T(8,128)(2,1)}), bf16[4,128,256]{2,1,0:T(8,128)(2,1)S(1)}, u32[]{:S(2)}, u32[]{:S(2)}) async-start(bf16[4,128,256]{2,1,0:T(8,128)(2,1)} %bitcast.16), calls=%async_computation.1 | async-start | bytes 524288 | tf_op jit(solution)/shard_map/all_to_all | solution.py:173
  56.0 4.2 %all-to-all-done.1 = bf16[4,128,256]{2,1,0:T(8,128)(2,1)S(1)} async-done(((bf16[4,128,256]{2,1,0:T(8,128)(2,1)}), bf16[4,128,256]{2,1,0:T(8,128)(2,1)S(1)}, u32[]{:S(2)}, u32[]{:S(2)}) %all-to-all-start.1) | async-done | bytes 262176 | tf_op jit(solution)/shard_map/all_to_all | solution.py:173
  60.3 7.3 %collective-permute-start.2 = (bf16[128,256]{1,0:T(8,128)(2,1)S(1)}, bf16[128,256]{1,0:T(8,128)(2,1)S(1)}, u32[]{:S(2)}, u32[]{:S(2)}) collective-permute-start(bf16[128,256]{1,0:T(8,128)(2,1)S(1)} %reduce_sum.34.mine), channel_id=1, source_target_pairs={{0,256},{32,288},{64,320},{96,352},{128,384},{160,416},{192,448},{... | collective-permute-start | bytes 196616 | tf_op jit(solution)/shard_map/ppermute | solution.py:178
  68.7 7.1 %all-to-all-start.2 = ((bf16[16,32,256]{2,1,0:T(8,128)(2,1)}), bf16[16,32,256]{2,1,0:T(8,128)(2,1)S(1)}, u32[]{:S(2)}, u32[]{:S(2)}) async-start(bf16[16,32,256]{2,1,0:T(8,128)(2,1)} %bitcast.17), calls=%async_computation.2 | async-start | bytes 524288 | tf_op jit(solution)/shard_map/all_to_all | solution.py:181
  78.0 7.1 %collective-permute-start.3 = (bf16[128,256]{1,0:T(8,128)(2,1)}, bf16[128,256]{1,0:T(8,128)(2,1)S(1)}, u32[]{:S(2)}, u32[]{:S(2)}) collective-permute-start(bf16[128,256]{1,0:T(8,128)(2,1)} %shard_map.112.mine), channel_id=1, source_target_pairs={{0,1},{1,0},{2,3},{3,2},{4,5},{5,4},{6,7},{7,6},{8,9},{9,8},{10,11... | collective-permute-start | bytes 196616 | tf_op jit(solution)/shard_map/ppermute | solution.py:186
  87.7 7.2 %all-to-all-start.3 = ((bf16[16,32,256]{2,1,0:T(8,128)(2,1)}), bf16[16,32,256]{2,1,0:T(8,128)(2,1)S(1)}, u32[]{:S(2)}, u32[]{:S(2)}) async-start(bf16[16,32,256]{2,1,0:T(8,128)(2,1)} %get-tuple-element.34), calls=%async_computation.3 | async-start | bytes 524288 | tf_op jit(solution)/shard_map/all_to_all | solution.py:195
  97.4 6.0 %all-to-all-done.3 = bf16[16,32,256]{2,1,0:T(8,128)(2,1)S(1)} async-done(((bf16[16,32,256]{2,1,0:T(8,128)(2,1)}), bf16[16,32,256]{2,1,0:T(8,128)(2,1)S(1)}, u32[]{:S(2)}, u32[]{:S(2)}) %all-to-all-start.3) | async-done | bytes 262176 | tf_op jit(solution)/shard_map/all_to_all | solution.py:195
  103.4 11.5 %all_to_all.45 = bf16[4,128,256]{2,1,0:T(8,128)(2,1)S(1)} all-to-all(bf16[4,128,256]{2,1,0:T(8,128)(2,1)} %get-tuple-element.39), channel_id=1, replica_groups={{0,64,128,192},{32,96,160,224},{256,320,384,448},{288,352,416,480},{1,6..., dimensions={0} | all-to-all | bytes 524288 | tf_op jit(solution)/shard_map/all_to_all | solution.py:205
  114.9 2.2 %all_gather.24.emb = bf16[8,128,256]{2,1,0:T(8,128)(2,1)S(1)} all-gather(bf16[4,128,256]{2,1,0:T(8,128)(2,1)S(1)} %all_to_all.45), channel_id=1, replica_groups={{0,32},{64,96},{128,160},{192,224},{256,288},{320,352},{384,416},{448,4..., dimensions={0}, use_global_device_ids=true | all-gather | bytes 786432 | tf_op jit(solution)/shard_map/all_gather | solution.py:206
  117.1 2.8 %select_convert_fusion = bf16[512,1024]{1,0:T(8,128)(2,1)S(1)} fusion(f32[512,1024]{1,0:T(8,128)} %select_bitcast_fusion, f32[512,1024]{1,0:T(8,128)S(1)} %copy-done.2, bf16[512,256]{1,0:T(8,128)(2,1)S(1)} %bitcast.66, bf16[1024,256]{1,0:T(8,128)(2,1)S(1)} %bitcast.56, pred[512]{0:T(512)(128)(4,1)S(1)} %add_compare_fusion), kind=kOutput, calls=%fused_computation.2 | convolution fusion | flops 273678336 | bytes 6029824 | tf_op jit(solution)/shard_map/dot_general | solution.py:158
  120.4 2.2 %all-gather.1 = bf16[1024,256]{1,0:T(8,128)(2,1)S(1)} all-gather(bf16[512,256]{1,0:T(8,128)(2,1)S(1)} %constant_dynamic-slice_fusion.1), channel_id=3, replica_groups={{0,32},{64,96},{128,160},{192,224},{256,288},{320,352},{384,416},{448,4..., dimensions={0}, use_global_device_ids=true | all-gather | bytes 786432 | tf_op jit(solution)/shard_map/all_gather | solution.py:170
  122.7 11.0 %all_to_all.46 = bf16[4,128,256]{2,1,0:T(8,128)(2,1)S(1)} all-to-all(bf16[4,128,256]{2,1,0:T(8,128)(2,1)S(1)} %bitcast.53), channel_id=1, replica_groups={{0,64,128,192},{32,96,160,224},{256,320,384,448},{288,352,416,480},{1,6..., dimensions={0} | all-to-all | bytes 524288 | tf_op jit(solution)/shard_map/all_to_all | solution.py:173
  133.7 5.5 %collective-permute-start.4 = (bf16[128,256]{1,0:T(8,128)(2,1)S(1)}, bf16[128,256]{1,0:T(8,128)(2,1)S(1)}, u32[]{:S(2)}, u32[]{:S(2)}) collective-permute-start(bf16[128,256]{1,0:T(8,128)(2,1)S(1)} %reduce_sum.35.mine), channel_id=1, source_target_pairs={{0,256},{32,288},{64,320},{96,352},{128,384},{160,416},{192,448},{... | collective-permute-start | bytes 196616 | tf_op jit(solution)/shard_map/ppermute | solution.py:178
  139.2 2.4 %convolution_convert_fusion.2 = bf16[512,256]{1,0:T(8,128)(2,1)} fusion(bf16[512,1024]{1,0:T(8,128)(2,1)} %copy-done.14, bf16[1024,256]{1,0:T(8,128)(2,1)S(1)} %bitcast.57), kind=kOutput, calls=%fused_computation.6 | convolution fusion | flops 268566528 | bytes 1835008 | tf_op jit(solution)/shard_map/dot_general | solution.py:180
  141.6 3.7 %all-to-all-start.6 = ((bf16[16,32,256]{2,1,0:T(8,128)(2,1)}), bf16[16,32,256]{2,1,0:T(8,128)(2,1)S(1)}, u32[]{:S(2)}, u32[]{:S(2)}) async-start(bf16[16,32,256]{2,1,0:T(8,128)(2,1)} %bitcast.26), calls=%async_computation.6 | async-start | bytes 524288 | tf_op jit(solution)/shard_map/all_to_all | solution.py:181
  147.8 5.9 %all-to-all-done.6.parts = bf16[16,32,256]{2,1,0:T(8,128)(2,1)S(1)} async-done(((bf16[16,32,256]{2,1,0:T(8,128)(2,1)}), bf16[16,32,256]{2,1,0:T(8,128)(2,1)S(1)}, u32[]{:S(2)}, u32[]{:S(2)}) %all-to-all-start.6) | async-done | bytes 262176 | tf_op jit(solution)/shard_map/all_to_all | solution.py:181
  156.3 5.5 %collective-permute-start.5 = (bf16[160,256]{1,0:T(8,128)(2,1)}, bf16[160,256]{1,0:T(8,128)(2,1)S(1)}, u32[]{:S(2)}, u32[]{:S(2)}) collective-permute-start(bf16[160,256]{1,0:T(8,128)(2,1)} %get-tuple-element.43), channel_id=1, source_target_pairs={{0,1},{1,0},{2,3},{3,2},{4,5},{5,4},{6,7},{7,6},{8,9},{9,8},{10,11... | collective-permute-start | bytes 245768 | tf_op jit(solution)/shard_map/ppermute | solution.py:218
  161.8 13.1 %collective-permute-done.5.theirs = bf16[160,256]{1,0:T(8,128)(2,1)S(1)} collective-permute-done((bf16[160,256]{1,0:T(8,128)(2,1)}, bf16[160,256]{1,0:T(8,128)(2,1)S(1)}, u32[]{:S(2)}, u32[]{:S(2)}) %collective-permute-start.5) | collective-permute-done | bytes 81952 | tf_op jit(solution)/shard_map/ppermute | solution.py:218
  175.5 2.0 shard_map.116
  177.4 10.4 %all_to_all.47 = bf16[4,128,256]{2,1,0:T(8,128)(2,1)S(1)} all-to-all(bf16[4,128,256]{2,1,0:T(8,128)(2,1)} %get-tuple-element.47), channel_id=1, replica_groups={{0,64,128,192},{32,96,160,224},{256,320,384,448},{288,352,416,480},{1,6..., dimensions={0} | all-to-all | bytes 524288 | tf_op jit(solution)/shard_map/all_to_all | solution.py:227
  187.9 4.2 %all-to-all-start.8 = ((bf16[16,32,384]{2,1,0:T(8,128)(2,1)}), bf16[16,32,384]{2,1,0:T(8,128)(2,1)S(1)}, u32[]{:S(2)}, u32[]{:S(2)}) async-start(bf16[16,32,384]{2,1,0:T(8,128)(2,1)} %get-tuple-element.48), calls=%async_computation.8 | async-start | bytes 786432 | tf_op jit(solution)/shard_map/all_to_all | solution.py:229
  192.1 2.2 %all_gather.27 = bf16[8,128,256]{2,1,0:T(8,128)(2,1)S(1)} all-gather(bf16[4,128,256]{2,1,0:T(8,128)(2,1)S(1)} %all_to_all.47), channel_id=1, replica_groups={{0,32},{64,96},{128,160},{192,224},{256,288},{320,352},{384,416},{448,4..., dimensions={0}, use_global_device_ids=true | all-gather | bytes 786432 | tf_op jit(solution)/shard_map/all_gather | solution.py:230
  194.3 6.9 %all-to-all-done.8 = bf16[16,32,384]{2,1,0:T(8,128)(2,1)S(1)} async-done(((bf16[16,32,384]{2,1,0:T(8,128)(2,1)}), bf16[16,32,384]{2,1,0:T(8,128)(2,1)S(1)}, u32[]{:S(2)}, u32[]{:S(2)}) %all-to-all-start.8) | async-done | bytes 393248 | tf_op jit(solution)/shard_map/all_to_all | solution.py:229
  (72 shorter events, 29.0 us)
Async XLA Ops:
  0.6 18.6 %copy-start = (f32[1,1024]{1,0:T(1,128)S(1)}, f32[1,1024]{1,0:T(1,128)}, u32[]{:S(2)}) copy-start(f32[1,1024]{1,0:T(1,128)} %param.11) | copy-start | bytes 12292
  1.5 25.8 %collective-permute-start.1 = (bf16[128,128]{1,0:T(8,128)(2,1)S(1)}, bf16[128,128]{1,0:T(8,128)(2,1)S(1)}, u32[]{:S(2)}, u32[]{:S(2)}) collective-permute-start(bf16[128,128]{1,0:T(8,128)(2,1)S(1)} %dynamic-slice_bitcast_fusion.1), channel_id=1, source_target_pairs={{0,1},{1,0},{2,3},{3,2},{4,5},{5,4},{6,7},{7,6},{8,9},{9,8},{10,11... | collective-permute-start | bytes 98312 | tf_op jit(solution)/shard_map/ppermute | solution.py:131
  17.3 24.4 %collective-permute-start = (bf16[512,128]{1,0:T(8,128)(2,1)S(1)}, bf16[512,128]{1,0:T(8,128)(2,1)S(1)}, u32[]{:S(2)}, u32[]{:S(2)}) collective-permute-start(bf16[512,128]{1,0:T(8,128)(2,1)S(1)} %get-tuple-element.57), channel_id=1, source_target_pairs={{0,1},{1,0},{2,3},{3,2},{4,5},{5,4},{6,7},{7,6},{8,9},{9,8},{10,11... | collective-permute-start | bytes 393224 | tf_op jit(solution)/shard_map/ppermute | solution.py:132
  23.0 11.5 %copy-start.1 = (s32[1,1,512,1024]{3,2,1,0:T(8,128)S(1)}, s32[1,1,512,1024]{3,2,1,0:T(8,128)}, u32[]{:S(2)}) copy-start(s32[1,1,512,1024]{3,2,1,0:T(8,128)} %param.12) | copy-start | bytes 6291460
  27.9 11.8 %all-to-all-start = ((bf16[4,128,128]{2,1,0:T(8,128)(2,1)}), bf16[4,128,128]{2,1,0:T(8,128)(2,1)S(1)}, u32[]{:S(2)}, u32[]{:S(2)}) async-start(bf16[4,128,128]{2,1,0:T(8,128)(2,1)} %broadcast_in_dim.40), calls=%async_computation | async-start | bytes 262144 | tf_op jit(solution)/shard_map/all_to_all | solution.py:133
  34.5 7.2 %copy-start.4 = (bf16[1,1024,128]{2,1,0:T(8,128)(2,1)S(1)}, bf16[1,1024,128]{2,1,0:T(8,128)(2,1)}, u32[]{:S(2)}) copy-start(bf16[1,1024,128]{2,1,0:T(8,128)(2,1)} %param.9) | copy-start | bytes 786436
  48.3 11.9 %all-to-all-start.1 = ((bf16[4,128,256]{2,1,0:T(8,128)(2,1)}), bf16[4,128,256]{2,1,0:T(8,128)(2,1)S(1)}, u32[]{:S(2)}, u32[]{:S(2)}) async-start(bf16[4,128,256]{2,1,0:T(8,128)(2,1)} %bitcast.16), calls=%async_computation.1 | async-start | bytes 524288 | tf_op jit(solution)/shard_map/all_to_all | solution.py:173
  60.2 15.6 %copy-start.8 = (bf16[128,256]{1,0:T(8,128)(2,1)}, bf16[128,256]{1,0:T(8,128)(2,1)S(1)}, u32[]{:S(2)}) copy-start(bf16[128,256]{1,0:T(8,128)(2,1)S(1)} %reduce_sum.34.mine) | copy-start | bytes 196612
  60.3 15.5 %collective-permute-start.2 = (bf16[128,256]{1,0:T(8,128)(2,1)S(1)}, bf16[128,256]{1,0:T(8,128)(2,1)S(1)}, u32[]{:S(2)}, u32[]{:S(2)}) collective-permute-start(bf16[128,256]{1,0:T(8,128)(2,1)S(1)} %reduce_sum.34.mine), channel_id=1, source_target_pairs={{0,256},{32,288},{64,320},{96,352},{128,384},{160,416},{192,448},{... | collective-permute-start | bytes 196616 | tf_op jit(solution)/shard_map/ppermute | solution.py:178
  68.7 16.3 %all-to-all-start.2 = ((bf16[16,32,256]{2,1,0:T(8,128)(2,1)}), bf16[16,32,256]{2,1,0:T(8,128)(2,1)S(1)}, u32[]{:S(2)}, u32[]{:S(2)}) async-start(bf16[16,32,256]{2,1,0:T(8,128)(2,1)} %bitcast.17), calls=%async_computation.2 | async-start | bytes 524288 | tf_op jit(solution)/shard_map/all_to_all | solution.py:181
  75.8 0.6 copy-start.12
  78.0 17.0 %collective-permute-start.3 = (bf16[128,256]{1,0:T(8,128)(2,1)}, bf16[128,256]{1,0:T(8,128)(2,1)S(1)}, u32[]{:S(2)}, u32[]{:S(2)}) collective-permute-start(bf16[128,256]{1,0:T(8,128)(2,1)} %shard_map.112.mine), channel_id=1, source_target_pairs={{0,1},{1,0},{2,3},{3,2},{4,5},{5,4},{6,7},{7,6},{8,9},{9,8},{10,11... | collective-permute-start | bytes 196616 | tf_op jit(solution)/shard_map/ppermute | solution.py:186
  85.1 0.7 copy-start.6
  87.7 15.7 %all-to-all-start.3 = ((bf16[16,32,256]{2,1,0:T(8,128)(2,1)}), bf16[16,32,256]{2,1,0:T(8,128)(2,1)S(1)}, u32[]{:S(2)}, u32[]{:S(2)}) async-start(bf16[16,32,256]{2,1,0:T(8,128)(2,1)} %get-tuple-element.34), calls=%async_computation.3 | async-start | bytes 524288 | tf_op jit(solution)/shard_map/all_to_all | solution.py:195
  94.9 22.2 %copy-start.2 = (f32[512,1024]{1,0:T(8,128)S(1)}, f32[512,1024]{1,0:T(8,128)}, u32[]{:S(2)}) copy-start(f32[512,1024]{1,0:T(8,128)} %bitcast_add_fusion) | copy-start | bytes 6291460
  94.9 0.6 copy-start.11
  103.4 16.5 %copy-start.5 = (bf16[16,32,256]{2,1,0:T(8,128)(2,1)}, bf16[16,32,256]{2,1,0:T(8,128)(2,1)S(1)}, u32[]{:S(2)}) copy-start(bf16[16,32,256]{2,1,0:T(8,128)(2,1)S(1)} %all-to-all-done.3) | copy-start | bytes 786436
  117.1 22.1 %copy-start.3 = (bf16[8,128,256]{2,1,0:T(8,128)(2,1)}, bf16[8,128,256]{2,1,0:T(8,128)(2,1)S(1)}, u32[]{:S(2)}) copy-start(bf16[8,128,256]{2,1,0:T(8,128)(2,1)S(1)} %all_gather.24.emb) | copy-start | bytes 1572868
  119.9 2.8 %copy-start.14 = (bf16[512,1024]{1,0:T(8,128)(2,1)}, bf16[512,1024]{1,0:T(8,128)(2,1)S(1)}, u32[]{:S(2)}) copy-start(bf16[512,1024]{1,0:T(8,128)(2,1)S(1)} %select_convert_fusion) | copy-start | bytes 3145732
  133.7 12.0 %copy-start.9 = (bf16[128,256]{1,0:T(8,128)(2,1)}, bf16[128,256]{1,0:T(8,128)(2,1)S(1)}, u32[]{:S(2)}) copy-start(bf16[128,256]{1,0:T(8,128)(2,1)S(1)} %reduce_sum.35.mine) | copy-start | bytes 196612
  133.7 11.9 %collective-permute-start.4 = (bf16[128,256]{1,0:T(8,128)(2,1)S(1)}, bf16[128,256]{1,0:T(8,128)(2,1)S(1)}, u32[]{:S(2)}, u32[]{:S(2)}) collective-permute-start(bf16[128,256]{1,0:T(8,128)(2,1)S(1)} %reduce_sum.35.mine), channel_id=1, source_target_pairs={{0,256},{32,288},{64,320},{96,352},{128,384},{160,416},{192,448},{... | collective-permute-start | bytes 196616 | tf_op jit(solution)/shard_map/ppermute | solution.py:178
  141.6 12.2 %all-to-all-start.6 = ((bf16[16,32,256]{2,1,0:T(8,128)(2,1)}), bf16[16,32,256]{2,1,0:T(8,128)(2,1)S(1)}, u32[]{:S(2)}, u32[]{:S(2)}) async-start(bf16[16,32,256]{2,1,0:T(8,128)(2,1)} %bitcast.26), calls=%async_computation.6 | async-start | bytes 524288 | tf_op jit(solution)/shard_map/all_to_all | solution.py:181
  145.7 0.6 copy-start.13
  153.7 0.7 copy-start.7
  156.3 18.6 %collective-permute-start.5 = (bf16[160,256]{1,0:T(8,128)(2,1)}, bf16[160,256]{1,0:T(8,128)(2,1)S(1)}, u32[]{:S(2)}, u32[]{:S(2)}) collective-permute-start(bf16[160,256]{1,0:T(8,128)(2,1)} %get-tuple-element.43), channel_id=1, source_target_pairs={{0,1},{1,0},{2,3},{3,2},{4,5},{5,4},{6,7},{7,6},{8,9},{9,8},{10,11... | collective-permute-start | bytes 245768 | tf_op jit(solution)/shard_map/ppermute | solution.py:218
  174.8 0.6 copy-start.10
  187.9 13.4 %all-to-all-start.8 = ((bf16[16,32,384]{2,1,0:T(8,128)(2,1)}), bf16[16,32,384]{2,1,0:T(8,128)(2,1)S(1)}, u32[]{:S(2)}, u32[]{:S(2)}) async-start(bf16[16,32,384]{2,1,0:T(8,128)(2,1)} %get-tuple-element.48), calls=%async_computation.8 | async-start | bytes 786432 | tf_op jit(solution)/shard_map/all_to_all | solution.py:229

commit v3 on v2

v3 whole, which is shorter than its diff:
```python
import jax
import jax.numpy as jnp
from jax import lax
from jax.experimental import pallas as pl
from jax.experimental.pallas import tpu as pltpu
from jax.sharding import PartitionSpec as P

STEPS = 2
LEARN_RATE = 0.1
SIDE = 1024
HALF_ROWS = 512
WIDTH = 256
HALF_D = 128
N_COL = 16
ROW_PART = HALF_ROWS // N_COL
COL_PART = 128
ROW_PAIR = 256
TILE_ROWS = 256

C_SHARE, C_PAIR, C_ROW, C_COL, C_ROW_LAST, C_COL_LAST, C_PACK = 20, 20, 1, 20, 1, 20, 20

CORE_PAIRS = [[2 * z, 2 * z + 1] for z in range(8)]
Z_QUADS = [[2 * (4 * h + k) + core for k in range(4)] for h in range(2) for core in range(2)]
FAR_Z = [(i, i ^ 8) for i in range(16)]
Y_SWAP = [(i, i ^ 1) for i in range(16)]
DIM_SWAP = [(0, 1), (1, 0)]

AT_DIM, AT_COL, AT_CORE, AT_COL_PART, AT_Y, AT_LIVE = range(6)


def to_f32(block):
    return block.astype(jnp.float32)


def swap_halves(block):
    return jnp.concatenate([block[:, HALF_D:], block[:, :HALF_D]], axis=1)


def diagonal(n):
    return lax.broadcasted_iota(jnp.int32, (n, n), 0) == lax.broadcasted_iota(jnp.int32, (n, n), 1)


def column(acc):
    if acc.shape[0] > 1:
        return acc
    return jnp.sum(jnp.where(diagonal(acc.shape[1]), acc, 0.0), axis=1, keepdims=True)


def line(acc):
    return jnp.sum(jnp.where(diagonal(acc.shape[0]), acc, 0.0), axis=0, keepdims=True)


def adagrad(total, acc, emb):
    squares = total * total
    square = jnp.sum(squares[:, :HALF_D] + squares[:, HALF_D:], axis=1, keepdims=True)
    acc = acc + square / WIDTH
    emb = to_f32(emb) - LEARN_RATE * total / jnp.sqrt(acc)
    return emb.astype(jnp.bfloat16), acc


def acc_lanes(acc, start, width):
    high = to_f32(acc.astype(jnp.bfloat16))
    lane = lax.broadcasted_iota(jnp.int32, (acc.shape[0], HALF_D), 1) - start
    part = jnp.where(lane < width, high, acc - high)
    return jnp.where((lane >= 0) & (lane < 2 * width), part, 0.0).astype(jnp.bfloat16)


def block_at(ref, index, size):
    return ref[pl.ds(pl.multiple_of(index * size, size), size), :]


def share_kernel(at, got, out):
    out[...] = jnp.broadcast_to(got[:COL_PART, :][None], out.shape)


def tile_terms(at, rows, cols, weight, target, kept, given, row_term, col_sum):
    cols_all = cols[...]
    for part in range(HALF_ROWS // TILE_ROWS):
        here = slice(part * TILE_ROWS, (part + 1) * TILE_ROWS)
        rows_here = rows[here, :]
        scores = lax.dot_general(
            rows_here, cols_all, (((1,), (1,)), ((), ())), preferred_element_type=jnp.float32
        )
        gap = scores - target[here, :]
        scale = weight[here, :]
        sigmoid = (0.5 / SIDE) * jnp.tanh(0.5 * gap) + 0.5 / SIDE
        cell = jnp.where(scale > 0, scale * gap, sigmoid)
        row = lax.broadcasted_iota(jnp.int32, cell.shape, 0) + part * TILE_ROWS
        grad = jnp.where(row < at[AT_LIVE], cell, 0.0).astype(jnp.bfloat16)
        row_term[here, :] = jnp.dot(grad, cols_all, preferred_element_type=jnp.float32).astype(jnp.bfloat16)
        term = lax.dot_general(
            grad, rows_here, (((0,), (0,)), ((), ())), preferred_element_type=jnp.float32
        )
        if part == 0:
            col_sum[...] = term
        else:
            col_sum[...] += term
    core = at[AT_CORE]
    kept[...] = block_at(col_sum, core, HALF_ROWS).astype(jnp.bfloat16)
    given[...] = block_at(col_sum, 1 - core, HALF_ROWS).astype(jnp.bfloat16)


def first_tile_kernel(
    at, row_emb, got, there, col_emb, col_other, weight, target, kept, given, row_term, rows, cols, col_sum
):
    side, y = at[AT_DIM], at[AT_Y]
    rows[:, :HALF_D] = block_at(row_emb, side, HALF_ROWS)
    rows[pl.ds(pl.multiple_of(y * ROW_PAIR, ROW_PAIR), ROW_PAIR), HALF_D:] = got[COL_PART:, :]
    rows[pl.ds(pl.multiple_of((1 - y) * ROW_PAIR, ROW_PAIR), ROW_PAIR), HALF_D:] = there[...]
    cols[:, :HALF_D] = col_emb[...]
    cols[:, HALF_D:] = col_other[...]
    tile_terms(at, rows, cols, weight, target, kept, given, row_term, col_sum)


def same_kernel(at, block, out):
    out[...] = block[...]


def half_kernel(at, kept, pair, half):
    theirs = pair[pl.ds(1 - at[AT_CORE], 1), :, :][0]
    half[...] = (to_f32(kept[...]) + to_f32(theirs)).astype(jnp.bfloat16).reshape(half.shape)


def near_kernel(at, parts, near):
    near[...] = jnp.sum(to_f32(parts[...]), axis=0).astype(jnp.bfloat16)


def pair_kernel(at, mine, theirs, both):
    both[...] = (to_f32(mine[...]) + to_f32(theirs[...])).astype(jnp.bfloat16)


def row_kernel(at, parts, acc, rows, emb_out, acc_out):
    total = jnp.sum(to_f32(parts[...]), axis=0)
    emb_new, acc_out[...] = adagrad(total, column(acc[...]), block_at(rows, at[AT_COL], ROW_PART))
    emb_out[...] = jnp.broadcast_to(emb_new[None], emb_out.shape)


def row_last_kernel(at, parts, acc, rows, kept, sent):
    total = jnp.sum(to_f32(parts[...]), axis=0)
    emb_new, acc_new = adagrad(total, acc[...], block_at(rows, at[AT_COL], ROW_PART))
    kept[:, :HALF_D] = emb_new[:, :HALF_D]
    kept[:, HALF_D:] = acc_lanes(acc_new, 0, 32)
    sent[:, :HALF_D] = emb_new[:, HALF_D:]
    sent[:, HALF_D:] = acc_lanes(acc_new, 64, 32)


def col_kernel(at, mine, theirs, acc, cols, emb_out, acc_out):
    total = to_f32(mine[...]) + swap_halves(to_f32(theirs[...]))
    emb_new, acc_out[...] = adagrad(total, column(acc[...]), block_at(cols, at[AT_COL_PART], COL_PART))
    emb_out[...] = jnp.broadcast_to(emb_new[None], emb_out.shape)


def col_last_kernel(at, mine, theirs, acc, cols, col_out):
    total = to_f32(mine[...]) + swap_halves(to_f32(theirs[...]))
    emb_new, acc_new = adagrad(total, acc[...], block_at(cols, at[AT_COL_PART], COL_PART))
    col_new = jnp.concatenate([emb_new[:, :HALF_D], acc_lanes(acc_new, 0, 64)], axis=1)
    col_out[...] = jnp.broadcast_to(col_new[None], col_out.shape)


def pack_kernel(at, kept, theirs, row_out):
    here, there = kept[...], theirs[...]
    both = (to_f32(here[:, HALF_D:]) + to_f32(there[:, HALF_D:])).astype(jnp.bfloat16)
    row_new = jnp.concatenate([here[:, :HALF_D], there[:, :HALF_D], both], axis=1)
    row_out[...] = jnp.broadcast_to(row_new[None], row_out.shape)


def out_kernel(at, rows, cols, row_out, row_acc_out, col_out, col_acc_out):
    side = at[AT_DIM]
    for half, first in ((side, 0), (1 - side, HALF_D)):
        start = pl.multiple_of(half * HALF_ROWS, HALF_ROWS)
        row_out[0, pl.ds(start, HALF_ROWS), :] = rows[:, first : first + HALF_D]
        lane = WIDTH + first // 2
        acc = to_f32(rows[:, lane : lane + 1]) + to_f32(rows[:, lane + 32 : lane + 33])
        for k in range(HALF_ROWS // HALF_D):
            part = line(acc[k * HALF_D : (k + 1) * HALF_D])
            row_acc_out[:, pl.ds(pl.multiple_of(start + k * HALF_D, HALF_D), HALF_D)] = part
    col_out[0] = cols[:, :HALF_D]
    acc = to_f32(cols[:, HALF_D : HALF_D + 1]) + to_f32(cols[:, HALF_D + 64 : HALF_D + 65])
    for k in range(SIDE // HALF_D):
        part = slice(k * HALF_D, (k + 1) * HALF_D)
        col_acc_out[:, part] = line(acc[part])


def on_device(kernel, at, operands, shapes, micros, vmem_mib=4, scratch=()):
    vmem = pl.BlockSpec(memory_space=pltpu.VMEM)
    return pl.pallas_call(
        kernel,
        in_specs=[pl.BlockSpec(memory_space=pltpu.SMEM)] + [vmem] * len(operands),
        out_specs=[vmem] * len(shapes),
        out_shape=shapes,
        scratch_shapes=scratch,
        cost_estimate=pl.CostEstimate(flops=micros * 10**9, bytes_accessed=1 << 18, transcendentals=0),
        compiler_params=pltpu.CompilerParams(vmem_limit_bytes=vmem_mib << 20),
    )(at, *operands)


def bf16(*shape):
    return jax.ShapeDtypeStruct(shape, jnp.bfloat16)


def f32(*shape):
    return jax.ShapeDtypeStruct(shape, jnp.float32)


def shards(row_emb, col_emb, row_acc, col_acc, counts, live_rows, row_marg, col_marg):
    d, r, c = (lax.axis_index(a) for a in ("dim", "row", "col"))
    core, quad, y = r % 2, (r // 2) % 4, c % 2
    row_emb, col_emb = row_emb[0], col_emb[0]
    col_part = core * 4 + quad
    live_here = live_rows[0, 0] - d * HALF_ROWS
    at = jnp.stack([d, c, core, col_part, y, live_here]).astype(jnp.int32)

    def rows_at(block, start, size):
        return lax.dynamic_slice_in_dim(block, start, size, 0)

    sent = jnp.concatenate(
        [
            rows_at(col_emb, col_part * COL_PART, COL_PART),
            rows_at(row_emb, (1 - d) * HALF_ROWS + y * ROW_PAIR, ROW_PAIR),
        ]
    )
    got = lax.ppermute(sent, "dim", DIM_SWAP)

    log_total = jnp.log(jnp.sum(row_marg).astype(jnp.float32))
    own_marg = lax.dynamic_index_in_dim(row_marg, r, 0, False)
    row_logs = jnp.log(rows_at(own_marg, d * HALF_ROWS, HALF_ROWS).astype(jnp.float32))
    col_logs = jnp.log(lax.dynamic_index_in_dim(col_marg, c, 0, False).astype(jnp.float32))
    shift_log = log_total - row_logs[:, None] - col_logs[None, :]
    tile = counts[0, 0]
    count_f = tile.astype(jnp.float32)
    weight = jnp.where(tile > 0, (0.1 + 0.25 * jnp.sqrt(count_f)) / SIDE, 0.0)
    target = jnp.log(jnp.maximum(count_f, 1.0)) + shift_log
    row_acc = rows_at(row_acc[0], d * HALF_ROWS + c * ROW_PART, ROW_PART)[None]
    col_acc = rows_at(col_acc[0], col_part * COL_PART, COL_PART)[None]

    there = lax.ppermute(got[COL_PART:], "col", Y_SWAP)
    (shared,) = on_device(share_kernel, at, (got,), (bf16(4, COL_PART, HALF_D),), 1)
    col_other = lax.all_to_all(shared, "row", 0, 0, axis_index_groups=Z_QUADS)
    (there,) = on_device(
        same_kernel, at, (there,), (bf16(ROW_PAIR, HALF_D),), C_SHARE
    )
    there, col_other = lax.optimization_barrier((there, col_other))
    col_other = lax.all_gather(col_other, "row", tiled=True, axis_index_groups=CORE_PAIRS)
    col_other = col_other.reshape(SIDE, HALF_D)
    weight, target, row_acc, col_acc = lax.optimization_barrier((weight, target, row_acc, col_acc))

    terms = (bf16(HALF_ROWS, WIDTH), bf16(HALF_ROWS, WIDTH), bf16(HALF_ROWS, WIDTH))
    for step in range(STEPS):
        last = step == STEPS - 1
        if step == 0:
            kept, given, row_term, rows, cols = on_device(
                first_tile_kernel,
                at,
                (row_emb, got, there, col_emb, col_other, weight, target),
                terms + (bf16(HALF_ROWS, WIDTH), bf16(SIDE, WIDTH)),
                3,
                24,
                [pltpu.VMEM((SIDE, WIDTH), jnp.float32)],
            )
        else:
            kept, given, row_term = on_device(
                tile_terms,
                at,
                (rows, cols, weight, target),
                terms,
                3,
                24,
                [pltpu.VMEM((SIDE, WIDTH), jnp.float32)],
            )

        pair = lax.all_gather(given, "row", axis_index_groups=CORE_PAIRS)
        (half,) = on_device(half_kernel, at, (kept, pair), (bf16(4, COL_PART, WIDTH),), 1)
        parts = lax.all_to_all(half, "row", 0, 0, axis_index_groups=Z_QUADS)
        (near,) = on_device(near_kernel, at, (parts,), (bf16(COL_PART, WIDTH),), 1)
        row_term, near = lax.optimization_barrier((row_term, near))
        far = lax.ppermute(near, "row", FAR_Z)

        row_parts = lax.all_to_all(row_term.reshape(N_COL, ROW_PART, WIDTH), "col", 0, 0)
        (near,) = on_device(pair_kernel, at, (near, far), (bf16(COL_PART, WIDTH),), C_PAIR)
        far = lax.ppermute(near, "dim", DIM_SWAP)
        if not last:
            rows, row_acc = on_device(
                row_kernel,
                at,
                (row_parts, row_acc, rows),
                (bf16(N_COL, ROW_PART, WIDTH), f32(ROW_PART, 1)),
                C_ROW,
            )
            rows = lax.all_to_all(rows, "col", 0, 0).reshape(HALF_ROWS, WIDTH)
            cols, col_acc = on_device(
                col_kernel,
                at,
                (near, far, col_acc, cols),
                (bf16(4, COL_PART, WIDTH), f32(COL_PART, 1)),
                C_COL,
            )
            rows, cols = lax.optimization_barrier((rows, cols))
            cols = lax.all_to_all(cols, "row", 0, 0, axis_index_groups=Z_QUADS)
            cols = lax.all_gather(cols, "row", tiled=True, axis_index_groups=CORE_PAIRS)
            cols = cols.reshape(SIDE, WIDTH)
            continue

        kept, sent = on_device(
            row_last_kernel,
            at,
            (row_parts, row_acc, rows),
            (bf16(ROW_PART, WIDTH), bf16(ROW_PART, WIDTH)),
            C_ROW_LAST,
        )
        rows_far = lax.ppermute(sent, "dim", DIM_SWAP)
        (cols,) = on_device(
            col_last_kernel, at, (near, far, col_acc, cols), (bf16(4, COL_PART, WIDTH),), C_COL_LAST
        )
        cols = lax.all_to_all(cols, "row", 0, 0, axis_index_groups=Z_QUADS)
        (rows,) = on_device(
            pack_kernel, at, (kept, rows_far), (bf16(N_COL, ROW_PART, WIDTH + HALF_D),), C_PACK
        )
        rows, cols = lax.optimization_barrier((rows, cols))
        rows = lax.all_to_all(rows, "col", 0, 0)
        cols = lax.all_gather(cols, "row", tiled=True, axis_index_groups=CORE_PAIRS)
        rows, cols = lax.optimization_barrier((rows, cols))

    rows = rows.reshape(HALF_ROWS, WIDTH + HALF_D)
    cols = cols.reshape(SIDE, WIDTH)
    return on_device(
        out_kernel,
        at,
        (rows, cols),
        (bf16(1, SIDE, HALF_D), f32(1, SIDE), bf16(1, SIDE, HALF_D), f32(1, SIDE)),
        1,
    )


def solution(mesh):
    return jax.shard_map(
        shards,
        mesh=mesh,
        in_specs=(
            P("row", None, "dim"),
            P("col", None, "dim"),
            P("row", None),
            P("col", None),
            P("row", "col", "dim", None),
            P("row", "col"),
            P(),
            P(),
        ),
        out_specs=(P("row", None, "dim"), P("row", None), P("col", None, "dim"), P("col", None)),
        check_vma=False,
    )
```

time: 207 us -> 192 us (0.928)
  the two profiles are of different devices: /device:TPU:32 before, /device:TPU:8 now
where the time goes in v3:
time: 192 us; the launch traced here: 191 us
  starting transfers between devices  86.2 us (45%)
  blocking collectives  43.9 us (23%)
  waiting for transfers between devices  23.6 us (12%)
  Pallas kernels  18.3 us (10%)
  other arithmetic  9.65 us (5%)
  local copies, waits for them, and re-layouts  6.68 us (3%)
  between operations  2.35 us (1%)
    all_to_all x2, blocking collectives, shards(): parts = lax.all_to_all(half, 'row', 0, 0, axis_index_groups=Z_QUADS)  23.7 us
    pallas_call x16, Pallas kernels, on_device(): pl.pallas_call(kernel, in_specs=[pl.BlockSpec(memory_space=pltpu.SMEM)] +...  18.3 us
    ppermute x1, starting transfers between devices, shards(): got = lax.ppermute(sent, 'dim', DIM_SWAP)  15.7 us
    ppermute x2, starting transfers between devices, shards(): far = lax.ppermute(near, 'dim', DIM_SWAP)  15.3 us
    all_to_all x2, starting transfers between devices, shards(): lax.all_to_all(row_term.reshape(N_COL, ROW_PART, WIDTH), 'col', 0, 0)  13.4 us
    ppermute x2, starting transfers between devices, shards(): far = lax.ppermute(near, 'row', FAR_Z)  10.7 us
    all_to_all x1, blocking collectives, shards(): cols = lax.all_to_all(cols, 'row', 0, 0, axis_index_groups=Z_QUADS)  9.5 us
    ppermute x1, starting transfers between devices, shards(): rows_far = lax.ppermute(sent, 'dim', DIM_SWAP)  8.22 us
  transfers between devices with their start and end apart: 13, of which 6 were waited for; matrix products, arithmetic and copies ran while one was open for 5% of the time, Pallas kernels for 4%

profile of v3, /device:TPU:8, one launch (start us, length us, event | category | flops | bytes accessed | tf_op | source)
XLA Modules:
  0.0 190.7 jit_solution(914542763283446739)
XLA Ops:
  2.3 15.7 %collective-permute-start = (bf16[384,128]{1,0:T(8,128)(2,1)S(1)}, bf16[384,128]{1,0:T(8,128)(2,1)S(1)}, u32[]{:S(2)}, u32[]{:S(2)}) collective-permute-start(bf16[384,128]{1,0:T(8,128)(2,1)S(1)} %pad_maximum_fusion), channel_id=1, source_target_pairs={{0,1},{1,0},{2,3},{3,2},{4,5},{5,4},{6,7},{7,6},{8,9},{9,8},{10,11... | collective-permute-start | bytes 294920 | tf_op jit(solution)/shard_map/ppermute | solution.py:222
  21.1 3.1 %select_bitcast_fusion.weight = f32[512,1024]{1,0:T(8,128)S(1)} fusion(s32[1,1,512,1024]{3,2,1,0:T(8,128)} %param.12), kind=kLoop, calls=%fused_computation.1 | loop fusion | flops 3145728 | bytes 4194304 | tf_op jit(solution)/shard_map/jit(_where)/select_n | solution.py:231
  25.8 3.4 %bitcast_add_fusion.target = f32[512,1024]{1,0:T(8,128)} fusion(s32[1,1,512,1024]{3,2,1,0:T(8,128)} %param.12, f32[1024]{0:T(1024)S(1)} %bitcast.40, f32[512]{0:T(512)S(1)} %bitcast.41), kind=kLoop, calls=%fused_computation | loop fusion | flops 2097152 | bytes 4200448 | tf_op jit(solution)/shard_map/add | solution.py:232
  30.0 2.4 %collective-permute-start.1 = (bf16[256,128]{1,0:T(8,128)(2,1)S(1)}, bf16[256,128]{1,0:T(8,128)(2,1)S(1)}, u32[]{:S(2)}, u32[]{:S(2)}) collective-permute-start(bf16[256,128]{1,0:T(8,128)(2,1)S(1)} %slice.4), channel_id=1, source_target_pairs={{0,2},{2,0},{4,6},{6,4},{8,10},{10,8},{12,14},{14,12},{16,18},{18,... | collective-permute-start | bytes 196616 | tf_op jit(solution)/shard_map/ppermute | solution.py:236
  33.5 3.3 %all-to-all-start = ((bf16[4,128,128]{2,1,0:T(8,128)(2,1)}), bf16[4,128,128]{2,1,0:T(8,128)(2,1)S(1)}, u32[]{:S(2)}, u32[]{:S(2)}) async-start(bf16[4,128,128]{2,1,0:T(8,128)(2,1)} %shard_map.112), calls=%async_computation | async-start | bytes 262144 | tf_op jit(solution)/shard_map/all_to_all | solution.py:238
  37.5 5.4 %all-to-all-done = bf16[4,128,128]{2,1,0:T(8,128)(2,1)S(1)} async-done(((bf16[4,128,128]{2,1,0:T(8,128)(2,1)}), bf16[4,128,128]{2,1,0:T(8,128)(2,1)S(1)}, u32[]{:S(2)}, u32[]{:S(2)}) %all-to-all-start) | async-done | bytes 131104 | tf_op jit(solution)/shard_map/all_to_all | solution.py:238
  42.8 2.0 %all_gather.21 = bf16[8,128,128]{2,1,0:T(8,128)(2,1)S(1)} all-gather(bf16[4,128,128]{2,1,0:T(8,128)(2,1)S(1)} %all-to-all-done), channel_id=1, replica_groups={{0,32},{64,96},{128,160},{192,224},{256,288},{320,352},{384,416},{448,4..., dimensions={0}, use_global_device_ids=true | all-gather | bytes 393216 | tf_op jit(solution)/shard_map/all_gather | solution.py:243
  44.8 1.6 copy-done.1
  46.4 2.7 %shard_map.113 = (bf16[512,256]{1,0:T(8,128)(2,1)S(1)}, bf16[512,256]{1,0:T(8,128)(2,1)S(1)}, bf16[512,256]{1,0:T(8,128)(2,1)}, bf16[512,256]{1,0:T(8,128)(2,1)S(1)}, bf16[1024,256]{1,0:T(8,128)(2,1)S(1)}) custom-call(s32[6]{0:T(128)S(1)} %stack.27.at, bf16[1024,128]{1,0:T(8,128)(2,1)S(1)} %bitcast.38, bf16[384,128]{1,0:T(8,128)(2,1)S(1)} %collective-permute-done.got, ...), custom_call_target="tpu_custom_call" | custom-call | flops 3000000000 | bytes 262144 | tf_op jit(solution)/shard_map/pallas_call | solution.py:186
  49.1 2.2 %all-gather = bf16[1024,256]{1,0:T(8,128)(2,1)S(1)} all-gather(bf16[512,256]{1,0:T(8,128)(2,1)S(1)} %get-tuple-element.40), channel_id=2, replica_groups={{0,32},{64,96},{128,160},{192,224},{256,288},{320,352},{384,416},{448,4..., dimensions={0}, use_global_device_ids=true | all-gather | bytes 786432 | tf_op jit(solution)/shard_map/all_gather | solution.py:271
  51.9 11.9 %all_to_all.45.parts = bf16[4,128,256]{2,1,0:T(8,128)(2,1)S(1)} all-to-all(bf16[4,128,256]{2,1,0:T(8,128)(2,1)S(1)} %shard_map.114), channel_id=1, replica_groups={{0,64,128,192},{32,96,160,224},{256,320,384,448},{288,352,416,480},{1,6..., dimensions={0} | all-to-all | bytes 524288 | tf_op jit(solution)/shard_map/all_to_all | solution.py:273
  64.4 4.3 %collective-permute-start.2 = (bf16[128,256]{1,0:T(8,128)(2,1)S(1)}, bf16[128,256]{1,0:T(8,128)(2,1)S(1)}, u32[]{:S(2)}, u32[]{:S(2)}) collective-permute-start(bf16[128,256]{1,0:T(8,128)(2,1)S(1)} %shard_map.115.mine), channel_id=1, source_target_pairs={{0,256},{32,288},{64,320},{96,352},{128,384},{160,416},{192,448},{... | collective-permute-start | bytes 196616 | tf_op jit(solution)/shard_map/ppermute | solution.py:276
  68.7 8.2 %all-to-all-start.2 = ((bf16[16,32,256]{2,1,0:T(8,128)(2,1)}), bf16[16,32,256]{2,1,0:T(8,128)(2,1)S(1)}, u32[]{:S(2)}, u32[]{:S(2)}) async-start(bf16[16,32,256]{2,1,0:T(8,128)(2,1)} %bitcast.17), calls=%async_computation.2 | async-start | bytes 524288 | tf_op jit(solution)/shard_map/all_to_all | solution.py:278
  77.5 8.9 %collective-permute-start.3 = (bf16[128,256]{1,0:T(8,128)(2,1)S(1)}, bf16[128,256]{1,0:T(8,128)(2,1)S(1)}, u32[]{:S(2)}, u32[]{:S(2)}) collective-permute-start(bf16[128,256]{1,0:T(8,128)(2,1)S(1)} %shard_map.117.mine), channel_id=1, source_target_pairs={{0,1},{1,0},{2,3},{3,2},{4,5},{5,4},{6,7},{7,6},{8,9},{9,8},{10,11... | collective-permute-start | bytes 196616 | tf_op jit(solution)/shard_map/ppermute | solution.py:280
  87.8 7.5 %all-to-all-start.3 = ((bf16[16,32,256]{2,1,0:T(8,128)(2,1)}), bf16[16,32,256]{2,1,0:T(8,128)(2,1)S(1)}, u32[]{:S(2)}, u32[]{:S(2)}) async-start(bf16[16,32,256]{2,1,0:T(8,128)(2,1)} %get-tuple-element.44), calls=%async_computation.3 | async-start | bytes 524288 | tf_op jit(solution)/shard_map/all_to_all | solution.py:289
  97.0 5.2 %all-to-all-done.3 = bf16[16,32,256]{2,1,0:T(8,128)(2,1)S(1)} async-done(((bf16[16,32,256]{2,1,0:T(8,128)(2,1)}), bf16[16,32,256]{2,1,0:T(8,128)(2,1)S(1)}, u32[]{:S(2)}, u32[]{:S(2)}) %all-to-all-start.3) | async-done | bytes 262176 | tf_op jit(solution)/shard_map/all_to_all | solution.py:289
  102.3 9.5 %all_to_all.46 = bf16[4,128,256]{2,1,0:T(8,128)(2,1)S(1)} all-to-all(bf16[4,128,256]{2,1,0:T(8,128)(2,1)S(1)} %get-tuple-element.50), channel_id=1, replica_groups={{0,64,128,192},{32,96,160,224},{256,320,384,448},{288,352,416,480},{1,6..., dimensions={0} | all-to-all | bytes 524288 | tf_op jit(solution)/shard_map/all_to_all | solution.py:298
  111.8 2.2 %all_gather.24 = bf16[8,128,256]{2,1,0:T(8,128)(2,1)S(1)} all-gather(bf16[4,128,256]{2,1,0:T(8,128)(2,1)S(1)} %all_to_all.46), channel_id=1, replica_groups={{0,32},{64,96},{128,160},{192,224},{256,288},{320,352},{384,416},{448,4..., dimensions={0}, use_global_device_ids=true | all-gather | bytes 786432 | tf_op jit(solution)/shard_map/all_gather | solution.py:299
  113.9 1.6 copy-done.2
  115.5 2.7 %shard_map.119 = (bf16[512,256]{1,0:T(8,128)(2,1)S(1)}, bf16[512,256]{1,0:T(8,128)(2,1)S(1)}, bf16[512,256]{1,0:T(8,128)(2,1)}) custom-call(s32[6]{0:T(128)S(1)} %stack.27.at, bf16[512,256]{1,0:T(8,128)(2,1)S(1)} %bitcast.36, bf16[1024,256]{1,0:T(8,128)(2,1)S(1)} %bitcast.29, f32[512,1024]{1,0:T(8,128)S(1)} %select_bitcast_fusion.weight, ...), custom_call_target="tpu_custom_call" | custom-call | flops 3000000000 | bytes 262144 | tf_op jit(solution)/shard_map/pallas_call | solution.py:186
  118.3 2.2 %all-gather.1 = bf16[1024,256]{1,0:T(8,128)(2,1)S(1)} all-gather(bf16[512,256]{1,0:T(8,128)(2,1)S(1)} %get-tuple-element.53), channel_id=3, replica_groups={{0,32},{64,96},{128,160},{192,224},{256,288},{320,352},{384,416},{448,4..., dimensions={0}, use_global_device_ids=true | all-gather | bytes 786432 | tf_op jit(solution)/shard_map/all_gather | solution.py:271
  121.0 11.9 %all_to_all.47.parts = bf16[4,128,256]{2,1,0:T(8,128)(2,1)S(1)} all-to-all(bf16[4,128,256]{2,1,0:T(8,128)(2,1)S(1)} %shard_map.120), channel_id=1, replica_groups={{0,64,128,192},{32,96,160,224},{256,320,384,448},{288,352,416,480},{1,6..., dimensions={0} | all-to-all | bytes 524288 | tf_op jit(solution)/shard_map/all_to_all | solution.py:273
  133.5 6.4 %collective-permute-start.5 = (bf16[128,256]{1,0:T(8,128)(2,1)S(1)}, bf16[128,256]{1,0:T(8,128)(2,1)S(1)}, u32[]{:S(2)}, u32[]{:S(2)}) collective-permute-start(bf16[128,256]{1,0:T(8,128)(2,1)S(1)} %shard_map.121.mine), channel_id=1, source_target_pairs={{0,256},{32,288},{64,320},{96,352},{128,384},{160,416},{192,448},{... | collective-permute-start | bytes 196616 | tf_op jit(solution)/shard_map/ppermute | solution.py:276
  139.9 5.2 %all-to-all-start.6 = ((bf16[16,32,256]{2,1,0:T(8,128)(2,1)}), bf16[16,32,256]{2,1,0:T(8,128)(2,1)S(1)}, u32[]{:S(2)}, u32[]{:S(2)}) async-start(bf16[16,32,256]{2,1,0:T(8,128)(2,1)} %bitcast.21), calls=%async_computation.6 | async-start | bytes 524288 | tf_op jit(solution)/shard_map/all_to_all | solution.py:278
  146.2 6.3 %collective-permute-start.6 = (bf16[128,256]{1,0:T(8,128)(2,1)S(1)}, bf16[128,256]{1,0:T(8,128)(2,1)S(1)}, u32[]{:S(2)}, u32[]{:S(2)}) collective-permute-start(bf16[128,256]{1,0:T(8,128)(2,1)S(1)} %shard_map.124.mine), channel_id=1, source_target_pairs={{0,1},{1,0},{2,3},{3,2},{4,5},{5,4},{6,7},{7,6},{8,9},{9,8},{10,11... | collective-permute-start | bytes 196616 | tf_op jit(solution)/shard_map/ppermute | solution.py:280
  153.4 8.2 %collective-permute-start.4 = (bf16[32,256]{1,0:T(8,128)(2,1)S(1)}, bf16[32,256]{1,0:T(8,128)(2,1)S(1)}, u32[]{:S(2)}, u32[]{:S(2)}) collective-permute-start(bf16[32,256]{1,0:T(8,128)(2,1)S(1)} %get-tuple-element.57), channel_id=1, source_target_pairs={{0,1},{1,0},{2,3},{3,2},{4,5},{5,4},{6,7},{7,6},{8,9},{9,8},{10,11... | collective-permute-start | bytes 49160 | tf_op jit(solution)/shard_map/ppermute | solution.py:310
  164.7 3.4 %all-to-all-start.7 = ((bf16[4,128,256]{2,1,0:T(8,128)(2,1)}), bf16[4,128,256]{2,1,0:T(8,128)(2,1)S(1)}, u32[]{:S(2)}, u32[]{:S(2)}) async-start(bf16[4,128,256]{2,1,0:T(8,128)(2,1)} %shard_map.125), calls=%async_computation.7 | async-start | bytes 524288 | tf_op jit(solution)/shard_map/all_to_all | solution.py:314
  169.4 5.4 %all-to-all-done.7 = bf16[4,128,256]{2,1,0:T(8,128)(2,1)S(1)} async-done(((bf16[4,128,256]{2,1,0:T(8,128)(2,1)}), bf16[4,128,256]{2,1,0:T(8,128)(2,1)S(1)}, u32[]{:S(2)}, u32[]{:S(2)}) %all-to-all-start.7) | async-done | bytes 262176 | tf_op jit(solution)/shard_map/all_to_all | solution.py:314
  174.8 6.4 %all-to-all-start.8 = ((bf16[16,32,384]{2,1,0:T(8,128)(2,1)}), bf16[16,32,384]{2,1,0:T(8,128)(2,1)S(1)}, u32[]{:S(2)}, u32[]{:S(2)}) async-start(bf16[16,32,384]{2,1,0:T(8,128)(2,1)} %shard_map.123), calls=%async_computation.8 | async-start | bytes 786432 | tf_op jit(solution)/shard_map/all_to_all | solution.py:319
  181.2 2.2 %all_gather.27 = bf16[8,128,256]{2,1,0:T(8,128)(2,1)S(1)} all-gather(bf16[4,128,256]{2,1,0:T(8,128)(2,1)S(1)} %all-to-all-done.7), channel_id=1, replica_groups={{0,32},{64,96},{128,160},{192,224},{256,288},{320,352},{384,416},{448,4..., dimensions={0}, use_global_device_ids=true | all-gather | bytes 786432 | tf_op jit(solution)/shard_map/all_gather | solution.py:320
  183.4 5.4 %all-to-all-done.8 = bf16[16,32,384]{2,1,0:T(8,128)(2,1)S(1)} async-done(((bf16[16,32,384]{2,1,0:T(8,128)(2,1)}), bf16[16,32,384]{2,1,0:T(8,128)(2,1)S(1)}, u32[]{:S(2)}, u32[]{:S(2)}) %all-to-all-start.8) | async-done | bytes 393248 | tf_op jit(solution)/shard_map/all_to_all | solution.py:319
  188.8 1.9 %shard_map.126 = (bf16[1,1024,128]{2,1,0:T(8,128)(2,1)}, f32[1,1024]{1,0:T(1,128)}, bf16[1,1024,128]{2,1,0:T(8,128)(2,1)}, f32[1,1024]{1,0:T(1,128)}) custom-call(s32[6]{0:T(128)S(1)} %stack.27.at, bf16[512,384]{1,0:T(8,128)(2,1)S(1)} %bitcast.34, bf16[1024,256]{1,0:T(8,128)(2,1)S(1)} %bitcast.31), custom_call_target="tpu_custom_call" | custom-call | flops 1000000000 | bytes 262144 | tf_op jit(solution)/shard_map/pallas_call | solution.py:186
  (44 shorter events, 19.8 us)
Async XLA Ops:
  0.6 20.4 %copy-start = (f32[1,1024]{1,0:T(1,128)S(1)}, f32[1,1024]{1,0:T(1,128)}, u32[]{:S(2)}) copy-start(f32[1,1024]{1,0:T(1,128)} %param.11) | copy-start | bytes 12292
  2.3 27.6 %collective-permute-start = (bf16[384,128]{1,0:T(8,128)(2,1)S(1)}, bf16[384,128]{1,0:T(8,128)(2,1)S(1)}, u32[]{:S(2)}, u32[]{:S(2)}) collective-permute-start(bf16[384,128]{1,0:T(8,128)(2,1)S(1)} %pad_maximum_fusion), channel_id=1, source_target_pairs={{0,1},{1,0},{2,3},{3,2},{4,5},{5,4},{6,7},{7,6},{8,9},{9,8},{10,11... | collective-permute-start | bytes 294920 | tf_op jit(solution)/shard_map/ppermute | solution.py:222
  30.0 6.9 %collective-permute-start.1 = (bf16[256,128]{1,0:T(8,128)(2,1)S(1)}, bf16[256,128]{1,0:T(8,128)(2,1)S(1)}, u32[]{:S(2)}, u32[]{:S(2)}) collective-permute-start(bf16[256,128]{1,0:T(8,128)(2,1)S(1)} %slice.4), channel_id=1, source_target_pairs={{0,2},{2,0},{4,6},{6,4},{8,10},{10,8},{12,14},{14,12},{16,18},{18,... | collective-permute-start | bytes 196616 | tf_op jit(solution)/shard_map/ppermute | solution.py:236
  33.5 9.3 %all-to-all-start = ((bf16[4,128,128]{2,1,0:T(8,128)(2,1)}), bf16[4,128,128]{2,1,0:T(8,128)(2,1)S(1)}, u32[]{:S(2)}, u32[]{:S(2)}) async-start(bf16[4,128,128]{2,1,0:T(8,128)(2,1)} %shard_map.112), calls=%async_computation | async-start | bytes 262144 | tf_op jit(solution)/shard_map/all_to_all | solution.py:238
  36.9 7.9 %copy-start.3 = (bf16[1,1024,128]{2,1,0:T(8,128)(2,1)S(1)}, bf16[1,1024,128]{2,1,0:T(8,128)(2,1)}, u32[]{:S(2)}) copy-start(bf16[1,1024,128]{2,1,0:T(8,128)(2,1)} %param.8) | copy-start | bytes 786436
  36.9 7.9 %copy-start.4 = (bf16[1,1024,128]{2,1,0:T(8,128)(2,1)S(1)}, bf16[1,1024,128]{2,1,0:T(8,128)(2,1)}, u32[]{:S(2)}) copy-start(bf16[1,1024,128]{2,1,0:T(8,128)(2,1)} %param.9) | copy-start | bytes 786436
  44.8 1.6 copy-start.1
  49.1 2.8 %copy-start.5 = (bf16[1024,256]{1,0:T(8,128)(2,1)}, bf16[1024,256]{1,0:T(8,128)(2,1)S(1)}, u32[]{:S(2)}) copy-start(bf16[1024,256]{1,0:T(8,128)(2,1)S(1)} %get-tuple-element.47.cols) | copy-start | bytes 1572868
  64.4 12.5 %collective-permute-start.2 = (bf16[128,256]{1,0:T(8,128)(2,1)S(1)}, bf16[128,256]{1,0:T(8,128)(2,1)S(1)}, u32[]{:S(2)}, u32[]{:S(2)}) collective-permute-start(bf16[128,256]{1,0:T(8,128)(2,1)S(1)} %shard_map.115.mine), channel_id=1, source_target_pairs={{0,256},{32,288},{64,320},{96,352},{128,384},{160,416},{192,448},{... | collective-permute-start | bytes 196616 | tf_op jit(solution)/shard_map/ppermute | solution.py:276
  68.7 17.7 %all-to-all-start.2 = ((bf16[16,32,256]{2,1,0:T(8,128)(2,1)}), bf16[16,32,256]{2,1,0:T(8,128)(2,1)S(1)}, u32[]{:S(2)}, u32[]{:S(2)}) async-start(bf16[16,32,256]{2,1,0:T(8,128)(2,1)} %bitcast.17), calls=%async_computation.2 | async-start | bytes 524288 | tf_op jit(solution)/shard_map/all_to_all | solution.py:278
  77.5 17.8 %collective-permute-start.3 = (bf16[128,256]{1,0:T(8,128)(2,1)S(1)}, bf16[128,256]{1,0:T(8,128)(2,1)S(1)}, u32[]{:S(2)}, u32[]{:S(2)}) collective-permute-start(bf16[128,256]{1,0:T(8,128)(2,1)S(1)} %shard_map.117.mine), channel_id=1, source_target_pairs={{0,1},{1,0},{2,3},{3,2},{4,5},{5,4},{6,7},{7,6},{8,9},{9,8},{10,11... | collective-permute-start | bytes 196616 | tf_op jit(solution)/shard_map/ppermute | solution.py:280
  87.8 14.5 %all-to-all-start.3 = ((bf16[16,32,256]{2,1,0:T(8,128)(2,1)}), bf16[16,32,256]{2,1,0:T(8,128)(2,1)S(1)}, u32[]{:S(2)}, u32[]{:S(2)}) async-start(bf16[16,32,256]{2,1,0:T(8,128)(2,1)} %get-tuple-element.44), calls=%async_computation.3 | async-start | bytes 524288 | tf_op jit(solution)/shard_map/all_to_all | solution.py:289
  95.3 1.0 copy-start.6
  113.9 1.6 copy-start.2
  133.5 12.2 %collective-permute-start.5 = (bf16[128,256]{1,0:T(8,128)(2,1)S(1)}, bf16[128,256]{1,0:T(8,128)(2,1)S(1)}, u32[]{:S(2)}, u32[]{:S(2)}) collective-permute-start(bf16[128,256]{1,0:T(8,128)(2,1)S(1)} %shard_map.121.mine), channel_id=1, source_target_pairs={{0,256},{32,288},{64,320},{96,352},{128,384},{160,416},{192,448},{... | collective-permute-start | bytes 196616 | tf_op jit(solution)/shard_map/ppermute | solution.py:276
  139.9 12.7 %all-to-all-start.6 = ((bf16[16,32,256]{2,1,0:T(8,128)(2,1)}), bf16[16,32,256]{2,1,0:T(8,128)(2,1)S(1)}, u32[]{:S(2)}, u32[]{:S(2)}) async-start(bf16[16,32,256]{2,1,0:T(8,128)(2,1)} %bitcast.21), calls=%async_computation.6 | async-start | bytes 524288 | tf_op jit(solution)/shard_map/all_to_all | solution.py:278
  146.2 16.9 %collective-permute-start.6 = (bf16[128,256]{1,0:T(8,128)(2,1)S(1)}, bf16[128,256]{1,0:T(8,128)(2,1)S(1)}, u32[]{:S(2)}, u32[]{:S(2)}) collective-permute-start(bf16[128,256]{1,0:T(8,128)(2,1)S(1)} %shard_map.124.mine), channel_id=1, source_target_pairs={{0,1},{1,0},{2,3},{3,2},{4,5},{5,4},{6,7},{7,6},{8,9},{9,8},{10,11... | collective-permute-start | bytes 196616 | tf_op jit(solution)/shard_map/ppermute | solution.py:280
  153.4 14.7 %collective-permute-start.4 = (bf16[32,256]{1,0:T(8,128)(2,1)S(1)}, bf16[32,256]{1,0:T(8,128)(2,1)S(1)}, u32[]{:S(2)}, u32[]{:S(2)}) collective-permute-start(bf16[32,256]{1,0:T(8,128)(2,1)S(1)} %get-tuple-element.57), channel_id=1, source_target_pairs={{0,1},{1,0},{2,3},{3,2},{4,5},{5,4},{6,7},{7,6},{8,9},{9,8},{10,11... | collective-permute-start | bytes 49160 | tf_op jit(solution)/shard_map/ppermute | solution.py:310
  164.7 10.2 %all-to-all-start.7 = ((bf16[4,128,256]{2,1,0:T(8,128)(2,1)}), bf16[4,128,256]{2,1,0:T(8,128)(2,1)S(1)}, u32[]{:S(2)}, u32[]{:S(2)}) async-start(bf16[4,128,256]{2,1,0:T(8,128)(2,1)} %shard_map.125), calls=%async_computation.7 | async-start | bytes 524288 | tf_op jit(solution)/shard_map/all_to_all | solution.py:314
  174.8 13.9 %all-to-all-start.8 = ((bf16[16,32,384]{2,1,0:T(8,128)(2,1)}), bf16[16,32,384]{2,1,0:T(8,128)(2,1)S(1)}, u32[]{:S(2)}, u32[]{:S(2)}) async-start(bf16[16,32,384]{2,1,0:T(8,128)(2,1)} %shard_map.123), calls=%async_computation.8 | async-start | bytes 786432 | tf_op jit(solution)/shard_map/all_to_all | solution.py:319

commit v4 on v3

--- a/solution.py
+++ b/solution.py
@@ -17,15 +17,16 @@
 ROW_PAIR = 256
 TILE_ROWS = 256
 
-C_SHARE, C_PAIR, C_ROW, C_COL, C_ROW_LAST, C_COL_LAST, C_PACK = 20, 20, 1, 20, 1, 20, 20
+C_COUNTS, C_SHARE, C_PAIR, C_ROW, C_COL, C_ROW_LAST, C_COL_LAST, C_PACK, C_QUAD, C_OUT = 5, 20, 20, 1, 20, 1, 20, 20, 20, 1
 
 CORE_PAIRS = [[2 * z, 2 * z + 1] for z in range(8)]
 Z_QUADS = [[2 * (4 * h + k) + core for k in range(4)] for h in range(2) for core in range(2)]
 FAR_Z = [(i, i ^ 8) for i in range(16)]
+IN_QUAD = [[(i, i ^ (2 * k)) for i in range(16)] for k in range(1, 4)]
 Y_SWAP = [(i, i ^ 1) for i in range(16)]
 DIM_SWAP = [(0, 1), (1, 0)]
 
-AT_DIM, AT_COL, AT_CORE, AT_COL_PART, AT_Y, AT_LIVE = range(6)
+AT_DIM, AT_ROW, AT_COL, AT_CORE, AT_COL_PART, AT_Y, AT_LIVE = range(7)
 
 
 def to_f32(block):
@@ -40,10 +41,10 @@
     return lax.broadcasted_iota(jnp.int32, (n, n), 0) == lax.broadcasted_iota(jnp.int32, (n, n), 1)
 
 
-def column(acc):
-    if acc.shape[0] > 1:
-        return acc
-    return jnp.sum(jnp.where(diagonal(acc.shape[1]), acc, 0.0), axis=1, keepdims=True)
+def column(values, start, n):
+    shape = (n, values.shape[1])
+    wanted = lax.broadcasted_iota(jnp.int32, shape, 1) == lax.broadcasted_iota(jnp.int32, shape, 0) + start
+    return jnp.sum(jnp.where(wanted, values, 0.0), axis=1, keepdims=True)
 
 
 def line(acc):
@@ -69,11 +70,30 @@
     return ref[pl.ds(pl.multiple_of(index * size, size), size), :]
 
 
+def counts_kernel(at, counts, row_marg, col_marg, weight, target):
+    marg = row_marg[...]
+    high, low = to_f32(marg >> 10), to_f32(marg & 1023)
+    high, low = (jnp.sum(jnp.sum(m, axis=0, keepdims=True), axis=1, keepdims=True) for m in (high, low))
+    log_total = jnp.log(high * 1024.0 + low)
+    col_logs = jnp.log(to_f32(col_marg[pl.ds(at[AT_COL], 1), :]))
+    start = pl.multiple_of(at[AT_DIM] * HALF_ROWS, HALF_ROWS)
+    row_logs = jnp.log(to_f32(row_marg[pl.ds(at[AT_ROW], 1), pl.ds(start, HALF_ROWS)]))
+    for part in range(HALF_ROWS // HALF_D):
+        here = slice(part * HALF_D, (part + 1) * HALF_D)
+        shift = log_total - column(row_logs[:, here], 0, HALF_D) - col_logs
+        tile = counts[here, :]
+        count = to_f32(tile)
+        weight[here, :] = jnp.where(tile > 0, (0.1 + 0.25 * jnp.sqrt(count)) / SIDE, 0.0)
+        target[here, :] = jnp.log(jnp.maximum(count, 1.0)) + shift
+
+
 def share_kernel(at, got, out):
     out[...] = jnp.broadcast_to(got[:COL_PART, :][None], out.shape)
 
 
-def tile_terms(at, rows, cols, weight, target, kept, given, row_term, col_sum):
+def tile_terms(at, rows, cols, weight, target, kept, given, row_term, row_was, col_was, col_sum):
+    row_was[...] = block_at(rows, at[AT_COL], ROW_PART)
+    col_was[...] = block_at(cols, at[AT_COL_PART], COL_PART)
     cols_all = cols[...]
     for part in range(HALF_ROWS // TILE_ROWS):
         here = slice(part * TILE_ROWS, (part + 1) * TILE_ROWS)
@@ -85,11 +105,13 @@
         scale = weight[here, :]
         sigmoid = (0.5 / SIDE) * jnp.tanh(0.5 * gap) + 0.5 / SIDE
         cell = jnp.where(scale > 0, scale * gap, sigmoid)
-        row = lax.broadcasted_iota(jnp.int32, cell.shape, 0) + part * TILE_ROWS
-        grad = jnp.where(row < at[AT_LIVE], cell, 0.0).astype(jnp.bfloat16)
-        row_term[here, :] = jnp.dot(grad, cols_all, preferred_element_type=jnp.float32).astype(jnp.bfloat16)
+        grad = cell.astype(jnp.bfloat16)
+        live = lax.broadcasted_iota(jnp.int32, (TILE_ROWS, WIDTH), 0) + part * TILE_ROWS < at[AT_LIVE]
+        row_sum = jnp.dot(grad, cols_all, preferred_element_type=jnp.float32)
+        row_term[here, :] = jnp.where(live, row_sum, 0.0).astype(jnp.bfloat16)
+        live_rows = jnp.where(live, to_f32(rows_here), 0.0).astype(jnp.bfloat16)
         term = lax.dot_general(
-            grad, rows_here, (((0,), (0,)), ((), ())), preferred_element_type=jnp.float32
+            grad, live_rows, (((0,), (0,)), ((), ())), preferred_element_type=jnp.float32
         )
         if part == 0:
             col_sum[...] = term
@@ -101,7 +123,22 @@
 
 
 def first_tile_kernel(
-    at, row_emb, got, there, col_emb, col_other, weight, target, kept, given, row_term, rows, cols, col_sum
+    at,
+    row_emb,
+    got,
+    there,
+    col_emb,
+    col_other,
+    weight,
+    target,
+    kept,
+    given,
+    row_term,
+    row_was,
+    col_was,
+    col_sum,
+    rows,
+    cols,
 ):
     side, y = at[AT_DIM], at[AT_Y]
     rows[:, :HALF_D] = block_at(row_emb, side, HALF_ROWS)
@@ -109,7 +146,7 @@
     rows[pl.ds(pl.multiple_of((1 - y) * ROW_PAIR, ROW_PAIR), ROW_PAIR), HALF_D:] = there[...]
     cols[:, :HALF_D] = col_emb[...]
     cols[:, HALF_D:] = col_other[...]
-    tile_terms(at, rows, cols, weight, target, kept, given, row_term, col_sum)
+    tile_terms(at, rows, cols, weight, target, kept, given, row_term, row_was, col_was, col_sum)
 
 
 def same_kernel(at, block, out):
@@ -131,13 +168,17 @@
 
 def row_kernel(at, parts, acc, rows, emb_out, acc_out):
     total = jnp.sum(to_f32(parts[...]), axis=0)
-    emb_new, acc_out[...] = adagrad(total, column(acc[...]), block_at(rows, at[AT_COL], ROW_PART))
+    emb_new, acc_out[...] = adagrad(
+        total,
+        column(acc[...], at[AT_DIM] * HALF_ROWS + at[AT_COL] * ROW_PART, ROW_PART),
+        rows[...],
+    )
     emb_out[...] = jnp.broadcast_to(emb_new[None], emb_out.shape)
 
 
 def row_last_kernel(at, parts, acc, rows, kept, sent):
     total = jnp.sum(to_f32(parts[...]), axis=0)
-    emb_new, acc_new = adagrad(total, acc[...], block_at(rows, at[AT_COL], ROW_PART))
+    emb_new, acc_new = adagrad(total, acc[...], rows[...])
     kept[:, :HALF_D] = emb_new[:, :HALF_D]
     kept[:, HALF_D:] = acc_lanes(acc_new, 0, 32)
     sent[:, :HALF_D] = emb_new[:, HALF_D:]
@@ -146,15 +187,26 @@
 
 def col_kernel(at, mine, theirs, acc, cols, emb_out, acc_out):
     total = to_f32(mine[...]) + swap_halves(to_f32(theirs[...]))
-    emb_new, acc_out[...] = adagrad(total, column(acc[...]), block_at(cols, at[AT_COL_PART], COL_PART))
-    emb_out[...] = jnp.broadcast_to(emb_new[None], emb_out.shape)
+    emb_new, acc_out[...] = adagrad(
+        total,
+        column(acc[...], at[AT_COL_PART] * COL_PART, COL_PART),
+        cols[...],
+    )
+    emb_out[...] = emb_new
 
 
 def col_last_kernel(at, mine, theirs, acc, cols, col_out):
     total = to_f32(mine[...]) + swap_halves(to_f32(theirs[...]))
-    emb_new, acc_new = adagrad(total, acc[...], block_at(cols, at[AT_COL_PART], COL_PART))
+    emb_new, acc_new = adagrad(total, acc[...], cols[...])
     col_new = jnp.concatenate([emb_new[:, :HALF_D], acc_lanes(acc_new, 0, 64)], axis=1)
-    col_out[...] = jnp.broadcast_to(col_new[None], col_out.shape)
+    col_out[...] = col_new
+
+
+def quad_kernel(at, own, one, two, three, out):
+    quad = at[AT_COL_PART] % 4
+    places = quad, quad + 1 - 2 * (quad % 2), (quad + 2) % 4, 3 - quad
+    for place, block in zip(places, (own, one, two, three), strict=True):
+        out[pl.ds(place, 1), :, :] = block[...][None]
 
 
 def pack_kernel(at, kept, theirs, row_out):
@@ -164,7 +216,7 @@
     row_out[...] = jnp.broadcast_to(row_new[None], row_out.shape)
 
 
-def out_kernel(at, rows, cols, row_out, row_acc_out, col_out, col_acc_out):
+def row_out_kernel(at, rows, row_out, acc_out):
     side = at[AT_DIM]
     for half, first in ((side, 0), (1 - side, HALF_D)):
         start = pl.multiple_of(half * HALF_ROWS, HALF_ROWS)
@@ -173,15 +225,18 @@
         acc = to_f32(rows[:, lane : lane + 1]) + to_f32(rows[:, lane + 32 : lane + 33])
         for k in range(HALF_ROWS // HALF_D):
             part = line(acc[k * HALF_D : (k + 1) * HALF_D])
-            row_acc_out[:, pl.ds(pl.multiple_of(start + k * HALF_D, HALF_D), HALF_D)] = part
+            acc_out[:, pl.ds(pl.multiple_of(start + k * HALF_D, HALF_D), HALF_D)] = part
+
+
+def col_out_kernel(at, cols, col_out, acc_out):
     col_out[0] = cols[:, :HALF_D]
     acc = to_f32(cols[:, HALF_D : HALF_D + 1]) + to_f32(cols[:, HALF_D + 64 : HALF_D + 65])
     for k in range(SIDE // HALF_D):
         part = slice(k * HALF_D, (k + 1) * HALF_D)
-        col_acc_out[:, part] = line(acc[part])
-
-
-def on_device(kernel, at, operands, shapes, micros, vmem_mib=4, scratch=()):
+        acc_out[:, part] = line(acc[part])
+
+
+def on_device(kernel, at, operands, shapes, micros, vmem_mib=2, scratch=()):
     vmem = pl.BlockSpec(memory_space=pltpu.VMEM)
     return pl.pallas_call(
         kernel,
@@ -208,7 +263,7 @@
     row_emb, col_emb = row_emb[0], col_emb[0]
     col_part = core * 4 + quad
     live_here = live_rows[0, 0] - d * HALF_ROWS
-    at = jnp.stack([d, c, core, col_part, y, live_here]).astype(jnp.int32)
+    at = jnp.stack([d, r, c, core, col_part, y, live_here]).astype(jnp.int32)
 
     def rows_at(block, start, size):
         return lax.dynamic_slice_in_dim(block, start, size, 0)
@@ -221,18 +276,14 @@
     )
     got = lax.ppermute(sent, "dim", DIM_SWAP)
 
-    log_total = jnp.log(jnp.sum(row_marg).astype(jnp.float32))
-    own_marg = lax.dynamic_index_in_dim(row_marg, r, 0, False)
-    row_logs = jnp.log(rows_at(own_marg, d * HALF_ROWS, HALF_ROWS).astype(jnp.float32))
-    col_logs = jnp.log(lax.dynamic_index_in_dim(col_marg, c, 0, False).astype(jnp.float32))
-    shift_log = log_total - row_logs[:, None] - col_logs[None, :]
-    tile = counts[0, 0]
-    count_f = tile.astype(jnp.float32)
-    weight = jnp.where(tile > 0, (0.1 + 0.25 * jnp.sqrt(count_f)) / SIDE, 0.0)
-    target = jnp.log(jnp.maximum(count_f, 1.0)) + shift_log
-    row_acc = rows_at(row_acc[0], d * HALF_ROWS + c * ROW_PART, ROW_PART)[None]
-    col_acc = rows_at(col_acc[0], col_part * COL_PART, COL_PART)[None]
-
+    weight, target = on_device(
+        counts_kernel,
+        at,
+        (counts[0, 0], row_marg, col_marg),
+        (f32(HALF_ROWS, SIDE), f32(HALF_ROWS, SIDE)),
+        C_COUNTS,
+        16,
+    )
     there = lax.ppermute(got[COL_PART:], "col", Y_SWAP)
     (shared,) = on_device(share_kernel, at, (got,), (bf16(4, COL_PART, HALF_D),), 1)
     col_other = lax.all_to_all(shared, "row", 0, 0, axis_index_groups=Z_QUADS)
@@ -242,30 +293,30 @@
     there, col_other = lax.optimization_barrier((there, col_other))
     col_other = lax.all_gather(col_other, "row", tiled=True, axis_index_groups=CORE_PAIRS)
     col_other = col_other.reshape(SIDE, HALF_D)
-    weight, target, row_acc, col_acc = lax.optimization_barrier((weight, target, row_acc, col_acc))
-
-    terms = (bf16(HALF_ROWS, WIDTH), bf16(HALF_ROWS, WIDTH), bf16(HALF_ROWS, WIDTH))
+
+    terms = (bf16(HALF_ROWS, WIDTH),) * 3 + (bf16(ROW_PART, WIDTH), bf16(COL_PART, WIDTH))
+    col_sum = pltpu.VMEM((SIDE, WIDTH), jnp.float32)
     for step in range(STEPS):
         last = step == STEPS - 1
         if step == 0:
-            kept, given, row_term, rows, cols = on_device(
+            kept, given, row_term, row_was, col_was = on_device(
                 first_tile_kernel,
                 at,
                 (row_emb, got, there, col_emb, col_other, weight, target),
-                terms + (bf16(HALF_ROWS, WIDTH), bf16(SIDE, WIDTH)),
+                terms,
                 3,
-                24,
-                [pltpu.VMEM((SIDE, WIDTH), jnp.float32)],
+                16,
+                [col_sum, pltpu.VMEM((HALF_ROWS, WIDTH), jnp.bfloat16), pltpu.VMEM((SIDE, WIDTH), jnp.bfloat16)],
             )
         else:
-            kept, given, row_term = on_device(
+            kept, given, row_term, row_was, col_was = on_device(
                 tile_terms,
                 at,
                 (rows, cols, weight, target),
                 terms,
                 3,
-                24,
-                [pltpu.VMEM((SIDE, WIDTH), jnp.float32)],
+                16,
+                [col_sum],
             )
 
         pair = lax.all_gather(given, "row", axis_index_groups=CORE_PAIRS)
@@ -282,7 +333,7 @@
             rows, row_acc = on_device(
                 row_kernel,
                 at,
-                (row_parts, row_acc, rows),
+                (row_parts, row_acc, row_was),
                 (bf16(N_COL, ROW_PART, WIDTH), f32(ROW_PART, 1)),
                 C_ROW,
             )
@@ -290,12 +341,13 @@
             cols, col_acc = on_device(
                 col_kernel,
                 at,
-                (near, far, col_acc, cols),
-                (bf16(4, COL_PART, WIDTH), f32(COL_PART, 1)),
+                (near, far, col_acc, col_was),
+                (bf16(COL_PART, WIDTH), f32(COL_PART, 1)),
                 C_COL,
             )
-            rows, cols = lax.optimization_barrier((rows, cols))
-            cols = lax.all_to_all(cols, "row", 0, 0, axis_index_groups=Z_QUADS)
+            blocks = [cols] + [lax.ppermute(cols, "row", swap) for swap in IN_QUAD]
+            rows, *blocks = lax.optimization_barrier((rows, *blocks))
+            (cols,) = on_device(quad_kernel, at, blocks, (bf16(4, COL_PART, WIDTH),), C_QUAD)
             cols = lax.all_gather(cols, "row", tiled=True, axis_index_groups=CORE_PAIRS)
             cols = cols.reshape(SIDE, WIDTH)
             continue
@@ -303,32 +355,27 @@
         kept, sent = on_device(
             row_last_kernel,
             at,
-            (row_parts, row_acc, rows),
+            (row_parts, row_acc, row_was),
             (bf16(ROW_PART, WIDTH), bf16(ROW_PART, WIDTH)),
             C_ROW_LAST,
         )
         rows_far = lax.ppermute(sent, "dim", DIM_SWAP)
         (cols,) = on_device(
-            col_last_kernel, at, (near, far, col_acc, cols), (bf16(4, COL_PART, WIDTH),), C_COL_LAST
-        )
-        cols = lax.all_to_all(cols, "row", 0, 0, axis_index_groups=Z_QUADS)
+            col_last_kernel, at, (near, far, col_acc, col_was), (bf16(COL_PART, WIDTH),), C_COL_LAST
+        )
+        blocks = [cols] + [lax.ppermute(cols, "row", swap) for swap in IN_QUAD]
         (rows,) = on_device(
             pack_kernel, at, (kept, rows_far), (bf16(N_COL, ROW_PART, WIDTH + HALF_D),), C_PACK
         )
-        rows, cols = lax.optimization_barrier((rows, cols))
         rows = lax.all_to_all(rows, "col", 0, 0)
+        (cols,) = on_device(quad_kernel, at, blocks, (bf16(4, COL_PART, WIDTH),), C_QUAD)
         cols = lax.all_gather(cols, "row", tiled=True, axis_index_groups=CORE_PAIRS)
-        rows, cols = lax.optimization_barrier((rows, cols))
-
+
+    shapes = bf16(1, SIDE, HALF_D), f32(1, SIDE)
+    cols = on_device(col_out_kernel, at, (cols.reshape(SIDE, WIDTH),), shapes, C_OUT)
+    rows, *cols = lax.optimization_barrier((rows, *cols))
     rows = rows.reshape(HALF_ROWS, WIDTH + HALF_D)
-    cols = cols.reshape(SIDE, WIDTH)
-    return on_device(
-        out_kernel,
-        at,
-        (rows, cols),
-        (bf16(1, SIDE, HALF_D), f32(1, SIDE), bf16(1, SIDE, HALF_D), f32(1, SIDE)),
-        1,
-    )
+    return (*on_device(row_out_kernel, at, (rows,), shapes, 1), *cols)
 
 
 def solution(mesh):

time: 192 us -> 188 us (0.979)
  starting transfers between devices: 86.2 us -> 109 us
  waiting for transfers between devices: 23.6 us -> 11.5 us
  other arithmetic: 9.65 us -> 0.01 us
  blocking collectives: 43.9 us -> 34.9 us
  Pallas kernels: 18.3 us -> 21.6 us
    ppermute x0 -> x6, starting transfers between devices: none -> 20.2 us  [shards(): blocks = [cols] + [lax.ppermute(cols, 'row', swap) for swap in IN_QUAD]]
    all_to_all x1 -> x0, blocking collectives: 9.5 us -> none  [shards(): cols = lax.all_to_all(cols, 'row', 0, 0, axis_index_groups=Z_QUADS)]
    all_to_all x1 -> x0, waiting for transfers between devices: 5.4 us -> none  [shards(): cols = lax.all_to_all(cols, 'row', 0, 0, axis_index_groups=Z_QUADS)]
    all_to_all x1, waiting for transfers between devices: 5.24 us -> 0.01 us  [shards(): rows = lax.all_to_all(rows, 'col', 0, 0).reshape(HALF_ROWS, WIDTH)]
    all_to_all x1 -> x0, starting transfers between devices: 3.41 us -> none  [shards(): cols = lax.all_to_all(cols, 'row', 0, 0, axis_index_groups=Z_QUADS)]
    add x1 -> x0, other arithmetic: 3.36 us -> none  [shards(): target = jnp.log(jnp.maximum(count_f, 1.0)) + shift_log]
    pallas_call x16 -> x20, Pallas kernels: 18.3 us -> 21.6 us  [on_device(): pl.pallas_call(kernel, in_specs=[pl.BlockSpec(memory_space=pltpu.SMEM)] +...]
    select_n x1 -> x0, other arithmetic: 3.11 us -> none  [shards(): weight = jnp.where(tile > 0, (0.1 + 0.25 * jnp.sqrt(count_f)) / SIDE, 0.0)]
  transfers between devices with their start and end apart: 13 -> 18, of which waited for: 6 -> 5; matrix products, arithmetic and copies ran while one was open for 5% -> 0% of each run, Pallas kernels for 4% -> 6%
where the time goes in v4:
time: 188 us; the launch traced here: 187 us
  starting transfers between devices  109 us (58%)
  blocking collectives  34.9 us (19%)
  Pallas kernels  21.6 us (11%)
  waiting for transfers between devices  11.5 us (6%)
  local copies, waits for them, and re-layouts  7.94 us (4%)
    all_to_all x2, blocking collectives, shards(): parts = lax.all_to_all(half, 'row', 0, 0, axis_index_groups=Z_QUADS)  24.1 us
    pallas_call x20, Pallas kernels, on_device(): pl.pallas_call(kernel, in_specs=[pl.BlockSpec(memory_space=pltpu.SMEM)] +...  21.6 us
    ppermute x6, starting transfers between devices, shards(): blocks = [cols] + [lax.ppermute(cols, 'row', swap) for swap in IN_QUAD]  20.2 us
    ppermute x2, starting transfers between devices, shards(): far = lax.ppermute(near, 'dim', DIM_SWAP)  16.6 us
    ppermute x1, starting transfers between devices, shards(): got = lax.ppermute(sent, 'dim', DIM_SWAP)  15.7 us
    all_to_all x2, starting transfers between devices, shards(): lax.all_to_all(row_term.reshape(N_COL, ROW_PART, WIDTH), 'col', 0, 0)  15.5 us
    ppermute x2, starting transfers between devices, shards(): far = lax.ppermute(near, 'row', FAR_Z)  13.4 us
    ppermute x1, starting transfers between devices, shards(): rows_far = lax.ppermute(sent, 'dim', DIM_SWAP)  7.75 us
  transfers between devices with their start and end apart: 18, of which 5 were waited for; matrix products, arithmetic and copies ran while one was open for 0% of the time, Pallas kernels for 6%

profile of v4, /device:TPU:8, one launch (start us, length us, event | category | flops | bytes accessed | tf_op | source)
XLA Modules:
  0.0 186.9 jit_solution(18353444656382022712)
XLA Ops:
  2.3 15.7 %collective-permute-start = (bf16[384,128]{1,0:T(8,128)(2,1)S(1)}, bf16[384,128]{1,0:T(8,128)(2,1)S(1)}, u32[]{:S(2)}, u32[]{:S(2)}) collective-permute-start(bf16[384,128]{1,0:T(8,128)(2,1)S(1)} %pad_maximum_fusion), channel_id=1, source_target_pairs={{0,1},{1,0},{2,3},{3,2},{4,5},{5,4},{6,7},{7,6},{8,9},{9,8},{10,11... | collective-permute-start | bytes 294920 | tf_op jit(solution)/shard_map/ppermute | solution.py:277
  18.8 1.6 copy-done.2
  22.1 2.1 %shard_map.113 = (f32[512,1024]{1,0:T(8,128)S(1)}, f32[512,1024]{1,0:T(8,128)S(1)}) custom-call(s32[7]{0:T(128)S(1)} %stack.31.at, s32[512,1024]{1,0:T(8,128)S(1)} %bitcast.34, s32[16,1024]{1,0:T(8,128)S(1)} %copy-done.3, s32[16,1024]{1,0:T(8,128)S(1)} %copy-done.4), custom_call_target="tpu_custom_call" | custom-call | flops 5000000000 | bytes 262144 | tf_op jit(solution)/shard_map/pallas_call | solution.py:241
  25.5 2.4 %collective-permute-start.1 = (bf16[256,128]{1,0:T(8,128)(2,1)S(1)}, bf16[256,128]{1,0:T(8,128)(2,1)S(1)}, u32[]{:S(2)}, u32[]{:S(2)}) collective-permute-start(bf16[256,128]{1,0:T(8,128)(2,1)S(1)} %slice.4), channel_id=1, source_target_pairs={{0,2},{2,0},{4,6},{6,4},{8,10},{10,8},{12,14},{14,12},{16,18},{18,... | collective-permute-start | bytes 196616 | tf_op jit(solution)/shard_map/ppermute | solution.py:287
  29.1 3.3 %all-to-all-start = ((bf16[4,128,128]{2,1,0:T(8,128)(2,1)}), bf16[4,128,128]{2,1,0:T(8,128)(2,1)S(1)}, u32[]{:S(2)}, u32[]{:S(2)}) async-start(bf16[4,128,128]{2,1,0:T(8,128)(2,1)} %shard_map.112), calls=%async_computation | async-start | bytes 262144 | tf_op jit(solution)/shard_map/all_to_all | solution.py:289
  33.0 5.4 %all-to-all-done = bf16[4,128,128]{2,1,0:T(8,128)(2,1)S(1)} async-done(((bf16[4,128,128]{2,1,0:T(8,128)(2,1)}), bf16[4,128,128]{2,1,0:T(8,128)(2,1)S(1)}, u32[]{:S(2)}, u32[]{:S(2)}) %all-to-all-start) | async-done | bytes 131104 | tf_op jit(solution)/shard_map/all_to_all | solution.py:289
  38.4 2.0 %all_gather.21 = bf16[8,128,128]{2,1,0:T(8,128)(2,1)S(1)} all-gather(bf16[4,128,128]{2,1,0:T(8,128)(2,1)S(1)} %all-to-all-done), channel_id=1, replica_groups={{0,32},{64,96},{128,160},{192,224},{256,288},{320,352},{384,416},{448,4..., dimensions={0}, use_global_device_ids=true | all-gather | bytes 393216 | tf_op jit(solution)/shard_map/all_gather | solution.py:294
  42.0 2.6 %shard_map.114 = (bf16[512,256]{1,0:T(8,128)(2,1)S(1)}, bf16[512,256]{1,0:T(8,128)(2,1)S(1)}, bf16[512,256]{1,0:T(8,128)(2,1)}, bf16[32,256]{1,0:T(8,128)(2,1)S(1)}, bf16[128,256]{1,0:T(8,128)(2,1)S(1)}) custom-call(s32[7]{0:T(128)S(1)} %stack.31.at, bf16[1024,128]{1,0:T(8,128)(2,1)S(1)} %bitcast.32, bf16[384,128]{1,0:T(8,128)(2,1)S(1)} %collective-permute-done.got, ...), custom_call_target="tpu_custom_call" | custom-call | flops 3000000000 | bytes 262144 | tf_op jit(solution)/shard_map/pallas_call | solution.py:241
  44.5 2.2 %all-gather = bf16[1024,256]{1,0:T(8,128)(2,1)S(1)} all-gather(bf16[512,256]{1,0:T(8,128)(2,1)S(1)} %get-tuple-element.46), channel_id=2, replica_groups={{0,32},{64,96},{128,160},{192,224},{256,288},{320,352},{384,416},{448,4..., dimensions={0}, use_global_device_ids=true | all-gather | bytes 786432 | tf_op jit(solution)/shard_map/all_gather | solution.py:322
  47.3 11.9 %all_to_all.35.parts = bf16[4,128,256]{2,1,0:T(8,128)(2,1)S(1)} all-to-all(bf16[4,128,256]{2,1,0:T(8,128)(2,1)S(1)} %shard_map.115), channel_id=1, replica_groups={{0,64,128,192},{32,96,160,224},{256,320,384,448},{288,352,416,480},{1,6..., dimensions={0} | all-to-all | bytes 524288 | tf_op jit(solution)/shard_map/all_to_all | solution.py:324
  59.8 7.8 %collective-permute-start.2 = (bf16[128,256]{1,0:T(8,128)(2,1)S(1)}, bf16[128,256]{1,0:T(8,128)(2,1)S(1)}, u32[]{:S(2)}, u32[]{:S(2)}) collective-permute-start(bf16[128,256]{1,0:T(8,128)(2,1)S(1)} %shard_map.116.mine), channel_id=1, source_target_pairs={{0,256},{32,288},{64,320},{96,352},{128,384},{160,416},{192,448},{... | collective-permute-start | bytes 196616 | tf_op jit(solution)/shard_map/ppermute | solution.py:327
  67.6 8.2 %all-to-all-start.2 = ((bf16[16,32,256]{2,1,0:T(8,128)(2,1)}), bf16[16,32,256]{2,1,0:T(8,128)(2,1)S(1)}, u32[]{:S(2)}, u32[]{:S(2)}) async-start(bf16[16,32,256]{2,1,0:T(8,128)(2,1)} %bitcast.15), calls=%async_computation.2 | async-start | bytes 524288 | tf_op jit(solution)/shard_map/all_to_all | solution.py:329
  76.4 9.8 %collective-permute-start.3 = (bf16[128,256]{1,0:T(8,128)(2,1)S(1)}, bf16[128,256]{1,0:T(8,128)(2,1)S(1)}, u32[]{:S(2)}, u32[]{:S(2)}) collective-permute-start(bf16[128,256]{1,0:T(8,128)(2,1)S(1)} %shard_map.118.mine), channel_id=1, source_target_pairs={{0,1},{1,0},{2,3},{3,2},{4,5},{5,4},{6,7},{7,6},{8,9},{9,8},{10,11... | collective-permute-start | bytes 196616 | tf_op jit(solution)/shard_map/ppermute | solution.py:331
  87.7 7.5 %all-to-all-start.3 = ((bf16[16,32,256]{2,1,0:T(8,128)(2,1)}), bf16[16,32,256]{2,1,0:T(8,128)(2,1)S(1)}, u32[]{:S(2)}, u32[]{:S(2)}) async-start(bf16[16,32,256]{2,1,0:T(8,128)(2,1)} %get-tuple-element.49), calls=%async_computation.3 | async-start | bytes 524288 | tf_op jit(solution)/shard_map/all_to_all | solution.py:340
  95.9 3.1 %collective-permute-start.6 = (bf16[128,256]{1,0:T(8,128)(2,1)S(1)}, bf16[128,256]{1,0:T(8,128)(2,1)S(1)}, u32[]{:S(2)}, u32[]{:S(2)}) collective-permute-start(bf16[128,256]{1,0:T(8,128)(2,1)S(1)} %get-tuple-element.54.own), channel_id=1, source_target_pairs={{0,192},{32,224},{64,128},{96,160},{128,64},{160,96},{192,0},{224,... | collective-permute-start | bytes 196616 | tf_op jit(solution)/shard_map/ppermute | solution.py:348
  99.0 2.1 %collective-permute-start.5 = (bf16[128,256]{1,0:T(8,128)(2,1)S(1)}, bf16[128,256]{1,0:T(8,128)(2,1)S(1)}, u32[]{:S(2)}, u32[]{:S(2)}) collective-permute-start(bf16[128,256]{1,0:T(8,128)(2,1)S(1)} %get-tuple-element.54.own), channel_id=1, source_target_pairs={{0,128},{32,160},{64,192},{96,224},{128,0},{160,32},{192,64},{224,... | collective-permute-start | bytes 196616 | tf_op jit(solution)/shard_map/ppermute | solution.py:348
  101.1 4.9 %collective-permute-start.4 = (bf16[128,256]{1,0:T(8,128)(2,1)S(1)}, bf16[128,256]{1,0:T(8,128)(2,1)S(1)}, u32[]{:S(2)}, u32[]{:S(2)}) collective-permute-start(bf16[128,256]{1,0:T(8,128)(2,1)S(1)} %get-tuple-element.54.own), channel_id=1, source_target_pairs={{0,64},{32,96},{64,0},{96,32},{128,192},{160,224},{192,128},{224,1... | collective-permute-start | bytes 196616 | tf_op jit(solution)/shard_map/ppermute | solution.py:348
  106.6 1.6 collective-permute-done.4.one
  108.8 2.3 %all_gather.24 = bf16[8,128,256]{2,1,0:T(8,128)(2,1)S(1)} all-gather(bf16[4,128,256]{2,1,0:T(8,128)(2,1)S(1)} %shard_map.120), channel_id=1, replica_groups={{0,32},{64,96},{128,160},{192,224},{256,288},{320,352},{384,416},{448,4..., dimensions={0}, use_global_device_ids=true | all-gather | bytes 786432 | tf_op jit(solution)/shard_map/all_gather | solution.py:351
  111.1 2.5 %shard_map.121 = (bf16[512,256]{1,0:T(8,128)(2,1)S(1)}, bf16[512,256]{1,0:T(8,128)(2,1)S(1)}, bf16[512,256]{1,0:T(8,128)(2,1)}, bf16[32,256]{1,0:T(8,128)(2,1)S(1)}, bf16[128,256]{1,0:T(8,128)(2,1)S(1)}) custom-call(s32[7]{0:T(128)S(1)} %stack.31.at, bf16[512,256]{1,0:T(8,128)(2,1)S(1)} %bitcast.31, bf16[1024,256]{1,0:T(8,128)(2,1)S(1)} %bitcast.25, ...), custom_call_target="tpu_custom_call" | custom-call | flops 3000000000 | bytes 262144 | tf_op jit(solution)/shard_map/pallas_call | solution.py:241
  113.6 2.2 %all-gather.1 = bf16[1024,256]{1,0:T(8,128)(2,1)S(1)} all-gather(bf16[512,256]{1,0:T(8,128)(2,1)S(1)} %get-tuple-element.60), channel_id=3, replica_groups={{0,32},{64,96},{128,160},{192,224},{256,288},{320,352},{384,416},{448,4..., dimensions={0}, use_global_device_ids=true | all-gather | bytes 786432 | tf_op jit(solution)/shard_map/all_gather | solution.py:322
  116.4 12.3 %all_to_all.36.parts = bf16[4,128,256]{2,1,0:T(8,128)(2,1)S(1)} all-to-all(bf16[4,128,256]{2,1,0:T(8,128)(2,1)S(1)} %shard_map.122), channel_id=1, replica_groups={{0,64,128,192},{32,96,160,224},{256,320,384,448},{288,352,416,480},{1,6..., dimensions={0} | all-to-all | bytes 524288 | tf_op jit(solution)/shard_map/all_to_all | solution.py:324
  129.3 5.5 %collective-permute-start.8 = (bf16[128,256]{1,0:T(8,128)(2,1)S(1)}, bf16[128,256]{1,0:T(8,128)(2,1)S(1)}, u32[]{:S(2)}, u32[]{:S(2)}) collective-permute-start(bf16[128,256]{1,0:T(8,128)(2,1)S(1)} %shard_map.123.mine), channel_id=1, source_target_pairs={{0,256},{32,288},{64,320},{96,352},{128,384},{160,416},{192,448},{... | collective-permute-start | bytes 196616 | tf_op jit(solution)/shard_map/ppermute | solution.py:327
  134.8 7.2 %all-to-all-start.5 = ((bf16[16,32,256]{2,1,0:T(8,128)(2,1)}), bf16[16,32,256]{2,1,0:T(8,128)(2,1)S(1)}, u32[]{:S(2)}, u32[]{:S(2)}) async-start(bf16[16,32,256]{2,1,0:T(8,128)(2,1)} %bitcast.19), calls=%async_computation.5 | async-start | bytes 524288 | tf_op jit(solution)/shard_map/all_to_all | solution.py:329
  142.6 6.8 %collective-permute-start.9 = (bf16[128,256]{1,0:T(8,128)(2,1)S(1)}, bf16[128,256]{1,0:T(8,128)(2,1)S(1)}, u32[]{:S(2)}, u32[]{:S(2)}) collective-permute-start(bf16[128,256]{1,0:T(8,128)(2,1)S(1)} %shard_map.126.mine), channel_id=1, source_target_pairs={{0,1},{1,0},{2,3},{3,2},{4,5},{5,4},{6,7},{7,6},{8,9},{9,8},{10,11... | collective-permute-start | bytes 196616 | tf_op jit(solution)/shard_map/ppermute | solution.py:331
  150.2 7.8 %collective-permute-start.7 = (bf16[32,256]{1,0:T(8,128)(2,1)S(1)}, bf16[32,256]{1,0:T(8,128)(2,1)S(1)}, u32[]{:S(2)}, u32[]{:S(2)}) collective-permute-start(bf16[32,256]{1,0:T(8,128)(2,1)S(1)} %get-tuple-element.65), channel_id=1, source_target_pairs={{0,1},{1,0},{2,3},{3,2},{4,5},{5,4},{6,7},{7,6},{8,9},{9,8},{10,11... | collective-permute-start | bytes 49160 | tf_op jit(solution)/shard_map/ppermute | solution.py:362
  159.4 3.6 %collective-permute-start.12 = (bf16[128,256]{1,0:T(8,128)(2,1)S(1)}, bf16[128,256]{1,0:T(8,128)(2,1)S(1)}, u32[]{:S(2)}, u32[]{:S(2)}) collective-permute-start(bf16[128,256]{1,0:T(8,128)(2,1)S(1)} %shard_map.127.own), channel_id=1, source_target_pairs={{0,192},{32,224},{64,128},{96,160},{128,64},{160,96},{192,0},{224,... | collective-permute-start | bytes 196616 | tf_op jit(solution)/shard_map/ppermute | solution.py:366
  163.1 1.9 %collective-permute-start.11 = (bf16[128,256]{1,0:T(8,128)(2,1)S(1)}, bf16[128,256]{1,0:T(8,128)(2,1)S(1)}, u32[]{:S(2)}, u32[]{:S(2)}) collective-permute-start(bf16[128,256]{1,0:T(8,128)(2,1)S(1)} %shard_map.127.own), channel_id=1, source_target_pairs={{0,128},{32,160},{64,192},{96,224},{128,0},{160,32},{192,64},{224,... | collective-permute-start | bytes 196616 | tf_op jit(solution)/shard_map/ppermute | solution.py:366
  165.0 4.5 %collective-permute-start.10 = (bf16[128,256]{1,0:T(8,128)(2,1)S(1)}, bf16[128,256]{1,0:T(8,128)(2,1)S(1)}, u32[]{:S(2)}, u32[]{:S(2)}) collective-permute-start(bf16[128,256]{1,0:T(8,128)(2,1)S(1)} %shard_map.127.own), channel_id=1, source_target_pairs={{0,64},{32,96},{64,0},{96,32},{128,192},{160,224},{192,128},{224,1... | collective-permute-start | bytes 196616 | tf_op jit(solution)/shard_map/ppermute | solution.py:366
  170.9 6.9 %all-to-all-start.6 = ((bf16[16,32,384]{2,1,0:T(8,128)(2,1)}), bf16[16,32,384]{2,1,0:T(8,128)(2,1)S(1)}, u32[]{:S(2)}, u32[]{:S(2)}) async-start(bf16[16,32,384]{2,1,0:T(8,128)(2,1)} %shard_map.125), calls=%async_computation.6 | async-start | bytes 786432 | tf_op jit(solution)/shard_map/all_to_all | solution.py:370
  178.4 2.2 %all_gather.27 = bf16[8,128,256]{2,1,0:T(8,128)(2,1)S(1)} all-gather(bf16[4,128,256]{2,1,0:T(8,128)(2,1)S(1)} %shard_map.128), channel_id=1, replica_groups={{0,32},{64,96},{128,160},{192,224},{256,288},{320,352},{384,416},{448,4..., dimensions={0}, use_global_device_ids=true | all-gather | bytes 786432 | tf_op jit(solution)/shard_map/all_gather | solution.py:372
  182.1 3.3 %all-to-all-done.6 = bf16[16,32,384]{2,1,0:T(8,128)(2,1)S(1)} async-done(((bf16[16,32,384]{2,1,0:T(8,128)(2,1)}), bf16[16,32,384]{2,1,0:T(8,128)(2,1)S(1)}, u32[]{:S(2)}, u32[]{:S(2)}) %all-to-all-start.6) | async-done | bytes 393248 | tf_op jit(solution)/shard_map/all_to_all | solution.py:370
  (56 shorter events, 22.1 us)
Async XLA Ops:
  2.3 23.2 %collective-permute-start = (bf16[384,128]{1,0:T(8,128)(2,1)S(1)}, bf16[384,128]{1,0:T(8,128)(2,1)S(1)}, u32[]{:S(2)}, u32[]{:S(2)}) collective-permute-start(bf16[384,128]{1,0:T(8,128)(2,1)S(1)} %pad_maximum_fusion), channel_id=1, source_target_pairs={{0,1},{1,0},{2,3},{3,2},{4,5},{5,4},{6,7},{7,6},{8,9},{9,8},{10,11... | collective-permute-start | bytes 294920 | tf_op jit(solution)/shard_map/ppermute | solution.py:277
  18.8 1.6 copy-start.2
  20.4 0.8 copy-start.3
  21.2 0.8 copy-start.4
  24.2 1.4 copy-start.7
  25.5 6.9 %collective-permute-start.1 = (bf16[256,128]{1,0:T(8,128)(2,1)S(1)}, bf16[256,128]{1,0:T(8,128)(2,1)S(1)}, u32[]{:S(2)}, u32[]{:S(2)}) collective-permute-start(bf16[256,128]{1,0:T(8,128)(2,1)S(1)} %slice.4), channel_id=1, source_target_pairs={{0,2},{2,0},{4,6},{6,4},{8,10},{10,8},{12,14},{14,12},{16,18},{18,... | collective-permute-start | bytes 196616 | tf_op jit(solution)/shard_map/ppermute | solution.py:287
  29.1 9.3 %all-to-all-start = ((bf16[4,128,128]{2,1,0:T(8,128)(2,1)}), bf16[4,128,128]{2,1,0:T(8,128)(2,1)S(1)}, u32[]{:S(2)}, u32[]{:S(2)}) async-start(bf16[4,128,128]{2,1,0:T(8,128)(2,1)} %shard_map.112), calls=%async_computation | async-start | bytes 262144 | tf_op jit(solution)/shard_map/all_to_all | solution.py:289
  32.5 7.9 %copy-start = (bf16[1,1024,128]{2,1,0:T(8,128)(2,1)S(1)}, bf16[1,1024,128]{2,1,0:T(8,128)(2,1)}, u32[]{:S(2)}) copy-start(bf16[1,1024,128]{2,1,0:T(8,128)(2,1)} %param.8) | copy-start | bytes 786436
  32.5 7.9 %copy-start.1 = (bf16[1,1024,128]{2,1,0:T(8,128)(2,1)S(1)}, bf16[1,1024,128]{2,1,0:T(8,128)(2,1)}, u32[]{:S(2)}) copy-start(bf16[1,1024,128]{2,1,0:T(8,128)(2,1)} %param.9) | copy-start | bytes 786436
  40.4 1.6 copy-start.8
  59.8 16.1 %collective-permute-start.2 = (bf16[128,256]{1,0:T(8,128)(2,1)S(1)}, bf16[128,256]{1,0:T(8,128)(2,1)S(1)}, u32[]{:S(2)}, u32[]{:S(2)}) collective-permute-start(bf16[128,256]{1,0:T(8,128)(2,1)S(1)} %shard_map.116.mine), channel_id=1, source_target_pairs={{0,256},{32,288},{64,320},{96,352},{128,384},{160,416},{192,448},{... | collective-permute-start | bytes 196616 | tf_op jit(solution)/shard_map/ppermute | solution.py:327
  67.6 18.6 %all-to-all-start.2 = ((bf16[16,32,256]{2,1,0:T(8,128)(2,1)}), bf16[16,32,256]{2,1,0:T(8,128)(2,1)S(1)}, u32[]{:S(2)}, u32[]{:S(2)}) async-start(bf16[16,32,256]{2,1,0:T(8,128)(2,1)} %bitcast.15), calls=%async_computation.2 | async-start | bytes 524288 | tf_op jit(solution)/shard_map/all_to_all | solution.py:329
  75.8 10.4 %copy-start.5 = (f32[1,1024]{1,0:T(1,128)S(1)}, f32[1,1024]{1,0:T(1,128)}, u32[]{:S(2)}) copy-start(f32[1,1024]{1,0:T(1,128)} %acc.2) | copy-start | bytes 12292
  76.4 18.7 %collective-permute-start.3 = (bf16[128,256]{1,0:T(8,128)(2,1)S(1)}, bf16[128,256]{1,0:T(8,128)(2,1)S(1)}, u32[]{:S(2)}, u32[]{:S(2)}) collective-permute-start(bf16[128,256]{1,0:T(8,128)(2,1)S(1)} %shard_map.118.mine), channel_id=1, source_target_pairs={{0,1},{1,0},{2,3},{3,2},{4,5},{5,4},{6,7},{7,6},{8,9},{9,8},{10,11... | collective-permute-start | bytes 196616 | tf_op jit(solution)/shard_map/ppermute | solution.py:331
  86.2 8.9 %copy-start.6 = (f32[1,1024]{1,0:T(1,128)S(1)}, f32[1,1024]{1,0:T(1,128)}, u32[]{:S(2)}) copy-start(f32[1,1024]{1,0:T(1,128)} %acc.3) | copy-start | bytes 12292
  87.7 20.6 %all-to-all-start.3 = ((bf16[16,32,256]{2,1,0:T(8,128)(2,1)}), bf16[16,32,256]{2,1,0:T(8,128)(2,1)S(1)}, u32[]{:S(2)}, u32[]{:S(2)}) async-start(bf16[16,32,256]{2,1,0:T(8,128)(2,1)} %get-tuple-element.49), calls=%async_computation.3 | async-start | bytes 524288 | tf_op jit(solution)/shard_map/all_to_all | solution.py:340
  95.9 10.1 %collective-permute-start.6 = (bf16[128,256]{1,0:T(8,128)(2,1)S(1)}, bf16[128,256]{1,0:T(8,128)(2,1)S(1)}, u32[]{:S(2)}, u32[]{:S(2)}) collective-permute-start(bf16[128,256]{1,0:T(8,128)(2,1)S(1)} %get-tuple-element.54.own), channel_id=1, source_target_pairs={{0,192},{32,224},{64,128},{96,160},{128,64},{160,96},{192,0},{224,... | collective-permute-start | bytes 196616 | tf_op jit(solution)/shard_map/ppermute | solution.py:348
  99.0 7.6 %collective-permute-start.5 = (bf16[128,256]{1,0:T(8,128)(2,1)S(1)}, bf16[128,256]{1,0:T(8,128)(2,1)S(1)}, u32[]{:S(2)}, u32[]{:S(2)}) collective-permute-start(bf16[128,256]{1,0:T(8,128)(2,1)S(1)} %get-tuple-element.54.own), channel_id=1, source_target_pairs={{0,128},{32,160},{64,192},{96,224},{128,0},{160,32},{192,64},{224,... | collective-permute-start | bytes 196616 | tf_op jit(solution)/shard_map/ppermute | solution.py:348
  101.1 7.1 %collective-permute-start.4 = (bf16[128,256]{1,0:T(8,128)(2,1)S(1)}, bf16[128,256]{1,0:T(8,128)(2,1)S(1)}, u32[]{:S(2)}, u32[]{:S(2)}) collective-permute-start(bf16[128,256]{1,0:T(8,128)(2,1)S(1)} %get-tuple-element.54.own), channel_id=1, source_target_pairs={{0,64},{32,96},{64,0},{96,32},{128,192},{160,224},{192,128},{224,1... | collective-permute-start | bytes 196616 | tf_op jit(solution)/shard_map/ppermute | solution.py:348
  108.2 2.9 %copy-start.9 = (f32[512,1024]{1,0:T(8,128)S(1)}, f32[512,1024]{1,0:T(8,128)}, u32[]{:S(2)}) copy-start(f32[512,1024]{1,0:T(8,128)} %copy-done.7) | copy-start | bytes 6291460
  129.3 12.8 %collective-permute-start.8 = (bf16[128,256]{1,0:T(8,128)(2,1)S(1)}, bf16[128,256]{1,0:T(8,128)(2,1)S(1)}, u32[]{:S(2)}, u32[]{:S(2)}) collective-permute-start(bf16[128,256]{1,0:T(8,128)(2,1)S(1)} %shard_map.123.mine), channel_id=1, source_target_pairs={{0,256},{32,288},{64,320},{96,352},{128,384},{160,416},{192,448},{... | collective-permute-start | bytes 196616 | tf_op jit(solution)/shard_map/ppermute | solution.py:327
  134.8 14.6 %all-to-all-start.5 = ((bf16[16,32,256]{2,1,0:T(8,128)(2,1)}), bf16[16,32,256]{2,1,0:T(8,128)(2,1)S(1)}, u32[]{:S(2)}, u32[]{:S(2)}) async-start(bf16[16,32,256]{2,1,0:T(8,128)(2,1)} %bitcast.19), calls=%async_computation.5 | async-start | bytes 524288 | tf_op jit(solution)/shard_map/all_to_all | solution.py:329
  142.6 16.0 %collective-permute-start.9 = (bf16[128,256]{1,0:T(8,128)(2,1)S(1)}, bf16[128,256]{1,0:T(8,128)(2,1)S(1)}, u32[]{:S(2)}, u32[]{:S(2)}) collective-permute-start(bf16[128,256]{1,0:T(8,128)(2,1)S(1)} %shard_map.126.mine), channel_id=1, source_target_pairs={{0,1},{1,0},{2,3},{3,2},{4,5},{5,4},{6,7},{7,6},{8,9},{9,8},{10,11... | collective-permute-start | bytes 196616 | tf_op jit(solution)/shard_map/ppermute | solution.py:331
  150.2 19.3 %collective-permute-start.7 = (bf16[32,256]{1,0:T(8,128)(2,1)S(1)}, bf16[32,256]{1,0:T(8,128)(2,1)S(1)}, u32[]{:S(2)}, u32[]{:S(2)}) collective-permute-start(bf16[32,256]{1,0:T(8,128)(2,1)S(1)} %get-tuple-element.65), channel_id=1, source_target_pairs={{0,1},{1,0},{2,3},{3,2},{4,5},{5,4},{6,7},{7,6},{8,9},{9,8},{10,11... | collective-permute-start | bytes 49160 | tf_op jit(solution)/shard_map/ppermute | solution.py:362
  159.4 18.4 %collective-permute-start.12 = (bf16[128,256]{1,0:T(8,128)(2,1)S(1)}, bf16[128,256]{1,0:T(8,128)(2,1)S(1)}, u32[]{:S(2)}, u32[]{:S(2)}) collective-permute-start(bf16[128,256]{1,0:T(8,128)(2,1)S(1)} %shard_map.127.own), channel_id=1, source_target_pairs={{0,192},{32,224},{64,128},{96,160},{128,64},{160,96},{192,0},{224,... | collective-permute-start | bytes 196616 | tf_op jit(solution)/shard_map/ppermute | solution.py:366
  163.1 14.8 %collective-permute-start.11 = (bf16[128,256]{1,0:T(8,128)(2,1)S(1)}, bf16[128,256]{1,0:T(8,128)(2,1)S(1)}, u32[]{:S(2)}, u32[]{:S(2)}) collective-permute-start(bf16[128,256]{1,0:T(8,128)(2,1)S(1)} %shard_map.127.own), channel_id=1, source_target_pairs={{0,128},{32,160},{64,192},{96,224},{128,0},{160,32},{192,64},{224,... | collective-permute-start | bytes 196616 | tf_op jit(solution)/shard_map/ppermute | solution.py:366
  165.0 12.8 %collective-permute-start.10 = (bf16[128,256]{1,0:T(8,128)(2,1)S(1)}, bf16[128,256]{1,0:T(8,128)(2,1)S(1)}, u32[]{:S(2)}, u32[]{:S(2)}) collective-permute-start(bf16[128,256]{1,0:T(8,128)(2,1)S(1)} %shard_map.127.own), channel_id=1, source_target_pairs={{0,64},{32,96},{64,0},{96,32},{128,192},{160,224},{192,128},{224,1... | collective-permute-start | bytes 196616 | tf_op jit(solution)/shard_map/ppermute | solution.py:366
  170.9 14.5 %all-to-all-start.6 = ((bf16[16,32,384]{2,1,0:T(8,128)(2,1)}), bf16[16,32,384]{2,1,0:T(8,128)(2,1)S(1)}, u32[]{:S(2)}, u32[]{:S(2)}) async-start(bf16[16,32,384]{2,1,0:T(8,128)(2,1)} %shard_map.125), calls=%async_computation.6 | async-start | bytes 786432 | tf_op jit(solution)/shard_map/all_to_all | solution.py:370

commit v5 on v4

--- a/solution.py
+++ b/solution.py
@@ -17,11 +17,25 @@
 ROW_PAIR = 256
 TILE_ROWS = 256
 
-C_COUNTS, C_SHARE, C_PAIR, C_ROW, C_COL, C_ROW_LAST, C_COL_LAST, C_PACK, C_QUAD, C_OUT = 5, 20, 20, 1, 20, 1, 20, 20, 20, 1
+C_FIRST, C_SAME, C_PAIR, C_ROW, C_COL, C_ROW_LAST, C_COL_LAST, C_PACK, C_QUAD, C_OUT = 5, 20, 20, 1, 20, 1, 20, 20, 20, 1
 
 CORE_PAIRS = [[2 * z, 2 * z + 1] for z in range(8)]
 Z_QUADS = [[2 * (4 * h + k) + core for k in range(4)] for h in range(2) for core in range(2)]
-FAR_Z = [(i, i ^ 8) for i in range(16)]
+
+
+def far_pairs():
+    def place(z, core):
+        return 2 * (2 * (z % 8) + core) + z // 8
+
+    pairs = []
+    for z in range(16):
+        up, down = (z + 4) % 16, (z - 4) % 16
+        first = z // 4 % 2 == 0
+        pairs += [(place(z, 0), place(up if first else down, 0)), (place(z, 1), place(down if first else up, 1))]
+    return sorted(pairs)
+
+
+FAR_Z = far_pairs()
 IN_QUAD = [[(i, i ^ (2 * k)) for i in range(16)] for k in range(1, 4)]
 Y_SWAP = [(i, i ^ 1) for i in range(16)]
 DIM_SWAP = [(0, 1), (1, 0)]
@@ -70,7 +84,7 @@
     return ref[pl.ds(pl.multiple_of(index * size, size), size), :]
 
 
-def counts_kernel(at, counts, row_marg, col_marg, weight, target):
+def count_terms(at, counts, row_marg, col_marg, weight, target):
     marg = row_marg[...]
     high, low = to_f32(marg >> 10), to_f32(marg & 1023)
     high, low = (jnp.sum(jnp.sum(m, axis=0, keepdims=True), axis=1, keepdims=True) for m in (high, low))
@@ -88,7 +102,7 @@
 
 
 def share_kernel(at, got, out):
-    out[...] = jnp.broadcast_to(got[:COL_PART, :][None], out.shape)
+    out[...] = jnp.broadcast_to(got[...][None], out.shape)
 
 
 def tile_terms(at, rows, cols, weight, target, kept, given, row_term, row_was, col_was, col_sum):
@@ -129,23 +143,27 @@
     there,
     col_emb,
     col_other,
-    weight,
-    target,
+    counts,
+    row_marg,
+    col_marg,
     kept,
     given,
     row_term,
     row_was,
     col_was,
+    weight,
+    target,
     col_sum,
     rows,
     cols,
 ):
     side, y = at[AT_DIM], at[AT_Y]
     rows[:, :HALF_D] = block_at(row_emb, side, HALF_ROWS)
-    rows[pl.ds(pl.multiple_of(y * ROW_PAIR, ROW_PAIR), ROW_PAIR), HALF_D:] = got[COL_PART:, :]
+    rows[pl.ds(pl.multiple_of(y * ROW_PAIR, ROW_PAIR), ROW_PAIR), HALF_D:] = got[...]
     rows[pl.ds(pl.multiple_of((1 - y) * ROW_PAIR, ROW_PAIR), ROW_PAIR), HALF_D:] = there[...]
     cols[:, :HALF_D] = col_emb[...]
     cols[:, HALF_D:] = col_other[...]
+    count_terms(at, counts, row_marg, col_marg, weight, target)
     tile_terms(at, rows, cols, weight, target, kept, given, row_term, row_was, col_was, col_sum)
 
 
@@ -163,7 +181,9 @@
 
 
 def pair_kernel(at, mine, theirs, both):
-    both[...] = (to_f32(mine[...]) + to_f32(theirs[...])).astype(jnp.bfloat16)
+    block = to_f32(theirs[...])
+    block = jnp.where(at[AT_CORE] == 1, swap_halves(block), block)
+    both[...] = (to_f32(mine[...]) + block).astype(jnp.bfloat16)
 
 
 def row_kernel(at, parts, acc, rows, emb_out, acc_out):
@@ -268,29 +288,14 @@
     def rows_at(block, start, size):
         return lax.dynamic_slice_in_dim(block, start, size, 0)
 
-    sent = jnp.concatenate(
-        [
-            rows_at(col_emb, col_part * COL_PART, COL_PART),
-            rows_at(row_emb, (1 - d) * HALF_ROWS + y * ROW_PAIR, ROW_PAIR),
-        ]
+    col_got = lax.ppermute(rows_at(col_emb, col_part * COL_PART, COL_PART), "dim", DIM_SWAP)
+    row_got = lax.ppermute(
+        rows_at(row_emb, (1 - d) * HALF_ROWS + y * ROW_PAIR, ROW_PAIR), "dim", DIM_SWAP
     )
-    got = lax.ppermute(sent, "dim", DIM_SWAP)
-
-    weight, target = on_device(
-        counts_kernel,
-        at,
-        (counts[0, 0], row_marg, col_marg),
-        (f32(HALF_ROWS, SIDE), f32(HALF_ROWS, SIDE)),
-        C_COUNTS,
-        16,
-    )
-    there = lax.ppermute(got[COL_PART:], "col", Y_SWAP)
-    (shared,) = on_device(share_kernel, at, (got,), (bf16(4, COL_PART, HALF_D),), 1)
+    (shared,) = on_device(share_kernel, at, (col_got,), (bf16(4, COL_PART, HALF_D),), 1)
     col_other = lax.all_to_all(shared, "row", 0, 0, axis_index_groups=Z_QUADS)
-    (there,) = on_device(
-        same_kernel, at, (there,), (bf16(ROW_PAIR, HALF_D),), C_SHARE
-    )
-    there, col_other = lax.optimization_barrier((there, col_other))
+    (row_got,) = on_device(same_kernel, at, (row_got,), (bf16(ROW_PAIR, HALF_D),), C_SAME)
+    there = lax.ppermute(row_got, "col", Y_SWAP)
     col_other = lax.all_gather(col_other, "row", tiled=True, axis_index_groups=CORE_PAIRS)
     col_other = col_other.reshape(SIDE, HALF_D)
 
@@ -299,11 +304,11 @@
     for step in range(STEPS):
         last = step == STEPS - 1
         if step == 0:
-            kept, given, row_term, row_was, col_was = on_device(
+            kept, given, row_term, row_was, col_was, weight, target = on_device(
                 first_tile_kernel,
                 at,
-                (row_emb, got, there, col_emb, col_other, weight, target),
-                terms,
+                (row_emb, row_got, there, col_emb, col_other, counts[0, 0], row_marg, col_marg),
+                terms + (f32(HALF_ROWS, SIDE),) * 2,
                 3,
                 16,
                 [col_sum, pltpu.VMEM((HALF_ROWS, WIDTH), jnp.bfloat16), pltpu.VMEM((SIDE, WIDTH), jnp.bfloat16)],
@@ -324,7 +329,7 @@
         parts = lax.all_to_all(half, "row", 0, 0, axis_index_groups=Z_QUADS)
         (near,) = on_device(near_kernel, at, (parts,), (bf16(COL_PART, WIDTH),), 1)
         row_term, near = lax.optimization_barrier((row_term, near))
-        far = lax.ppermute(near, "row", FAR_Z)
+        far = lax.ppermute(near, ("row", "dim"), FAR_Z)
 
         row_parts = lax.all_to_all(row_term.reshape(N_COL, ROW_PART, WIDTH), "col", 0, 0)
         (near,) = on_device(pair_kernel, at, (near, far), (bf16(COL_PART, WIDTH),), C_PAIR)

time: 188 us -> 184 us (0.979)
  waiting for transfers between devices: 11.5 us -> 24.9 us
  starting transfers between devices: 109 us -> 97.2 us
  local copies, waits for them, and re-layouts: 7.94 us -> 1.76 us
    ppermute x4 -> x5, waiting for transfers between devices: 0.01 us -> 15.6 us  [the longest x1 10.5 us: shards(): lax.ppermute(rows_at(row_emb, (1 - d) * HALF_ROWS + y * ROW_PAIR, ROW_PAI...]
    unnamed x20 -> x22, local copies, waits for them, and re-layouts: 6.24 us -> 0.06 us
    ppermute x4 -> x5, starting transfers between devices: 31.5 us -> 25.7 us  [the longest x1 15.7 us: shards(): lax.ppermute(rows_at(col_emb, col_part * COL_PART, COL_PART), 'dim', DIM_...]
    all_to_all x1, waiting for transfers between devices: 5.36 us -> 0.01 us  [shards(): col_other = lax.all_to_all(shared, 'row', 0, 0, axis_index_groups=Z_QUADS)]
    ppermute x2, starting transfers between devices: 16.6 us -> 11.5 us  [shards(): far = lax.ppermute(near, 'dim', DIM_SWAP)]
    ppermute x2, waiting for transfers between devices: 0.64 us -> 3.82 us  [shards(): far = lax.ppermute(near, 'dim', DIM_SWAP)]
    pallas_call x20 -> x19, Pallas kernels: 21.6 us -> 20.6 us  [on_device(): pl.pallas_call(kernel, in_specs=[pl.BlockSpec(memory_space=pltpu.SMEM)] +...]
  transfers between devices with their start and end apart: 18 -> 19, of which waited for: 5 -> 7; matrix products, arithmetic and copies ran while one was open for 0% -> 1% of each run, Pallas kernels for 6% -> 5%
where the time goes in v5:
time: 184 us; the launch traced here: 182 us
  starting transfers between devices  97.2 us (53%)
  blocking collectives  36.2 us (20%)
  waiting for transfers between devices  24.9 us (14%)
  Pallas kernels  20.6 us (11%)
    all_to_all x2, blocking collectives, shards(): parts = lax.all_to_all(half, 'row', 0, 0, axis_index_groups=Z_QUADS)  25.4 us
    pallas_call x19, Pallas kernels, on_device(): pl.pallas_call(kernel, in_specs=[pl.BlockSpec(memory_space=pltpu.SMEM)] +...  20.6 us
    ppermute x6, starting transfers between devices, shards(): blocks = [cols] + [lax.ppermute(cols, 'row', swap) for swap in IN_QUAD]  20.2 us
    ppermute x1, starting transfers between devices, shards(): lax.ppermute(rows_at(col_emb, col_part * COL_PART, COL_PART), 'dim', DIM_...  15.7 us
    all_to_all x2, starting transfers between devices, shards(): lax.all_to_all(row_term.reshape(N_COL, ROW_PART, WIDTH), 'col', 0, 0)  14.6 us
    ppermute x2, starting transfers between devices, shards(): far = lax.ppermute(near, 'dim', DIM_SWAP)  11.5 us
    ppermute x1, waiting for transfers between devices, shards(): lax.ppermute(rows_at(row_emb, (1 - d) * HALF_ROWS + y * ROW_PAIR, ROW_PAI...  10.5 us
    ppermute x1, starting transfers between devices, shards(): rows_far = lax.ppermute(sent, 'dim', DIM_SWAP)  7.38 us
  transfers between devices with their start and end apart: 19, of which 7 were waited for; matrix products, arithmetic and copies ran while one was open for 1% of the time, Pallas kernels for 5%

profile of v5, /device:TPU:8, one launch (start us, length us, event | category | flops | bytes accessed | tf_op | source)
XLA Modules:
  0.0 182.5 jit_solution(13875120884055626034)
XLA Ops:
  1.4 15.7 %collective-permute-start.2 = (bf16[128,128]{1,0:T(8,128)(2,1)S(1)}, bf16[128,128]{1,0:T(8,128)(2,1)S(1)}, u32[]{:S(2)}, u32[]{:S(2)}) collective-permute-start(bf16[128,128]{1,0:T(8,128)(2,1)S(1)} %dynamic-slice_bitcast_fusion.1), channel_id=1, source_target_pairs={{0,1},{1,0},{2,3},{3,2},{4,5},{5,4},{6,7},{7,6},{8,9},{9,8},{10,11... | collective-permute-start | bytes 98312 | tf_op jit(solution)/shard_map/ppermute | solution.py:291
  21.9 3.3 %all-to-all-start = ((bf16[4,128,128]{2,1,0:T(8,128)(2,1)}), bf16[4,128,128]{2,1,0:T(8,128)(2,1)S(1)}, u32[]{:S(2)}, u32[]{:S(2)}) async-start(bf16[4,128,128]{2,1,0:T(8,128)(2,1)} %shard_map.112), calls=%async_computation | async-start | bytes 262144 | tf_op jit(solution)/shard_map/all_to_all | solution.py:296
  25.3 10.5 %collective-permute-done.block = bf16[256,128]{1,0:T(8,128)(2,1)S(1)} collective-permute-done((bf16[256,128]{1,0:T(8,128)(2,1)S(1)}, bf16[256,128]{1,0:T(8,128)(2,1)S(1)}, u32[]{:S(2)}, u32[]{:S(2)}) %collective-permute-start) | collective-permute-done | bytes 65568 | tf_op jit(solution)/shard_map/ppermute | solution.py:292
  36.3 2.0 %collective-permute-start.1 = (bf16[256,128]{1,0:T(8,128)(2,1)S(1)}, bf16[256,128]{1,0:T(8,128)(2,1)S(1)}, u32[]{:S(2)}, u32[]{:S(2)}) collective-permute-start(bf16[256,128]{1,0:T(8,128)(2,1)S(1)} %shard_map.111.got), channel_id=1, source_target_pairs={{0,2},{2,0},{4,6},{6,4},{8,10},{10,8},{12,14},{14,12},{16,18},{18,... | collective-permute-start | bytes 196616 | tf_op jit(solution)/shard_map/ppermute | solution.py:298
  38.4 2.0 %all_gather.21 = bf16[8,128,128]{2,1,0:T(8,128)(2,1)S(1)} all-gather(bf16[4,128,128]{2,1,0:T(8,128)(2,1)S(1)} %all-to-all-done), channel_id=1, replica_groups={{0,32},{64,96},{128,160},{192,224},{256,288},{320,352},{384,416},{448,4..., dimensions={0}, use_global_device_ids=true | all-gather | bytes 393216 | tf_op jit(solution)/shard_map/all_gather | solution.py:299
  40.4 2.1 %collective-permute-done.1.there = bf16[256,128]{1,0:T(8,128)(2,1)S(1)} collective-permute-done((bf16[256,128]{1,0:T(8,128)(2,1)S(1)}, bf16[256,128]{1,0:T(8,128)(2,1)S(1)}, u32[]{:S(2)}, u32[]{:S(2)}) %collective-permute-start.1) | collective-permute-done | bytes 65568 | tf_op jit(solution)/shard_map/ppermute | solution.py:298
  42.5 3.7 %shard_map.113 = (bf16[512,256]{1,0:T(8,128)(2,1)S(1)}, bf16[512,256]{1,0:T(8,128)(2,1)S(1)}, bf16[512,256]{1,0:T(8,128)(2,1)}, bf16[32,256]{1,0:T(8,128)(2,1)S(...) custom-call(s32[7]{0:T(128)S(1)} %stack.31.at, ...), custom_call_target="tpu_custom_call" | custom-call | flops 3000000000 | bytes 262144 | tf_op jit(solution)/shard_map/pallas_call | solution.py:261
  46.2 2.2 %all-gather = bf16[1024,256]{1,0:T(8,128)(2,1)S(1)} all-gather(bf16[512,256]{1,0:T(8,128)(2,1)S(1)} %get-tuple-element.40), channel_id=2, replica_groups={{0,32},{64,96},{128,160},{192,224},{256,288},{320,352},{384,416},{448,4..., dimensions={0}, use_global_device_ids=true | all-gather | bytes 786432 | tf_op jit(solution)/shard_map/all_gather | solution.py:327
  49.0 13.2 %all_to_all.35.parts = bf16[4,128,256]{2,1,0:T(8,128)(2,1)S(1)} all-to-all(bf16[4,128,256]{2,1,0:T(8,128)(2,1)S(1)} %shard_map.114), channel_id=1, replica_groups={{0,64,128,192},{32,96,160,224},{256,320,384,448},{288,352,416,480},{1,6..., dimensions={0} | all-to-all | bytes 524288 | tf_op jit(solution)/shard_map/all_to_all | solution.py:329
  62.8 2.0 %collective-permute-start.3 = (bf16[128,256]{1,0:T(8,128)(2,1)S(1)}, bf16[128,256]{1,0:T(8,128)(2,1)S(1)}, u32[]{:S(2)}, u32[]{:S(2)}) collective-permute-start(bf16[128,256]{1,0:T(8,128)(2,1)S(1)} %shard_map.115.mine), channel_id=1, source_target_pairs={{0,256},{1,257},{32,289},{33,288},{64,320},{65,321},{96,353},{97,3... | collective-permute-start | bytes 196616 | tf_op jit(solution)/shard_map/ppermute | solution.py:332
  64.8 7.4 %all-to-all-start.2 = ((bf16[16,32,256]{2,1,0:T(8,128)(2,1)}), bf16[16,32,256]{2,1,0:T(8,128)(2,1)S(1)}, u32[]{:S(2)}, u32[]{:S(2)}) async-start(bf16[16,32,256]{2,1,0:T(8,128)(2,1)} %bitcast.15), calls=%async_computation.2 | async-start | bytes 524288 | tf_op jit(solution)/shard_map/all_to_all | solution.py:334
  72.2 2.4 %collective-permute-done.3.theirs = bf16[128,256]{1,0:T(8,128)(2,1)S(1)} collective-permute-done((bf16[128,256]{1,0:T(8,128)(2,1)S(1)}, bf16[128,256]{1,0:T(8,128)(2,1)S(1)}, u32[]{:S(2)}, u32[]{:S(2)}) %collective-permute-start.3) | collective-permute-done | bytes 65568 | tf_op jit(solution)/shard_map/ppermute | solution.py:332
  75.2 4.4 %collective-permute-start.4 = (bf16[128,256]{1,0:T(8,128)(2,1)S(1)}, bf16[128,256]{1,0:T(8,128)(2,1)S(1)}, u32[]{:S(2)}, u32[]{:S(2)}) collective-permute-start(bf16[128,256]{1,0:T(8,128)(2,1)S(1)} %shard_map.117.mine), channel_id=1, source_target_pairs={{0,1},{1,0},{2,3},{3,2},{4,5},{5,4},{6,7},{7,6},{8,9},{9,8},{10,11... | collective-permute-start | bytes 196616 | tf_op jit(solution)/shard_map/ppermute | solution.py:336
  81.0 7.2 %all-to-all-start.3 = ((bf16[16,32,256]{2,1,0:T(8,128)(2,1)}), bf16[16,32,256]{2,1,0:T(8,128)(2,1)S(1)}, u32[]{:S(2)}, u32[]{:S(2)}) async-start(bf16[16,32,256]{2,1,0:T(8,128)(2,1)} %get-tuple-element.43), calls=%async_computation.3 | async-start | bytes 524288 | tf_op jit(solution)/shard_map/all_to_all | solution.py:345
  88.2 3.8 %collective-permute-done.4.theirs = bf16[128,256]{1,0:T(8,128)(2,1)S(1)} collective-permute-done((bf16[128,256]{1,0:T(8,128)(2,1)S(1)}, bf16[128,256]{1,0:T(8,128)(2,1)S(1)}, u32[]{:S(2)}, u32[]{:S(2)}) %collective-permute-start.4) | collective-permute-done | bytes 65568 | tf_op jit(solution)/shard_map/ppermute | solution.py:336
  92.8 1.9 %collective-permute-start.7 = (bf16[128,256]{1,0:T(8,128)(2,1)S(1)}, bf16[128,256]{1,0:T(8,128)(2,1)S(1)}, u32[]{:S(2)}, u32[]{:S(2)}) collective-permute-start(bf16[128,256]{1,0:T(8,128)(2,1)S(1)} %get-tuple-element.48.own), channel_id=1, source_target_pairs={{0,192},{32,224},{64,128},{96,160},{128,64},{160,96},{192,0},{224,... | collective-permute-start | bytes 196616 | tf_op jit(solution)/shard_map/ppermute | solution.py:353
  94.7 2.0 %collective-permute-start.6 = (bf16[128,256]{1,0:T(8,128)(2,1)S(1)}, bf16[128,256]{1,0:T(8,128)(2,1)S(1)}, u32[]{:S(2)}, u32[]{:S(2)}) collective-permute-start(bf16[128,256]{1,0:T(8,128)(2,1)S(1)} %get-tuple-element.48.own), channel_id=1, source_target_pairs={{0,128},{32,160},{64,192},{96,224},{128,0},{160,32},{192,64},{224,... | collective-permute-start | bytes 196616 | tf_op jit(solution)/shard_map/ppermute | solution.py:353
  96.7 6.2 %collective-permute-start.5 = (bf16[128,256]{1,0:T(8,128)(2,1)S(1)}, bf16[128,256]{1,0:T(8,128)(2,1)S(1)}, u32[]{:S(2)}, u32[]{:S(2)}) collective-permute-start(bf16[128,256]{1,0:T(8,128)(2,1)S(1)} %get-tuple-element.48.own), channel_id=1, source_target_pairs={{0,64},{32,96},{64,0},{96,32},{128,192},{160,224},{192,128},{224,1... | collective-permute-start | bytes 196616 | tf_op jit(solution)/shard_map/ppermute | solution.py:353
  102.9 2.2 %collective-permute-done.5.one = bf16[128,256]{1,0:T(8,128)(2,1)S(1)} collective-permute-done((bf16[128,256]{1,0:T(8,128)(2,1)S(1)}, bf16[128,256]{1,0:T(8,128)(2,1)S(1)}, u32[]{:S(2)}, u32[]{:S(2)}) %collective-permute-start.5) | collective-permute-done | bytes 65568 | tf_op jit(solution)/shard_map/ppermute | solution.py:353
  105.7 2.3 %all_gather.24 = bf16[8,128,256]{2,1,0:T(8,128)(2,1)S(1)} all-gather(bf16[4,128,256]{2,1,0:T(8,128)(2,1)S(1)} %shard_map.119), channel_id=1, replica_groups={{0,32},{64,96},{128,160},{192,224},{256,288},{320,352},{384,416},{448,4..., dimensions={0}, use_global_device_ids=true | all-gather | bytes 786432 | tf_op jit(solution)/shard_map/all_gather | solution.py:356
  108.0 2.5 %shard_map.120 = (bf16[512,256]{1,0:T(8,128)(2,1)S(1)}, bf16[512,256]{1,0:T(8,128)(2,1)S(1)}, bf16[512,256]{1,0:T(8,128)(2,1)}, bf16[32,256]{1,0:T(8,128)(2,1)S(1)}, bf16[128,256]{1,0:T(8,128)(2,1)S(1)}) custom-call(s32[7]{0:T(128)S(1)} %stack.31.at, bf16[512,256]{1,0:T(8,128)(2,1)S(1)} %bitcast.31, bf16[1024,256]{1,0:T(8,128)(2,1)S(1)} %bitcast.25, ...), custom_call_target="tpu_custom_call" | custom-call | flops 3000000000 | bytes 262144 | tf_op jit(solution)/shard_map/pallas_call | solution.py:261
  110.5 2.2 %all-gather.1 = bf16[1024,256]{1,0:T(8,128)(2,1)S(1)} all-gather(bf16[512,256]{1,0:T(8,128)(2,1)S(1)} %get-tuple-element.56), channel_id=3, replica_groups={{0,32},{64,96},{128,160},{192,224},{256,288},{320,352},{384,416},{448,4..., dimensions={0}, use_global_device_ids=true | all-gather | bytes 786432 | tf_op jit(solution)/shard_map/all_gather | solution.py:327
  113.3 12.3 %all_to_all.36.parts = bf16[4,128,256]{2,1,0:T(8,128)(2,1)S(1)} all-to-all(bf16[4,128,256]{2,1,0:T(8,128)(2,1)S(1)} %shard_map.121), channel_id=1, replica_groups={{0,64,128,192},{32,96,160,224},{256,320,384,448},{288,352,416,480},{1,6..., dimensions={0} | all-to-all | bytes 524288 | tf_op jit(solution)/shard_map/all_to_all | solution.py:329
  126.1 4.0 %collective-permute-start.9 = (bf16[128,256]{1,0:T(8,128)(2,1)S(1)}, bf16[128,256]{1,0:T(8,128)(2,1)S(1)}, u32[]{:S(2)}, u32[]{:S(2)}) collective-permute-start(bf16[128,256]{1,0:T(8,128)(2,1)S(1)} %shard_map.122.mine), channel_id=1, source_target_pairs={{0,256},{1,257},{32,289},{33,288},{64,320},{65,321},{96,353},{97,3... | collective-permute-start | bytes 196616 | tf_op jit(solution)/shard_map/ppermute | solution.py:332
  130.1 7.2 %all-to-all-start.5 = ((bf16[16,32,256]{2,1,0:T(8,128)(2,1)}), bf16[16,32,256]{2,1,0:T(8,128)(2,1)S(1)}, u32[]{:S(2)}, u32[]{:S(2)}) async-start(bf16[16,32,256]{2,1,0:T(8,128)(2,1)} %bitcast.19), calls=%async_computation.5 | async-start | bytes 524288 | tf_op jit(solution)/shard_map/all_to_all | solution.py:334
  138.5 7.2 %collective-permute-start.10 = (bf16[128,256]{1,0:T(8,128)(2,1)S(1)}, bf16[128,256]{1,0:T(8,128)(2,1)S(1)}, u32[]{:S(2)}, u32[]{:S(2)}) collective-permute-start(bf16[128,256]{1,0:T(8,128)(2,1)S(1)} %shard_map.125.mine), channel_id=1, source_target_pairs={{0,1},{1,0},{2,3},{3,2},{4,5},{5,4},{6,7},{7,6},{8,9},{9,8},{10,11... | collective-permute-start | bytes 196616 | tf_op jit(solution)/shard_map/ppermute | solution.py:336
  146.5 7.4 %collective-permute-start.8 = (bf16[32,256]{1,0:T(8,128)(2,1)S(1)}, bf16[32,256]{1,0:T(8,128)(2,1)S(1)}, u32[]{:S(2)}, u32[]{:S(2)}) collective-permute-start(bf16[32,256]{1,0:T(8,128)(2,1)S(1)} %get-tuple-element.61), channel_id=1, source_target_pairs={{0,1},{1,0},{2,3},{3,2},{4,5},{5,4},{6,7},{7,6},{8,9},{9,8},{10,11... | collective-permute-start | bytes 49160 | tf_op jit(solution)/shard_map/ppermute | solution.py:367
  154.7 4.1 %collective-permute-start.13 = (bf16[128,256]{1,0:T(8,128)(2,1)S(1)}, bf16[128,256]{1,0:T(8,128)(2,1)S(1)}, u32[]{:S(2)}, u32[]{:S(2)}) collective-permute-start(bf16[128,256]{1,0:T(8,128)(2,1)S(1)} %shard_map.126.own), channel_id=1, source_target_pairs={{0,192},{32,224},{64,128},{96,160},{128,64},{160,96},{192,0},{224,... | collective-permute-start | bytes 196616 | tf_op jit(solution)/shard_map/ppermute | solution.py:371
  160.7 4.1 %collective-permute-start.11 = (bf16[128,256]{1,0:T(8,128)(2,1)S(1)}, bf16[128,256]{1,0:T(8,128)(2,1)S(1)}, u32[]{:S(2)}, u32[]{:S(2)}) collective-permute-start(bf16[128,256]{1,0:T(8,128)(2,1)S(1)} %shard_map.126.own), channel_id=1, source_target_pairs={{0,64},{32,96},{64,0},{96,32},{128,192},{160,224},{192,128},{224,1... | collective-permute-start | bytes 196616 | tf_op jit(solution)/shard_map/ppermute | solution.py:371
  166.1 7.2 %all-to-all-start.6 = ((bf16[16,32,384]{2,1,0:T(8,128)(2,1)}), bf16[16,32,384]{2,1,0:T(8,128)(2,1)S(1)}, u32[]{:S(2)}, u32[]{:S(2)}) async-start(bf16[16,32,384]{2,1,0:T(8,128)(2,1)} %shard_map.124), calls=%async_computation.6 | async-start | bytes 786432 | tf_op jit(solution)/shard_map/all_to_all | solution.py:375
  174.0 2.2 %all_gather.27 = bf16[8,128,256]{2,1,0:T(8,128)(2,1)S(1)} all-gather(bf16[4,128,256]{2,1,0:T(8,128)(2,1)S(1)} %shard_map.127), channel_id=1, replica_groups={{0,32},{64,96},{128,160},{192,224},{256,288},{320,352},{384,416},{448,4..., dimensions={0}, use_global_device_ids=true | all-gather | bytes 786432 | tf_op jit(solution)/shard_map/all_gather | solution.py:377
  177.7 3.3 %all-to-all-done.6 = bf16[16,32,384]{2,1,0:T(8,128)(2,1)S(1)} async-done(((bf16[16,32,384]{2,1,0:T(8,128)(2,1)}), bf16[16,32,384]{2,1,0:T(8,128)(2,1)S(1)}, u32[]{:S(2)}, u32[]{:S(2)}) %all-to-all-start.6) | async-done | bytes 393248 | tf_op jit(solution)/shard_map/all_to_all | solution.py:375
  (57 shorter events, 20.6 us)
Async XLA Ops:
  1.4 19.2 %collective-permute-start.2 = (bf16[128,128]{1,0:T(8,128)(2,1)S(1)}, bf16[128,128]{1,0:T(8,128)(2,1)S(1)}, u32[]{:S(2)}, u32[]{:S(2)}) collective-permute-start(bf16[128,128]{1,0:T(8,128)(2,1)S(1)} %dynamic-slice_bitcast_fusion.1), channel_id=1, source_target_pairs={{0,1},{1,0},{2,3},{3,2},{4,5},{5,4},{6,7},{7,6},{8,9},{9,8},{10,11... | collective-permute-start | bytes 98312 | tf_op jit(solution)/shard_map/ppermute | solution.py:291
  18.0 17.8 %collective-permute-start = (bf16[256,128]{1,0:T(8,128)(2,1)S(1)}, bf16[256,128]{1,0:T(8,128)(2,1)S(1)}, u32[]{:S(2)}, u32[]{:S(2)}) collective-permute-start(bf16[256,128]{1,0:T(8,128)(2,1)S(1)} %dynamic-slice_bitcast_fusion), channel_id=1, source_target_pairs={{0,1},{1,0},{2,3},{3,2},{4,5},{5,4},{6,7},{7,6},{8,9},{9,8},{10,11... | collective-permute-start | bytes 196616 | tf_op jit(solution)/shard_map/ppermute | solution.py:292
  21.9 16.5 %all-to-all-start = ((bf16[4,128,128]{2,1,0:T(8,128)(2,1)}), bf16[4,128,128]{2,1,0:T(8,128)(2,1)S(1)}, u32[]{:S(2)}, u32[]{:S(2)}) async-start(bf16[4,128,128]{2,1,0:T(8,128)(2,1)} %shard_map.112), calls=%async_computation | async-start | bytes 262144 | tf_op jit(solution)/shard_map/all_to_all | solution.py:296
  25.2 17.3 %copy-start = (bf16[1,1024,128]{2,1,0:T(8,128)(2,1)S(1)}, bf16[1,1024,128]{2,1,0:T(8,128)(2,1)}, u32[]{:S(2)}) copy-start(bf16[1,1024,128]{2,1,0:T(8,128)(2,1)} %param.8) | copy-start | bytes 786436
  25.2 17.3 %copy-start.1 = (bf16[1,1024,128]{2,1,0:T(8,128)(2,1)S(1)}, bf16[1,1024,128]{2,1,0:T(8,128)(2,1)}, u32[]{:S(2)}) copy-start(bf16[1,1024,128]{2,1,0:T(8,128)(2,1)} %param.9) | copy-start | bytes 786436
  25.3 17.2 %copy-start.2 = (s32[1,1,512,1024]{3,2,1,0:T(8,128)S(1)}, s32[1,1,512,1024]{3,2,1,0:T(8,128)}, u32[]{:S(2)}) copy-start(s32[1,1,512,1024]{3,2,1,0:T(8,128)} %param.12) | copy-start | bytes 6291460
  25.3 17.2 %copy-start.3 = (s32[16,1024]{1,0:T(8,128)S(1)}, s32[16,1024]{1,0:T(8,128)}, u32[]{:S(2)}) copy-start(s32[16,1024]{1,0:T(8,128)} %row_marg.1) | copy-start | bytes 196612
  25.3 17.2 %copy-start.4 = (s32[16,1024]{1,0:T(8,128)S(1)}, s32[16,1024]{1,0:T(8,128)}, u32[]{:S(2)}) copy-start(s32[16,1024]{1,0:T(8,128)} %col_marg.1) | copy-start | bytes 196612
  36.3 6.2 %collective-permute-start.1 = (bf16[256,128]{1,0:T(8,128)(2,1)S(1)}, bf16[256,128]{1,0:T(8,128)(2,1)S(1)}, u32[]{:S(2)}, u32[]{:S(2)}) collective-permute-start(bf16[256,128]{1,0:T(8,128)(2,1)S(1)} %shard_map.111.got), channel_id=1, source_target_pairs={{0,2},{2,0},{4,6},{6,4},{8,10},{10,8},{12,14},{14,12},{16,18},{18,... | collective-permute-start | bytes 196616 | tf_op jit(solution)/shard_map/ppermute | solution.py:298
  46.2 2.8 %copy-start.7 = (f32[512,1024]{1,0:T(8,128)}, f32[512,1024]{1,0:T(8,128)S(1)}, u32[]{:S(2)}) copy-start(f32[512,1024]{1,0:T(8,128)S(1)} %get-tuple-element.52.weight) | copy-start | bytes 6291460
  46.2 2.8 %copy-start.9 = (f32[512,1024]{1,0:T(8,128)}, f32[512,1024]{1,0:T(8,128)S(1)}, u32[]{:S(2)}) copy-start(f32[512,1024]{1,0:T(8,128)S(1)} %get-tuple-element.53.target) | copy-start | bytes 6291460
  62.8 11.8 %collective-permute-start.3 = (bf16[128,256]{1,0:T(8,128)(2,1)S(1)}, bf16[128,256]{1,0:T(8,128)(2,1)S(1)}, u32[]{:S(2)}, u32[]{:S(2)}) collective-permute-start(bf16[128,256]{1,0:T(8,128)(2,1)S(1)} %shard_map.115.mine), channel_id=1, source_target_pairs={{0,256},{1,257},{32,289},{33,288},{64,320},{65,321},{96,353},{97,3... | collective-permute-start | bytes 196616 | tf_op jit(solution)/shard_map/ppermute | solution.py:332
  64.8 14.7 %all-to-all-start.2 = ((bf16[16,32,256]{2,1,0:T(8,128)(2,1)}), bf16[16,32,256]{2,1,0:T(8,128)(2,1)S(1)}, u32[]{:S(2)}, u32[]{:S(2)}) async-start(bf16[16,32,256]{2,1,0:T(8,128)(2,1)} %bitcast.15), calls=%async_computation.2 | async-start | bytes 524288 | tf_op jit(solution)/shard_map/all_to_all | solution.py:334
  72.2 7.3 %copy-start.5 = (f32[1,1024]{1,0:T(1,128)S(1)}, f32[1,1024]{1,0:T(1,128)}, u32[]{:S(2)}) copy-start(f32[1,1024]{1,0:T(1,128)} %acc.2) | copy-start | bytes 12292
  75.2 16.9 %collective-permute-start.4 = (bf16[128,256]{1,0:T(8,128)(2,1)S(1)}, bf16[128,256]{1,0:T(8,128)(2,1)S(1)}, u32[]{:S(2)}, u32[]{:S(2)}) collective-permute-start(bf16[128,256]{1,0:T(8,128)(2,1)S(1)} %shard_map.117.mine), channel_id=1, source_target_pairs={{0,1},{1,0},{2,3},{3,2},{4,5},{5,4},{6,7},{7,6},{8,9},{9,8},{10,11... | collective-permute-start | bytes 196616 | tf_op jit(solution)/shard_map/ppermute | solution.py:336
  79.6 12.5 %copy-start.6 = (f32[1,1024]{1,0:T(1,128)S(1)}, f32[1,1024]{1,0:T(1,128)}, u32[]{:S(2)}) copy-start(f32[1,1024]{1,0:T(1,128)} %acc.3) | copy-start | bytes 12292
  81.0 24.1 %all-to-all-start.3 = ((bf16[16,32,256]{2,1,0:T(8,128)(2,1)}), bf16[16,32,256]{2,1,0:T(8,128)(2,1)S(1)}, u32[]{:S(2)}, u32[]{:S(2)}) async-start(bf16[16,32,256]{2,1,0:T(8,128)(2,1)} %get-tuple-element.43), calls=%async_computation.3 | async-start | bytes 524288 | tf_op jit(solution)/shard_map/all_to_all | solution.py:345
  92.8 10.1 %collective-permute-start.7 = (bf16[128,256]{1,0:T(8,128)(2,1)S(1)}, bf16[128,256]{1,0:T(8,128)(2,1)S(1)}, u32[]{:S(2)}, u32[]{:S(2)}) collective-permute-start(bf16[128,256]{1,0:T(8,128)(2,1)S(1)} %get-tuple-element.48.own), channel_id=1, source_target_pairs={{0,192},{32,224},{64,128},{96,160},{128,64},{160,96},{192,0},{224,... | collective-permute-start | bytes 196616 | tf_op jit(solution)/shard_map/ppermute | solution.py:353
  94.7 8.2 %collective-permute-start.6 = (bf16[128,256]{1,0:T(8,128)(2,1)S(1)}, bf16[128,256]{1,0:T(8,128)(2,1)S(1)}, u32[]{:S(2)}, u32[]{:S(2)}) collective-permute-start(bf16[128,256]{1,0:T(8,128)(2,1)S(1)} %get-tuple-element.48.own), channel_id=1, source_target_pairs={{0,128},{32,160},{64,192},{96,224},{128,0},{160,32},{192,64},{224,... | collective-permute-start | bytes 196616 | tf_op jit(solution)/shard_map/ppermute | solution.py:353
  96.7 8.4 %collective-permute-start.5 = (bf16[128,256]{1,0:T(8,128)(2,1)S(1)}, bf16[128,256]{1,0:T(8,128)(2,1)S(1)}, u32[]{:S(2)}, u32[]{:S(2)}) collective-permute-start(bf16[128,256]{1,0:T(8,128)(2,1)S(1)} %get-tuple-element.48.own), channel_id=1, source_target_pairs={{0,64},{32,96},{64,0},{96,32},{128,192},{160,224},{192,128},{224,1... | collective-permute-start | bytes 196616 | tf_op jit(solution)/shard_map/ppermute | solution.py:353
  105.1 2.9 %copy-start.8 = (f32[512,1024]{1,0:T(8,128)S(1)}, f32[512,1024]{1,0:T(8,128)}, u32[]{:S(2)}) copy-start(f32[512,1024]{1,0:T(8,128)} %copy-done.7) | copy-start | bytes 6291460
  105.1 2.9 %copy-start.10 = (f32[512,1024]{1,0:T(8,128)S(1)}, f32[512,1024]{1,0:T(8,128)}, u32[]{:S(2)}) copy-start(f32[512,1024]{1,0:T(8,128)} %copy-done.9) | copy-start | bytes 6291460
  126.1 11.8 %collective-permute-start.9 = (bf16[128,256]{1,0:T(8,128)(2,1)S(1)}, bf16[128,256]{1,0:T(8,128)(2,1)S(1)}, u32[]{:S(2)}, u32[]{:S(2)}) collective-permute-start(bf16[128,256]{1,0:T(8,128)(2,1)S(1)} %shard_map.122.mine), channel_id=1, source_target_pairs={{0,256},{1,257},{32,289},{33,288},{64,320},{65,321},{96,353},{97,3... | collective-permute-start | bytes 196616 | tf_op jit(solution)/shard_map/ppermute | solution.py:332
  130.1 15.6 %all-to-all-start.5 = ((bf16[16,32,256]{2,1,0:T(8,128)(2,1)}), bf16[16,32,256]{2,1,0:T(8,128)(2,1)S(1)}, u32[]{:S(2)}, u32[]{:S(2)}) async-start(bf16[16,32,256]{2,1,0:T(8,128)(2,1)} %bitcast.19), calls=%async_computation.5 | async-start | bytes 524288 | tf_op jit(solution)/shard_map/all_to_all | solution.py:334
  138.5 15.4 %collective-permute-start.10 = (bf16[128,256]{1,0:T(8,128)(2,1)S(1)}, bf16[128,256]{1,0:T(8,128)(2,1)S(1)}, u32[]{:S(2)}, u32[]{:S(2)}) collective-permute-start(bf16[128,256]{1,0:T(8,128)(2,1)S(1)} %shard_map.125.mine), channel_id=1, source_target_pairs={{0,1},{1,0},{2,3},{3,2},{4,5},{5,4},{6,7},{7,6},{8,9},{9,8},{10,11... | collective-permute-start | bytes 196616 | tf_op jit(solution)/shard_map/ppermute | solution.py:336
  146.5 18.3 %collective-permute-start.8 = (bf16[32,256]{1,0:T(8,128)(2,1)S(1)}, bf16[32,256]{1,0:T(8,128)(2,1)S(1)}, u32[]{:S(2)}, u32[]{:S(2)}) collective-permute-start(bf16[32,256]{1,0:T(8,128)(2,1)S(1)} %get-tuple-element.61), channel_id=1, source_target_pairs={{0,1},{1,0},{2,3},{3,2},{4,5},{5,4},{6,7},{7,6},{8,9},{9,8},{10,11... | collective-permute-start | bytes 49160 | tf_op jit(solution)/shard_map/ppermute | solution.py:367
  154.7 18.7 %collective-permute-start.13 = (bf16[128,256]{1,0:T(8,128)(2,1)S(1)}, bf16[128,256]{1,0:T(8,128)(2,1)S(1)}, u32[]{:S(2)}, u32[]{:S(2)}) collective-permute-start(bf16[128,256]{1,0:T(8,128)(2,1)S(1)} %shard_map.126.own), channel_id=1, source_target_pairs={{0,192},{32,224},{64,128},{96,160},{128,64},{160,96},{192,0},{224,... | collective-permute-start | bytes 196616 | tf_op jit(solution)/shard_map/ppermute | solution.py:371
  158.8 14.6 %collective-permute-start.12 = (bf16[128,256]{1,0:T(8,128)(2,1)S(1)}, bf16[128,256]{1,0:T(8,128)(2,1)S(1)}, u32[]{:S(2)}, u32[]{:S(2)}) collective-permute-start(bf16[128,256]{1,0:T(8,128)(2,1)S(1)} %shard_map.126.own), channel_id=1, source_target_pairs={{0,128},{32,160},{64,192},{96,224},{128,0},{160,32},{192,64},{224,... | collective-permute-start | bytes 196616 | tf_op jit(solution)/shard_map/ppermute | solution.py:371
  160.7 12.7 %collective-permute-start.11 = (bf16[128,256]{1,0:T(8,128)(2,1)S(1)}, bf16[128,256]{1,0:T(8,128)(2,1)S(1)}, u32[]{:S(2)}, u32[]{:S(2)}) collective-permute-start(bf16[128,256]{1,0:T(8,128)(2,1)S(1)} %shard_map.126.own), channel_id=1, source_target_pairs={{0,64},{32,96},{64,0},{96,32},{128,192},{160,224},{192,128},{224,1... | collective-permute-start | bytes 196616 | tf_op jit(solution)/shard_map/ppermute | solution.py:371
  166.1 14.8 %all-to-all-start.6 = ((bf16[16,32,384]{2,1,0:T(8,128)(2,1)}), bf16[16,32,384]{2,1,0:T(8,128)(2,1)S(1)}, u32[]{:S(2)}, u32[]{:S(2)}) async-start(bf16[16,32,384]{2,1,0:T(8,128)(2,1)} %shard_map.124), calls=%async_computation.6 | async-start | bytes 786432 | tf_op jit(solution)/shard_map/all_to_all | solution.py:375

commit v6 on v5

--- a/solution.py
+++ b/solution.py
@@ -310,7 +310,7 @@
                 (row_emb, row_got, there, col_emb, col_other, counts[0, 0], row_marg, col_marg),
                 terms + (f32(HALF_ROWS, SIDE),) * 2,
                 3,
-                16,
+                8,
                 [col_sum, pltpu.VMEM((HALF_ROWS, WIDTH), jnp.bfloat16), pltpu.VMEM((SIDE, WIDTH), jnp.bfloat16)],
             )
         else:
@@ -320,7 +320,7 @@
                 (rows, cols, weight, target),
                 terms,
                 3,
-                16,
+                8,
                 [col_sum],
             )
 

time: 184 us -> 184 us (level)
  no operation moved by 1% of the time
where the time goes in v6:
time: 184 us; the launch traced here: 182 us
  starting transfers between devices  97.2 us (53%)
  blocking collectives  36.2 us (20%)
  waiting for transfers between devices  24.9 us (14%)
  Pallas kernels  20.6 us (11%)
    all_to_all x2, blocking collectives, shards(): parts = lax.all_to_all(half, 'row', 0, 0, axis_index_groups=Z_QUADS)  25.4 us
    pallas_call x19, Pallas kernels, on_device(): pl.pallas_call(kernel, in_specs=[pl.BlockSpec(memory_space=pltpu.SMEM)] +...  20.6 us
    ppermute x6, starting transfers between devices, shards(): blocks = [cols] + [lax.ppermute(cols, 'row', swap) for swap in IN_QUAD]  20.2 us
    ppermute x1, starting transfers between devices, shards(): lax.ppermute(rows_at(col_emb, col_part * COL_PART, COL_PART), 'dim', DIM_...  15.7 us
    all_to_all x2, starting transfers between devices, shards(): lax.all_to_all(row_term.reshape(N_COL, ROW_PART, WIDTH), 'col', 0, 0)  14.6 us
    ppermute x2, starting transfers between devices, shards(): far = lax.ppermute(near, 'dim', DIM_SWAP)  11.5 us
    ppermute x1, waiting for transfers between devices, shards(): lax.ppermute(rows_at(row_emb, (1 - d) * HALF_ROWS + y * ROW_PAIR, ROW_PAI...  10.5 us
    ppermute x1, starting transfers between devices, shards(): rows_far = lax.ppermute(sent, 'dim', DIM_SWAP)  7.38 us
  transfers between devices with their start and end apart: 19, of which 7 were waited for; matrix products, arithmetic and copies ran while one was open for 1% of the time, Pallas kernels for 5%

profile of v6, /device:TPU:8, one launch (start us, length us, event | category | flops | bytes accessed | tf_op | source)
XLA Modules:
  0.0 182.5 jit_solution(3570530649548188145)
XLA Ops:
  1.4 15.7 %collective-permute-start.2 = (bf16[128,128]{1,0:T(8,128)(2,1)S(1)}, bf16[128,128]{1,0:T(8,128)(2,1)S(1)}, u32[]{:S(2)}, u32[]{:S(2)}) collective-permute-start(bf16[128,128]{1,0:T(8,128)(2,1)S(1)} %dynamic-slice_bitcast_fusion.1), channel_id=1, source_target_pairs={{0,1},{1,0},{2,3},{3,2},{4,5},{5,4},{6,7},{7,6},{8,9},{9,8},{10,11... | collective-permute-start | bytes 98312 | tf_op jit(solution)/shard_map/ppermute | solution.py:291
  21.9 3.3 %all-to-all-start = ((bf16[4,128,128]{2,1,0:T(8,128)(2,1)}), bf16[4,128,128]{2,1,0:T(8,128)(2,1)S(1)}, u32[]{:S(2)}, u32[]{:S(2)}) async-start(bf16[4,128,128]{2,1,0:T(8,128)(2,1)} %shard_map.112), calls=%async_computation | async-start | bytes 262144 | tf_op jit(solution)/shard_map/all_to_all | solution.py:296
  25.3 10.5 %collective-permute-done.block = bf16[256,128]{1,0:T(8,128)(2,1)S(1)} collective-permute-done((bf16[256,128]{1,0:T(8,128)(2,1)S(1)}, bf16[256,128]{1,0:T(8,128)(2,1)S(1)}, u32[]{:S(2)}, u32[]{:S(2)}) %collective-permute-start) | collective-permute-done | bytes 65568 | tf_op jit(solution)/shard_map/ppermute | solution.py:292
  36.3 2.0 %collective-permute-start.1 = (bf16[256,128]{1,0:T(8,128)(2,1)S(1)}, bf16[256,128]{1,0:T(8,128)(2,1)S(1)}, u32[]{:S(2)}, u32[]{:S(2)}) collective-permute-start(bf16[256,128]{1,0:T(8,128)(2,1)S(1)} %shard_map.111.got), channel_id=1, source_target_pairs={{0,2},{2,0},{4,6},{6,4},{8,10},{10,8},{12,14},{14,12},{16,18},{18,... | collective-permute-start | bytes 196616 | tf_op jit(solution)/shard_map/ppermute | solution.py:298
  38.4 2.0 %all_gather.21 = bf16[8,128,128]{2,1,0:T(8,128)(2,1)S(1)} all-gather(bf16[4,128,128]{2,1,0:T(8,128)(2,1)S(1)} %all-to-all-done), channel_id=1, replica_groups={{0,32},{64,96},{128,160},{192,224},{256,288},{320,352},{384,416},{448,4..., dimensions={0}, use_global_device_ids=true | all-gather | bytes 393216 | tf_op jit(solution)/shard_map/all_gather | solution.py:299
  40.4 2.1 %collective-permute-done.1.there = bf16[256,128]{1,0:T(8,128)(2,1)S(1)} collective-permute-done((bf16[256,128]{1,0:T(8,128)(2,1)S(1)}, bf16[256,128]{1,0:T(8,128)(2,1)S(1)}, u32[]{:S(2)}, u32[]{:S(2)}) %collective-permute-start.1) | collective-permute-done | bytes 65568 | tf_op jit(solution)/shard_map/ppermute | solution.py:298
  42.5 3.7 %shard_map.113 = (bf16[512,256]{1,0:T(8,128)(2,1)S(1)}, bf16[512,256]{1,0:T(8,128)(2,1)S(1)}, bf16[512,256]{1,0:T(8,128)(2,1)}, bf16[32,256]{1,0:T(8,128)(2,1)S(...) custom-call(s32[7]{0:T(128)S(1)} %stack.31.at, ...), custom_call_target="tpu_custom_call" | custom-call | flops 3000000000 | bytes 262144 | tf_op jit(solution)/shard_map/pallas_call | solution.py:261
  46.2 2.2 %all-gather = bf16[1024,256]{1,0:T(8,128)(2,1)S(1)} all-gather(bf16[512,256]{1,0:T(8,128)(2,1)S(1)} %get-tuple-element.40), channel_id=2, replica_groups={{0,32},{64,96},{128,160},{192,224},{256,288},{320,352},{384,416},{448,4..., dimensions={0}, use_global_device_ids=true | all-gather | bytes 786432 | tf_op jit(solution)/shard_map/all_gather | solution.py:327
  49.0 13.2 %all_to_all.35.parts = bf16[4,128,256]{2,1,0:T(8,128)(2,1)S(1)} all-to-all(bf16[4,128,256]{2,1,0:T(8,128)(2,1)S(1)} %shard_map.114), channel_id=1, replica_groups={{0,64,128,192},{32,96,160,224},{256,320,384,448},{288,352,416,480},{1,6..., dimensions={0} | all-to-all | bytes 524288 | tf_op jit(solution)/shard_map/all_to_all | solution.py:329
  62.8 2.0 %collective-permute-start.3 = (bf16[128,256]{1,0:T(8,128)(2,1)S(1)}, bf16[128,256]{1,0:T(8,128)(2,1)S(1)}, u32[]{:S(2)}, u32[]{:S(2)}) collective-permute-start(bf16[128,256]{1,0:T(8,128)(2,1)S(1)} %shard_map.115.mine), channel_id=1, source_target_pairs={{0,256},{1,257},{32,289},{33,288},{64,320},{65,321},{96,353},{97,3... | collective-permute-start | bytes 196616 | tf_op jit(solution)/shard_map/ppermute | solution.py:332
  64.8 7.4 %all-to-all-start.2 = ((bf16[16,32,256]{2,1,0:T(8,128)(2,1)}), bf16[16,32,256]{2,1,0:T(8,128)(2,1)S(1)}, u32[]{:S(2)}, u32[]{:S(2)}) async-start(bf16[16,32,256]{2,1,0:T(8,128)(2,1)} %bitcast.15), calls=%async_computation.2 | async-start | bytes 524288 | tf_op jit(solution)/shard_map/all_to_all | solution.py:334
  72.2 2.4 %collective-permute-done.3.theirs = bf16[128,256]{1,0:T(8,128)(2,1)S(1)} collective-permute-done((bf16[128,256]{1,0:T(8,128)(2,1)S(1)}, bf16[128,256]{1,0:T(8,128)(2,1)S(1)}, u32[]{:S(2)}, u32[]{:S(2)}) %collective-permute-start.3) | collective-permute-done | bytes 65568 | tf_op jit(solution)/shard_map/ppermute | solution.py:332
  75.2 4.4 %collective-permute-start.4 = (bf16[128,256]{1,0:T(8,128)(2,1)S(1)}, bf16[128,256]{1,0:T(8,128)(2,1)S(1)}, u32[]{:S(2)}, u32[]{:S(2)}) collective-permute-start(bf16[128,256]{1,0:T(8,128)(2,1)S(1)} %shard_map.117.mine), channel_id=1, source_target_pairs={{0,1},{1,0},{2,3},{3,2},{4,5},{5,4},{6,7},{7,6},{8,9},{9,8},{10,11... | collective-permute-start | bytes 196616 | tf_op jit(solution)/shard_map/ppermute | solution.py:336
  81.0 7.2 %all-to-all-start.3 = ((bf16[16,32,256]{2,1,0:T(8,128)(2,1)}), bf16[16,32,256]{2,1,0:T(8,128)(2,1)S(1)}, u32[]{:S(2)}, u32[]{:S(2)}) async-start(bf16[16,32,256]{2,1,0:T(8,128)(2,1)} %get-tuple-element.43), calls=%async_computation.3 | async-start | bytes 524288 | tf_op jit(solution)/shard_map/all_to_all | solution.py:345
  88.2 3.8 %collective-permute-done.4.theirs = bf16[128,256]{1,0:T(8,128)(2,1)S(1)} collective-permute-done((bf16[128,256]{1,0:T(8,128)(2,1)S(1)}, bf16[128,256]{1,0:T(8,128)(2,1)S(1)}, u32[]{:S(2)}, u32[]{:S(2)}) %collective-permute-start.4) | collective-permute-done | bytes 65568 | tf_op jit(solution)/shard_map/ppermute | solution.py:336
  92.8 1.9 %collective-permute-start.7 = (bf16[128,256]{1,0:T(8,128)(2,1)S(1)}, bf16[128,256]{1,0:T(8,128)(2,1)S(1)}, u32[]{:S(2)}, u32[]{:S(2)}) collective-permute-start(bf16[128,256]{1,0:T(8,128)(2,1)S(1)} %get-tuple-element.48.own), channel_id=1, source_target_pairs={{0,192},{32,224},{64,128},{96,160},{128,64},{160,96},{192,0},{224,... | collective-permute-start | bytes 196616 | tf_op jit(solution)/shard_map/ppermute | solution.py:353
  94.7 2.0 %collective-permute-start.6 = (bf16[128,256]{1,0:T(8,128)(2,1)S(1)}, bf16[128,256]{1,0:T(8,128)(2,1)S(1)}, u32[]{:S(2)}, u32[]{:S(2)}) collective-permute-start(bf16[128,256]{1,0:T(8,128)(2,1)S(1)} %get-tuple-element.48.own), channel_id=1, source_target_pairs={{0,128},{32,160},{64,192},{96,224},{128,0},{160,32},{192,64},{224,... | collective-permute-start | bytes 196616 | tf_op jit(solution)/shard_map/ppermute | solution.py:353
  96.7 6.2 %collective-permute-start.5 = (bf16[128,256]{1,0:T(8,128)(2,1)S(1)}, bf16[128,256]{1,0:T(8,128)(2,1)S(1)}, u32[]{:S(2)}, u32[]{:S(2)}) collective-permute-start(bf16[128,256]{1,0:T(8,128)(2,1)S(1)} %get-tuple-element.48.own), channel_id=1, source_target_pairs={{0,64},{32,96},{64,0},{96,32},{128,192},{160,224},{192,128},{224,1... | collective-permute-start | bytes 196616 | tf_op jit(solution)/shard_map/ppermute | solution.py:353
  102.9 2.2 %collective-permute-done.5.one = bf16[128,256]{1,0:T(8,128)(2,1)S(1)} collective-permute-done((bf16[128,256]{1,0:T(8,128)(2,1)S(1)}, bf16[128,256]{1,0:T(8,128)(2,1)S(1)}, u32[]{:S(2)}, u32[]{:S(2)}) %collective-permute-start.5) | collective-permute-done | bytes 65568 | tf_op jit(solution)/shard_map/ppermute | solution.py:353
  105.7 2.3 %all_gather.24 = bf16[8,128,256]{2,1,0:T(8,128)(2,1)S(1)} all-gather(bf16[4,128,256]{2,1,0:T(8,128)(2,1)S(1)} %shard_map.119), channel_id=1, replica_groups={{0,32},{64,96},{128,160},{192,224},{256,288},{320,352},{384,416},{448,4..., dimensions={0}, use_global_device_ids=true | all-gather | bytes 786432 | tf_op jit(solution)/shard_map/all_gather | solution.py:356
  108.0 2.5 %shard_map.120 = (bf16[512,256]{1,0:T(8,128)(2,1)S(1)}, bf16[512,256]{1,0:T(8,128)(2,1)S(1)}, bf16[512,256]{1,0:T(8,128)(2,1)}, bf16[32,256]{1,0:T(8,128)(2,1)S(1)}, bf16[128,256]{1,0:T(8,128)(2,1)S(1)}) custom-call(s32[7]{0:T(128)S(1)} %stack.31.at, bf16[512,256]{1,0:T(8,128)(2,1)S(1)} %bitcast.31, bf16[1024,256]{1,0:T(8,128)(2,1)S(1)} %bitcast.25, ...), custom_call_target="tpu_custom_call" | custom-call | flops 3000000000 | bytes 262144 | tf_op jit(solution)/shard_map/pallas_call | solution.py:261
  110.5 2.2 %all-gather.1 = bf16[1024,256]{1,0:T(8,128)(2,1)S(1)} all-gather(bf16[512,256]{1,0:T(8,128)(2,1)S(1)} %get-tuple-element.56), channel_id=3, replica_groups={{0,32},{64,96},{128,160},{192,224},{256,288},{320,352},{384,416},{448,4..., dimensions={0}, use_global_device_ids=true | all-gather | bytes 786432 | tf_op jit(solution)/shard_map/all_gather | solution.py:327
  113.3 12.3 %all_to_all.36.parts = bf16[4,128,256]{2,1,0:T(8,128)(2,1)S(1)} all-to-all(bf16[4,128,256]{2,1,0:T(8,128)(2,1)S(1)} %shard_map.121), channel_id=1, replica_groups={{0,64,128,192},{32,96,160,224},{256,320,384,448},{288,352,416,480},{1,6..., dimensions={0} | all-to-all | bytes 524288 | tf_op jit(solution)/shard_map/all_to_all | solution.py:329
  126.1 4.0 %collective-permute-start.9 = (bf16[128,256]{1,0:T(8,128)(2,1)S(1)}, bf16[128,256]{1,0:T(8,128)(2,1)S(1)}, u32[]{:S(2)}, u32[]{:S(2)}) collective-permute-start(bf16[128,256]{1,0:T(8,128)(2,1)S(1)} %shard_map.122.mine), channel_id=1, source_target_pairs={{0,256},{1,257},{32,289},{33,288},{64,320},{65,321},{96,353},{97,3... | collective-permute-start | bytes 196616 | tf_op jit(solution)/shard_map/ppermute | solution.py:332
  130.1 7.2 %all-to-all-start.5 = ((bf16[16,32,256]{2,1,0:T(8,128)(2,1)}), bf16[16,32,256]{2,1,0:T(8,128)(2,1)S(1)}, u32[]{:S(2)}, u32[]{:S(2)}) async-start(bf16[16,32,256]{2,1,0:T(8,128)(2,1)} %bitcast.19), calls=%async_computation.5 | async-start | bytes 524288 | tf_op jit(solution)/shard_map/all_to_all | solution.py:334
  138.5 7.2 %collective-permute-start.10 = (bf16[128,256]{1,0:T(8,128)(2,1)S(1)}, bf16[128,256]{1,0:T(8,128)(2,1)S(1)}, u32[]{:S(2)}, u32[]{:S(2)}) collective-permute-start(bf16[128,256]{1,0:T(8,128)(2,1)S(1)} %shard_map.125.mine), channel_id=1, source_target_pairs={{0,1},{1,0},{2,3},{3,2},{4,5},{5,4},{6,7},{7,6},{8,9},{9,8},{10,11... | collective-permute-start | bytes 196616 | tf_op jit(solution)/shard_map/ppermute | solution.py:336
  146.5 7.4 %collective-permute-start.8 = (bf16[32,256]{1,0:T(8,128)(2,1)S(1)}, bf16[32,256]{1,0:T(8,128)(2,1)S(1)}, u32[]{:S(2)}, u32[]{:S(2)}) collective-permute-start(bf16[32,256]{1,0:T(8,128)(2,1)S(1)} %get-tuple-element.61), channel_id=1, source_target_pairs={{0,1},{1,0},{2,3},{3,2},{4,5},{5,4},{6,7},{7,6},{8,9},{9,8},{10,11... | collective-permute-start | bytes 49160 | tf_op jit(solution)/shard_map/ppermute | solution.py:367
  154.7 4.1 %collective-permute-start.13 = (bf16[128,256]{1,0:T(8,128)(2,1)S(1)}, bf16[128,256]{1,0:T(8,128)(2,1)S(1)}, u32[]{:S(2)}, u32[]{:S(2)}) collective-permute-start(bf16[128,256]{1,0:T(8,128)(2,1)S(1)} %shard_map.126.own), channel_id=1, source_target_pairs={{0,192},{32,224},{64,128},{96,160},{128,64},{160,96},{192,0},{224,... | collective-permute-start | bytes 196616 | tf_op jit(solution)/shard_map/ppermute | solution.py:371
  160.7 4.1 %collective-permute-start.11 = (bf16[128,256]{1,0:T(8,128)(2,1)S(1)}, bf16[128,256]{1,0:T(8,128)(2,1)S(1)}, u32[]{:S(2)}, u32[]{:S(2)}) collective-permute-start(bf16[128,256]{1,0:T(8,128)(2,1)S(1)} %shard_map.126.own), channel_id=1, source_target_pairs={{0,64},{32,96},{64,0},{96,32},{128,192},{160,224},{192,128},{224,1... | collective-permute-start | bytes 196616 | tf_op jit(solution)/shard_map/ppermute | solution.py:371
  166.1 7.2 %all-to-all-start.6 = ((bf16[16,32,384]{2,1,0:T(8,128)(2,1)}), bf16[16,32,384]{2,1,0:T(8,128)(2,1)S(1)}, u32[]{:S(2)}, u32[]{:S(2)}) async-start(bf16[16,32,384]{2,1,0:T(8,128)(2,1)} %shard_map.124), calls=%async_computation.6 | async-start | bytes 786432 | tf_op jit(solution)/shard_map/all_to_all | solution.py:375
  174.0 2.2 %all_gather.27 = bf16[8,128,256]{2,1,0:T(8,128)(2,1)S(1)} all-gather(bf16[4,128,256]{2,1,0:T(8,128)(2,1)S(1)} %shard_map.127), channel_id=1, replica_groups={{0,32},{64,96},{128,160},{192,224},{256,288},{320,352},{384,416},{448,4..., dimensions={0}, use_global_device_ids=true | all-gather | bytes 786432 | tf_op jit(solution)/shard_map/all_gather | solution.py:377
  177.7 3.3 %all-to-all-done.6 = bf16[16,32,384]{2,1,0:T(8,128)(2,1)S(1)} async-done(((bf16[16,32,384]{2,1,0:T(8,128)(2,1)}), bf16[16,32,384]{2,1,0:T(8,128)(2,1)S(1)}, u32[]{:S(2)}, u32[]{:S(2)}) %all-to-all-start.6) | async-done | bytes 393248 | tf_op jit(solution)/shard_map/all_to_all | solution.py:375
  (57 shorter events, 20.6 us)
Async XLA Ops:
  1.4 19.2 %collective-permute-start.2 = (bf16[128,128]{1,0:T(8,128)(2,1)S(1)}, bf16[128,128]{1,0:T(8,128)(2,1)S(1)}, u32[]{:S(2)}, u32[]{:S(2)}) collective-permute-start(bf16[128,128]{1,0:T(8,128)(2,1)S(1)} %dynamic-slice_bitcast_fusion.1), channel_id=1, source_target_pairs={{0,1},{1,0},{2,3},{3,2},{4,5},{5,4},{6,7},{7,6},{8,9},{9,8},{10,11... | collective-permute-start | bytes 98312 | tf_op jit(solution)/shard_map/ppermute | solution.py:291
  18.0 17.8 %collective-permute-start = (bf16[256,128]{1,0:T(8,128)(2,1)S(1)}, bf16[256,128]{1,0:T(8,128)(2,1)S(1)}, u32[]{:S(2)}, u32[]{:S(2)}) collective-permute-start(bf16[256,128]{1,0:T(8,128)(2,1)S(1)} %dynamic-slice_bitcast_fusion), channel_id=1, source_target_pairs={{0,1},{1,0},{2,3},{3,2},{4,5},{5,4},{6,7},{7,6},{8,9},{9,8},{10,11... | collective-permute-start | bytes 196616 | tf_op jit(solution)/shard_map/ppermute | solution.py:292
  21.9 16.5 %all-to-all-start = ((bf16[4,128,128]{2,1,0:T(8,128)(2,1)}), bf16[4,128,128]{2,1,0:T(8,128)(2,1)S(1)}, u32[]{:S(2)}, u32[]{:S(2)}) async-start(bf16[4,128,128]{2,1,0:T(8,128)(2,1)} %shard_map.112), calls=%async_computation | async-start | bytes 262144 | tf_op jit(solution)/shard_map/all_to_all | solution.py:296
  25.2 17.3 %copy-start = (bf16[1,1024,128]{2,1,0:T(8,128)(2,1)S(1)}, bf16[1,1024,128]{2,1,0:T(8,128)(2,1)}, u32[]{:S(2)}) copy-start(bf16[1,1024,128]{2,1,0:T(8,128)(2,1)} %param.8) | copy-start | bytes 786436
  25.2 17.3 %copy-start.1 = (bf16[1,1024,128]{2,1,0:T(8,128)(2,1)S(1)}, bf16[1,1024,128]{2,1,0:T(8,128)(2,1)}, u32[]{:S(2)}) copy-start(bf16[1,1024,128]{2,1,0:T(8,128)(2,1)} %param.9) | copy-start | bytes 786436
  25.3 17.2 %copy-start.2 = (s32[1,1,512,1024]{3,2,1,0:T(8,128)S(1)}, s32[1,1,512,1024]{3,2,1,0:T(8,128)}, u32[]{:S(2)}) copy-start(s32[1,1,512,1024]{3,2,1,0:T(8,128)} %param.12) | copy-start | bytes 6291460
  25.3 17.2 %copy-start.3 = (s32[16,1024]{1,0:T(8,128)S(1)}, s32[16,1024]{1,0:T(8,128)}, u32[]{:S(2)}) copy-start(s32[16,1024]{1,0:T(8,128)} %row_marg.1) | copy-start | bytes 196612
  25.3 17.2 %copy-start.4 = (s32[16,1024]{1,0:T(8,128)S(1)}, s32[16,1024]{1,0:T(8,128)}, u32[]{:S(2)}) copy-start(s32[16,1024]{1,0:T(8,128)} %col_marg.1) | copy-start | bytes 196612
  36.3 6.2 %collective-permute-start.1 = (bf16[256,128]{1,0:T(8,128)(2,1)S(1)}, bf16[256,128]{1,0:T(8,128)(2,1)S(1)}, u32[]{:S(2)}, u32[]{:S(2)}) collective-permute-start(bf16[256,128]{1,0:T(8,128)(2,1)S(1)} %shard_map.111.got), channel_id=1, source_target_pairs={{0,2},{2,0},{4,6},{6,4},{8,10},{10,8},{12,14},{14,12},{16,18},{18,... | collective-permute-start | bytes 196616 | tf_op jit(solution)/shard_map/ppermute | solution.py:298
  46.2 2.8 %copy-start.7 = (f32[512,1024]{1,0:T(8,128)}, f32[512,1024]{1,0:T(8,128)S(1)}, u32[]{:S(2)}) copy-start(f32[512,1024]{1,0:T(8,128)S(1)} %get-tuple-element.52.weight) | copy-start | bytes 6291460
  46.2 2.8 %copy-start.9 = (f32[512,1024]{1,0:T(8,128)}, f32[512,1024]{1,0:T(8,128)S(1)}, u32[]{:S(2)}) copy-start(f32[512,1024]{1,0:T(8,128)S(1)} %get-tuple-element.53.target) | copy-start | bytes 6291460
  62.8 11.8 %collective-permute-start.3 = (bf16[128,256]{1,0:T(8,128)(2,1)S(1)}, bf16[128,256]{1,0:T(8,128)(2,1)S(1)}, u32[]{:S(2)}, u32[]{:S(2)}) collective-permute-start(bf16[128,256]{1,0:T(8,128)(2,1)S(1)} %shard_map.115.mine), channel_id=1, source_target_pairs={{0,256},{1,257},{32,289},{33,288},{64,320},{65,321},{96,353},{97,3... | collective-permute-start | bytes 196616 | tf_op jit(solution)/shard_map/ppermute | solution.py:332
  64.8 14.7 %all-to-all-start.2 = ((bf16[16,32,256]{2,1,0:T(8,128)(2,1)}), bf16[16,32,256]{2,1,0:T(8,128)(2,1)S(1)}, u32[]{:S(2)}, u32[]{:S(2)}) async-start(bf16[16,32,256]{2,1,0:T(8,128)(2,1)} %bitcast.15), calls=%async_computation.2 | async-start | bytes 524288 | tf_op jit(solution)/shard_map/all_to_all | solution.py:334
  72.2 7.3 %copy-start.5 = (f32[1,1024]{1,0:T(1,128)S(1)}, f32[1,1024]{1,0:T(1,128)}, u32[]{:S(2)}) copy-start(f32[1,1024]{1,0:T(1,128)} %acc.2) | copy-start | bytes 12292
  75.2 16.9 %collective-permute-start.4 = (bf16[128,256]{1,0:T(8,128)(2,1)S(1)}, bf16[128,256]{1,0:T(8,128)(2,1)S(1)}, u32[]{:S(2)}, u32[]{:S(2)}) collective-permute-start(bf16[128,256]{1,0:T(8,128)(2,1)S(1)} %shard_map.117.mine), channel_id=1, source_target_pairs={{0,1},{1,0},{2,3},{3,2},{4,5},{5,4},{6,7},{7,6},{8,9},{9,8},{10,11... | collective-permute-start | bytes 196616 | tf_op jit(solution)/shard_map/ppermute | solution.py:336
  79.6 12.5 %copy-start.6 = (f32[1,1024]{1,0:T(1,128)S(1)}, f32[1,1024]{1,0:T(1,128)}, u32[]{:S(2)}) copy-start(f32[1,1024]{1,0:T(1,128)} %acc.3) | copy-start | bytes 12292
  81.0 24.1 %all-to-all-start.3 = ((bf16[16,32,256]{2,1,0:T(8,128)(2,1)}), bf16[16,32,256]{2,1,0:T(8,128)(2,1)S(1)}, u32[]{:S(2)}, u32[]{:S(2)}) async-start(bf16[16,32,256]{2,1,0:T(8,128)(2,1)} %get-tuple-element.43), calls=%async_computation.3 | async-start | bytes 524288 | tf_op jit(solution)/shard_map/all_to_all | solution.py:345
  92.8 10.1 %collective-permute-start.7 = (bf16[128,256]{1,0:T(8,128)(2,1)S(1)}, bf16[128,256]{1,0:T(8,128)(2,1)S(1)}, u32[]{:S(2)}, u32[]{:S(2)}) collective-permute-start(bf16[128,256]{1,0:T(8,128)(2,1)S(1)} %get-tuple-element.48.own), channel_id=1, source_target_pairs={{0,192},{32,224},{64,128},{96,160},{128,64},{160,96},{192,0},{224,... | collective-permute-start | bytes 196616 | tf_op jit(solution)/shard_map/ppermute | solution.py:353
  94.7 8.2 %collective-permute-start.6 = (bf16[128,256]{1,0:T(8,128)(2,1)S(1)}, bf16[128,256]{1,0:T(8,128)(2,1)S(1)}, u32[]{:S(2)}, u32[]{:S(2)}) collective-permute-start(bf16[128,256]{1,0:T(8,128)(2,1)S(1)} %get-tuple-element.48.own), channel_id=1, source_target_pairs={{0,128},{32,160},{64,192},{96,224},{128,0},{160,32},{192,64},{224,... | collective-permute-start | bytes 196616 | tf_op jit(solution)/shard_map/ppermute | solution.py:353
  96.7 8.4 %collective-permute-start.5 = (bf16[128,256]{1,0:T(8,128)(2,1)S(1)}, bf16[128,256]{1,0:T(8,128)(2,1)S(1)}, u32[]{:S(2)}, u32[]{:S(2)}) collective-permute-start(bf16[128,256]{1,0:T(8,128)(2,1)S(1)} %get-tuple-element.48.own), channel_id=1, source_target_pairs={{0,64},{32,96},{64,0},{96,32},{128,192},{160,224},{192,128},{224,1... | collective-permute-start | bytes 196616 | tf_op jit(solution)/shard_map/ppermute | solution.py:353
  105.1 2.9 %copy-start.8 = (f32[512,1024]{1,0:T(8,128)S(1)}, f32[512,1024]{1,0:T(8,128)}, u32[]{:S(2)}) copy-start(f32[512,1024]{1,0:T(8,128)} %copy-done.7) | copy-start | bytes 6291460
  105.1 2.9 %copy-start.10 = (f32[512,1024]{1,0:T(8,128)S(1)}, f32[512,1024]{1,0:T(8,128)}, u32[]{:S(2)}) copy-start(f32[512,1024]{1,0:T(8,128)} %copy-done.9) | copy-start | bytes 6291460
  126.1 11.8 %collective-permute-start.9 = (bf16[128,256]{1,0:T(8,128)(2,1)S(1)}, bf16[128,256]{1,0:T(8,128)(2,1)S(1)}, u32[]{:S(2)}, u32[]{:S(2)}) collective-permute-start(bf16[128,256]{1,0:T(8,128)(2,1)S(1)} %shard_map.122.mine), channel_id=1, source_target_pairs={{0,256},{1,257},{32,289},{33,288},{64,320},{65,321},{96,353},{97,3... | collective-permute-start | bytes 196616 | tf_op jit(solution)/shard_map/ppermute | solution.py:332
  130.1 15.6 %all-to-all-start.5 = ((bf16[16,32,256]{2,1,0:T(8,128)(2,1)}), bf16[16,32,256]{2,1,0:T(8,128)(2,1)S(1)}, u32[]{:S(2)}, u32[]{:S(2)}) async-start(bf16[16,32,256]{2,1,0:T(8,128)(2,1)} %bitcast.19), calls=%async_computation.5 | async-start | bytes 524288 | tf_op jit(solution)/shard_map/all_to_all | solution.py:334
  138.5 15.4 %collective-permute-start.10 = (bf16[128,256]{1,0:T(8,128)(2,1)S(1)}, bf16[128,256]{1,0:T(8,128)(2,1)S(1)}, u32[]{:S(2)}, u32[]{:S(2)}) collective-permute-start(bf16[128,256]{1,0:T(8,128)(2,1)S(1)} %shard_map.125.mine), channel_id=1, source_target_pairs={{0,1},{1,0},{2,3},{3,2},{4,5},{5,4},{6,7},{7,6},{8,9},{9,8},{10,11... | collective-permute-start | bytes 196616 | tf_op jit(solution)/shard_map/ppermute | solution.py:336
  146.5 18.3 %collective-permute-start.8 = (bf16[32,256]{1,0:T(8,128)(2,1)S(1)}, bf16[32,256]{1,0:T(8,128)(2,1)S(1)}, u32[]{:S(2)}, u32[]{:S(2)}) collective-permute-start(bf16[32,256]{1,0:T(8,128)(2,1)S(1)} %get-tuple-element.61), channel_id=1, source_target_pairs={{0,1},{1,0},{2,3},{3,2},{4,5},{5,4},{6,7},{7,6},{8,9},{9,8},{10,11... | collective-permute-start | bytes 49160 | tf_op jit(solution)/shard_map/ppermute | solution.py:367
  154.7 18.7 %collective-permute-start.13 = (bf16[128,256]{1,0:T(8,128)(2,1)S(1)}, bf16[128,256]{1,0:T(8,128)(2,1)S(1)}, u32[]{:S(2)}, u32[]{:S(2)}) collective-permute-start(bf16[128,256]{1,0:T(8,128)(2,1)S(1)} %shard_map.126.own), channel_id=1, source_target_pairs={{0,192},{32,224},{64,128},{96,160},{128,64},{160,96},{192,0},{224,... | collective-permute-start | bytes 196616 | tf_op jit(solution)/shard_map/ppermute | solution.py:371
  158.8 14.6 %collective-permute-start.12 = (bf16[128,256]{1,0:T(8,128)(2,1)S(1)}, bf16[128,256]{1,0:T(8,128)(2,1)S(1)}, u32[]{:S(2)}, u32[]{:S(2)}) collective-permute-start(bf16[128,256]{1,0:T(8,128)(2,1)S(1)} %shard_map.126.own), channel_id=1, source_target_pairs={{0,128},{32,160},{64,192},{96,224},{128,0},{160,32},{192,64},{224,... | collective-permute-start | bytes 196616 | tf_op jit(solution)/shard_map/ppermute | solution.py:371
  160.7 12.7 %collective-permute-start.11 = (bf16[128,256]{1,0:T(8,128)(2,1)S(1)}, bf16[128,256]{1,0:T(8,128)(2,1)S(1)}, u32[]{:S(2)}, u32[]{:S(2)}) collective-permute-start(bf16[128,256]{1,0:T(8,128)(2,1)S(1)} %shard_map.126.own), channel_id=1, source_target_pairs={{0,64},{32,96},{64,0},{96,32},{128,192},{160,224},{192,128},{224,1... | collective-permute-start | bytes 196616 | tf_op jit(solution)/shard_map/ppermute | solution.py:371
  166.1 14.8 %all-to-all-start.6 = ((bf16[16,32,384]{2,1,0:T(8,128)(2,1)}), bf16[16,32,384]{2,1,0:T(8,128)(2,1)S(1)}, u32[]{:S(2)}, u32[]{:S(2)}) async-start(bf16[16,32,384]{2,1,0:T(8,128)(2,1)} %shard_map.124), calls=%async_computation.6 | async-start | bytes 786432 | tf_op jit(solution)/shard_map/all_to_all | solution.py:375
